TPU v7x, 32 devices: a whole 2x2x4 slice. The times are simulated.
32 devices in a mesh: dp: 4 (over x, core), expert: 8 (over z, y).
Axes of the slice: x: 2, y: 2, z: 4, core: 2. Of those that a mesh axis runs over, the one named last changes fastest.
Arguments:
- out_grad: bfloat16 [4096, 2048], P(('dp', 'expert')), may hold values from -6 to 6
- combine: bfloat16 [4096, 6], P(('dp', 'expert')), may hold values from 0.049804688 to 0.59765625
- expert_ids: int32 [4096, 6], P(('dp', 'expert')), may hold values from 0 to 7, all different within a row; in each aligned block of 128 rows (0 to 127, 128 to 255, ...) at most 128 rows name the same one
- hidden: bfloat16 [8, 32, 128, 1408], P('expert', 'dp'), may hold values from -0.59765625 to 0.59765625
- w_down: bfloat16 [8, 2048, 1408], P('expert'), may hold values from -0.15625 to 0.15625
Outputs:
- grad_hidden: bfloat16 [8, 32, 128, 1408], P('expert', 'dp')
- grad_down: bfloat16 [8, 2048, 1408], P('expert', 'dp')
- grad_probs: float32 [4096, 6], P(('dp', 'expert'))
Inputs may be any that keep to these rules, and one draw needn't show every extreme that they name: `expert_ids`: each row names 6 different experts. Among the 128 rows of one source device no expert is named more than 128 times, and in every draw some expert is named exactly 128 times by the rows of some device.
All inputs are finite; a program needn't handle non-finite values.
Results may differ from a plain program's by a relative error of at most 0.013.
Values may be sent and summed in bfloat16 or wider, within the bound.
No kernel may reach another device: no remote copies, remote signals or barrier semaphores. Data moves between devices by JAX's collectives and lax.ppermute only.
A program may use at most 64 MiB of HBM per device.

v0:
```python
import jax
import jax.numpy as jnp
from jax import lax
from jax.sharding import PartitionSpec as P


def body(out_grad, combine, expert_ids, hidden, w_down):
    tok_rows, picks = expert_ids.shape
    local_experts, senders, capacity, inner = hidden.shape
    model_width = out_grad.shape[1]
    experts_all = local_experts * lax.axis_size("expert")
    chosen = expert_ids.reshape(-1)
    onehot = (chosen[:, None] == jnp.arange(experts_all, dtype=jnp.int32)[None, :]).astype(
        jnp.int32
    )
    before = jnp.cumsum(onehot, axis=0) - onehot
    slot_rank = jnp.sum(before * onehot, axis=1)
    bucket_pos = chosen * capacity + slot_rank
    repeated = jnp.broadcast_to(out_grad[:, None, :], (tok_rows, picks, model_width)).reshape(
        -1, model_width
    )
    send_grad = (
        jnp.zeros((experts_all * capacity, model_width), out_grad.dtype)
        .at[bucket_pos]
        .set(repeated)
    )
    send_prob = (
        jnp.zeros((experts_all * capacity,), combine.dtype).at[bucket_pos].set(combine.reshape(-1))
    )
    recv_grad, recv_prob = (
        lax.all_to_all(
            send_grad.reshape(experts_all, 1, capacity, model_width),
            "expert",
            split_axis=0,
            concat_axis=1,
            tiled=True,
        ),
        lax.all_to_all(
            send_prob.reshape(experts_all, 1, capacity),
            "expert",
            split_axis=0,
            concat_axis=1,
            tiled=True,
        ),
    )
    hidden_grads, slot_grads, scaled_rows, saved_rows = ([], [], [], [])
    expert = 0
    grad_rows = recv_grad[expert].reshape(-1, model_width)
    slot_prob = recv_prob[expert].reshape(-1, 1).astype(jnp.float32)
    saved = hidden[expert].reshape(-1, inner)
    projected = jnp.dot(grad_rows, w_down[expert], preferred_element_type=jnp.float32)
    hidden_grads.append(
        (slot_prob * projected).astype(jnp.bfloat16).reshape(senders, capacity, inner)
    )
    slot_grads.append(jnp.sum(projected * saved, axis=1).reshape(senders, capacity))
    scaled_rows.append((slot_prob * grad_rows).astype(jnp.bfloat16))
    saved_rows.append(saved)
    expert = 0
    left = scaled_rows[expert]
    blocks = lax.dot_general(
        left, saved_rows[expert], (((0,), (0,)), ((), ())), preferred_element_type=jnp.float32
    )
    summed = lax.psum_scatter(
        blocks.astype(jnp.bfloat16), "dp", scatter_dimension=0, tiled=True
    ).astype(jnp.float32)
    grad_down = jnp.transpose(
        summed.reshape(summed.shape[0], local_experts, inner), (1, 0, 2)
    ).astype(jnp.bfloat16)
    returned = lax.all_to_all(
        jnp.stack(slot_grads), "expert", split_axis=1, concat_axis=0, tiled=True
    )
    grad_probs = returned.reshape(-1)[bucket_pos].reshape(tok_rows, picks)
    return (jnp.stack(hidden_grads), grad_down, grad_probs)


def solution(mesh):
    in_specs = (
        P(("dp", "expert"), None),
        P(("dp", "expert"), None),
        P(("dp", "expert"), None),
        P("expert", "dp", None, None),
        P("expert", None, None),
    )
    out_specs = (P("expert", "dp", None, None), P("expert", "dp", None), P(("dp", "expert"), None))
    return jax.shard_map(body, mesh=mesh, in_specs=in_specs, out_specs=out_specs, check_vma=False)
```

profile of v0, /device:TPU:0, one launch (start us, length us, event | category | flops | bytes accessed | tf_op | source)
XLA Modules:
  0.0 218.3 jit_solution(9691871908156078406)
XLA Ops:
  7.2 0.7 broadcast_multiply_fusion
  7.9 0.8 copy.18
  8.6 0.1 eq.29
  8.8 0.1 eq.25
  8.9 0.8 copy.22
  9.7 0.1 reshape.125
  9.9 0.1 copy.17
  10.0 0.1 mul.41
  10.2 1.7 reduce-window.6
  11.9 0.1 slice.10
  11.9 0.1 copy.20
  12.1 0.2 reduce-window.9
  12.2 0.1 copy.21
  12.3 0.1 fusion.5
  12.4 8.6 %scatter_custom_fusion = bf16[1024]{0:T(1024)(128)(2,1)S(1)} fusion(s32[768]{0:T(1024)S(1)} %fusion.7, bf16[768]{0:T(1024)(128)(2,1)S(1)} %reshape.125, bf16[]{:T(256)} %constant.5.clone.1), kind=kCustom, calls=%fused_computation.21 | custom fusion | bytes 2050 | tf_op jit(solution)/shard_map/scatter | solution.py:28
  21.1 0.6 copy.23
  21.7 7.3 %all-to-all-start = ((bf16[8,1,128]{2,1,0:T(2,128)(2,1)}), bf16[8,1,128]{2,1,0:T(2,128)(2,1)S(1)}, u32[]{:S(2)}, u32[]{:S(2)}) async-start(bf16[8,1,128]{2,1,0:T(2,128)(2,1)} %copy.23), calls=%async_computation | async-start | bytes 8192 | tf_op jit(solution)/shard_map/all_to_all | solution.py:38
  28.9 3.6 %broadcast_in_dim.8 = bf16[128,6,2048]{2,1,0:T(8,128)(2,1)} broadcast(bf16[128,2048]{1,0:T(8,128)(2,1)} %param.5), dimensions={0,2} | broadcast | bytes 3670016 | tf_op jit(solution)/shard_map/broadcast_in_dim | solution.py:19
  32.6 4.9 %reshape.133 = bf16[768,2048]{1,0:T(8,128)(2,1)S(1)} reshape(bf16[128,6,2048]{2,1,0:T(8,128)(2,1)} %broadcast_in_dim.8) | data formatting | bytes 6291456 | tf_op jit(solution)/shard_map/reshape | solution.py:19
  37.5 9.4 %scatter_custom_fusion.1 = bf16[1024,2048]{1,0:T(8,128)(2,1)} fusion(s32[768]{0:T(1024)S(1)} %fusion.7, bf16[768,2048]{1,0:T(8,128)(2,1)S(1)} %reshape.133, bf16[]{:T(256)} %constant.5.clone.1), kind=kCustom, calls=%fused_computation.9 | custom fusion | bytes 4194306 | tf_op jit(solution)/shard_map/scatter | solution.py:25
  46.8 0.0 all-to-all-done
  46.8 6.0 %all-to-all-start.1 = ((bf16[8,1,128,2048]{3,2,1,0:T(8,128)(2,1)}), bf16[8,1,128,2048]{3,2,1,0:T(8,128)(2,1)}, u32[]{:S(2)}, u32[]{:S(2)}) async-start(bf16[8,1,128,2048]{3,2,1,0:T(8,128)(2,1)} %bitcast.33), calls=%async_computation.1 | async-start | bytes 8388608 | tf_op jit(solution)/shard_map/all_to_all | solution.py:31
  52.8 0.2 reduce-scatter.2.cloned.1.call-start
  53.1 92.5 %all-to-all-done.1 = bf16[8,1,128,2048]{3,2,1,0:T(8,128)(2,1)} async-done(((bf16[8,1,128,2048]{3,2,1,0:T(8,128)(2,1)}), bf16[8,1,128,2048]{3,2,1,0:T(8,128)(2,1)}, u32[]{:S(2)}, u32[]{:S(2)}) %all-to-all-start.1) | async-done | bytes 4194336 | tf_op jit(solution)/shard_map/all_to_all | solution.py:31
  145.5 0.0 copy-start
  145.5 3.1 %multiply_convert_fusion = bf16[8,1,128,2048]{3,2,1,0:T(8,128)(2,1)S(1)} fusion(bf16[8,1,128,2048]{3,2,1,0:T(8,128)(2,1)} %all-to-all-done.1, f32[8,128]{1,0:T(8,128)S(1)} %bitcast.35), kind=kLoop, calls=%fused_computation.3 | loop fusion | flops 6291456 | bytes 8392704 | tf_op jit(solution)/shard_map/convert_element_type | solution.py:56
  148.6 0.0 copy-done
  148.6 8.7 %convolution_convert_fusion = bf16[2048,1408]{1,0:T(8,128)(2,1)} fusion(bf16[1024,2048]{1,0:T(8,128)(2,1)S(1)} %bitcast.34, bf16[1024,1408]{1,0:T(8,128)(2,1)S(1)} %bitcast.40), kind=kOutput, calls=%fused_computation.4 | convolution fusion | flops 5908463616 | bytes 12845056 | tf_op jit(solution)/shard_map/dot_general | solution.py:60
  157.3 0.0 reduce-scatter.2.cloned.1.call-update
  157.4 12.0 %multiply_reduce_fusion = (f32[1024]{0:T(1024)}, bf16[1024,1408]{1,0:T(8,128)(2,1)}) fusion(bf16[1,8,128,1408]{3,2,1,0:T(8,128)(2,1)S(1)} %copy-done, f32[1024]{0:T(1024)S(1)} %bitcast.36, bf16[1024,2048]{1,0:T(8,128)(2,1)} %bitcast.6, bf16[1,2048,1408]{2,1,0:T(8,128)(2,1)} %param.9), kind=kOutput, calls=%fused_computation.7 | convolution fusion | flops 5912787968 | bytes 15736832 | tf_op jit(solution)/shard_map/dot_general | solution.py:51
  169.3 3.6 %all-to-all-start.2 = ((f32[1,8,128]{2,0,1:T(1,128)}), f32[1,8,128]{2,0,1:T(1,128)S(1)}, u32[]{:S(2)}, u32[]{:S(2)}) async-start(f32[1,8,128]{2,0,1:T(1,128)} %bitcast.13), calls=%async_computation.3 | async-start | bytes 8192 | tf_op jit(solution)/shard_map/all_to_all | solution.py:69
  173.0 6.4 %all-to-all-done.2 = f32[1,8,128]{2,0,1:T(1,128)S(1)} async-done(((f32[1,8,128]{2,0,1:T(1,128)}), f32[1,8,128]{2,0,1:T(1,128)S(1)}, u32[]{:S(2)}, u32[]{:S(2)}) %all-to-all-start.2) | async-done | bytes 4128 | tf_op jit(solution)/shard_map/all_to_all | solution.py:69
  179.4 3.2 %gather_fusion = f32[768]{0:T(1024)S(1)} fusion(f32[1024]{0:T(1024)S(1)} %bitcast.32, s32[1024]{0:T(1024)S(1)} %pad_clamp_fusion), kind=kCustom, calls=%fused_computation | custom fusion | bytes 9216 | tf_op jit(solution)/shard_map/gather | solution.py:72
  182.6 0.1 reshape.110
  182.7 0.7 copy.24
  183.4 28.1 %reduce-scatter.2.cloned.1.call-done = bf16[512,1408]{1,0:T(8,128)(2,1)} async-done(((bf16[2048,1408]{1,0:T(8,128)(2,1)}), bf16[512,1408]{1,0:T(8,128)(2,1)}) %reduce-scatter.2.cloned.1.call-update) | async-done | bytes 1441808 | tf_op jit(solution)/shard_map/reduce_scatter | solution.py:63
  (4 shorter events, 0.0 us)
Async XLA Ops:
  21.7 25.2 %all-to-all-start = ((bf16[8,1,128]{2,1,0:T(2,128)(2,1)}), bf16[8,1,128]{2,1,0:T(2,128)(2,1)S(1)}, u32[]{:S(2)}, u32[]{:S(2)}) async-start(bf16[8,1,128]{2,1,0:T(2,128)(2,1)} %copy.23), calls=%async_computation | async-start | bytes 8192 | tf_op jit(solution)/shard_map/all_to_all | solution.py:38
  46.8 98.7 %all-to-all-start.1 = ((bf16[8,1,128,2048]{3,2,1,0:T(8,128)(2,1)}), bf16[8,1,128,2048]{3,2,1,0:T(8,128)(2,1)}, u32[]{:S(2)}, u32[]{:S(2)}) async-start(bf16[8,1,128,2048]{3,2,1,0:T(8,128)(2,1)} %bitcast.33), calls=%async_computation.1 | async-start | bytes 8388608 | tf_op jit(solution)/shard_map/all_to_all | solution.py:31
  52.8 158.6 %reduce-scatter.2.cloned.1.call-start = ((), (), s32[]{:S(2)}) async-start(), calls=%async_computation.4 | async-start | bytes 7208960 | tf_op jit(solution)/shard_map/reduce_scatter | solution.py:63
  145.5 3.1 %copy-start = (bf16[1,8,128,1408]{3,2,1,0:T(8,128)(2,1)S(1)}, bf16[1,8,128,1408]{3,2,1,0:T(8,128)(2,1)}, u32[]{:S(2)}) copy-start(bf16[1,8,128,1408]{3,2,1,0:T(8,128)(2,1)} %param.8) | copy-start | bytes 8650756
  169.3 10.0 %all-to-all-start.2 = ((f32[1,8,128]{2,0,1:T(1,128)}), f32[1,8,128]{2,0,1:T(1,128)S(1)}, u32[]{:S(2)}, u32[]{:S(2)}) async-start(f32[1,8,128]{2,0,1:T(1,128)} %bitcast.13), calls=%async_computation.3 | async-start | bytes 8192 | tf_op jit(solution)/shard_map/all_to_all | solution.py:69
Sparse Core Ops, SparseCore 0:
  157.5 53.9 reduce-scatter.1
where the time goes:
time: 219 us; the launch traced here: 218 us
  waiting for transfers between devices  127 us (58%)
  local copies, waits for them, and re-layouts  33.6 us (15%)
  matrix products  20.7 us (9%)
  starting transfers between devices  17.1 us (8%)
  between operations  14.1 us (6%)
  other arithmetic  5.76 us (3%)
    all_to_all x1, waiting for transfers between devices, body(): lax.all_to_all(send_grad.reshape(experts_all, 1, capacity, model_width),...  92.5 us
    reduce_scatter x1, waiting for transfers between devices, body(): lax.psum_scatter(blocks.astype(jnp.bfloat16), 'dp', scatter_dimension=0,...  28.1 us
    dot_general x1, matrix products, body(): jnp.dot(grad_rows, w_down[expert], preferred_element_type=jnp.float32)  12 us
    scatter x1, local copies, waits for them, and re-layouts, body(): send_grad = jnp.zeros((experts_all * capacity, model_width), out_grad.dty...  9.35 us
    dot_general x1, matrix products, body(): lax.dot_general(left, saved_rows[expert], (((0,), (0,)), ((), ())), prefe...  8.71 us
    scatter x1, local copies, waits for them, and re-layouts, body(): jnp.zeros((experts_all * capacity,), combine.dtype).at[bucket_pos]  8.61 us
    all_to_all x1, starting transfers between devices, body(): lax.all_to_all(send_prob.reshape(experts_all, 1, capacity), 'expert', spl...  7.28 us
    all_to_all x1, waiting for transfers between devices, body(): lax.all_to_all(jnp.stack(slot_grads), 'expert', split_axis=1, concat_axis...  6.38 us
  transfers between devices with their start and end apart: 4, of which 3 were waited for; matrix products, arithmetic and copies ran while one was open for 15% of the time, Pallas kernels for 0%

commit v1 on v0

v1 whole, which is shorter than its diff:
```python
import functools

import jax
import jax.numpy as jnp
import numpy as np
from jax import lax
from jax.experimental import pallas as pl
from jax.experimental.pallas import tpu as pltpu
from jax.sharding import PartitionSpec as P

MIB = 1024 * 1024
CHUNKS = 2


def cycle_of(count):
    bits = count.bit_length() - 1
    if count != 1 << bits or count < 4:
        return list(range(count))
    width = 1 << (bits // 2)
    depth = count // width
    walk = [z * width for z in range(depth)]
    for turn, z in enumerate(reversed(range(depth))):
        columns = list(range(1, width))
        walk += [z * width + y for y in (columns if turn % 2 == 0 else columns[::-1])]
    return walk


def offsets_of(count, chunk):
    far = count // 2
    behind = far if chunk % 2 == 0 else count - 1 - far
    ahead = count - 1 - behind
    return [0] + [-k for k in range(1, behind + 1)] + [k for k in range(1, ahead + 1)]


def order_table(count, chunk):
    walk = cycle_of(count)
    place = {expert: at for at, expert in enumerate(walk)}
    offsets = offsets_of(count, chunk)
    return np.array(
        [[walk[(place[e] + o) % count] for o in offsets] for e in range(count)], np.int32
    )


def meta_kernel(experts, ids_ref, combine_ref, meta_ref):
    rows, picks = ids_ref.shape
    ids = ids_ref[...]
    weights = combine_ref[...].astype(jnp.float32)
    lane = lax.broadcasted_iota(jnp.int32, (rows, 128), 1)
    named = jnp.zeros((rows, 128), jnp.float32)
    prob = jnp.zeros((rows, 128), jnp.float32)
    for k in range(picks):
        hit = ids[:, k : k + 1] == lane
        named = jnp.where(hit, 1.0, named)
        prob = jnp.where(hit, weights[:, k : k + 1], prob)
    named_t = jnp.transpose(named)
    prob_t = jnp.transpose(prob)
    earlier = (
        lax.broadcasted_iota(jnp.int32, (rows, rows), 0)
        < lax.broadcasted_iota(jnp.int32, (rows, rows), 1)
    ).astype(jnp.bfloat16)
    before = jnp.dot(named_t.astype(jnp.bfloat16), earlier, preferred_element_type=jnp.float32)
    slot_t = jnp.where(named_t > 0.5, before, -1.0)
    both = jnp.concatenate([prob_t[:experts], slot_t[:experts]], axis=0).astype(jnp.bfloat16)
    meta_ref[...] = jnp.zeros_like(meta_ref)
    for group in range(2 * experts // 16):
        meta_ref[:, group * rows : (group + 1) * rows] = both[group * 16 : (group + 1) * 16]


def place_kernel(has_meta, count, cap, tokens, mine_ref, order_ref, *refs):
    blocks, refs = refs[:count], refs[count:]
    if has_meta:
        hidden_ref, placed_ref, part_ref, rows_ref, scaled_ref = refs
    else:
        rows_in, hidden_ref, placed_ref, part_ref, scaled_ref = refs
    expert = mine_ref[0]
    sub = lax.broadcasted_iota(jnp.int32, (16, tokens), 0)
    at = lax.broadcasted_iota(jnp.int32, (cap, tokens), 0).astype(jnp.float32)
    for i in range(count):
        source = order_ref[i]
        block = blocks[i]
        if has_meta:
            prob = jnp.zeros((1, tokens), jnp.float32)
            slot = jnp.zeros((1, tokens), jnp.float32)
            for group in range(2 * count // 16):
                piece = block[tokens : tokens + 16, group * tokens : (group + 1) * tokens].astype(
                    jnp.float32
                )
                row = sub + group * 16
                prob = prob + jnp.sum(jnp.where(row == expert, piece, 0.0), 0, keepdims=True)
                slot = slot + jnp.sum(
                    jnp.where(row == expert + count, piece, 0.0), 0, keepdims=True
                )
            rows_ref[pl.ds(source, 1), :] = jnp.concatenate([prob, slot], axis=1)
        else:
            both = rows_in[pl.ds(source, 1), :]
            prob, slot = both[:, :tokens], both[:, tokens:]
        hit = slot == at
        pick = jnp.where(hit, 1.0, 0.0).astype(jnp.bfloat16)
        weighted = jnp.where(hit, prob, 0.0).astype(jnp.bfloat16)
        grads = block[:tokens, :]
        start = pl.multiple_of(source * cap, cap)
        placed_ref[pl.ds(start, cap), :] = jnp.dot(
            pick, grads, preferred_element_type=jnp.float32
        ).astype(jnp.bfloat16)
        scaled_ref[pl.ds(start, cap), :] = jnp.dot(
            weighted, grads, preferred_element_type=jnp.float32
        ).astype(jnp.bfloat16)
    columns = scaled_ref.shape[1]
    step = min(256, columns)
    for c in range(columns // step):
        part_ref[c * step : (c + 1) * step, :] = lax.dot_general(
            scaled_ref[:, c * step : (c + 1) * step],
            hidden_ref[...],
            (((0,), (0,)), ((), ())),
            preferred_element_type=jnp.float32,
        ).astype(jnp.bfloat16)


def project_kernel(masks, count, cap, tokens, group, mine_ref, *refs):
    placed = refs[:CHUNKS]
    rows_ref, hidden_ref, w_ref, grad_ref, token_ref = refs[CHUNKS:]
    dp = mine_ref[1]
    pieces = len(masks)
    wide = placed[0].shape[1] // pieces
    per = wide * CHUNKS
    step = pl.program_id(0)
    acc = None
    for c in range(CHUNKS):
        for j, mask in enumerate(masks):
            start = pl.multiple_of((dp ^ mask) * per + c * wide, wide)
            term = jnp.dot(
                placed[c][:, j * wide : (j + 1) * wide],
                w_ref[pl.ds(start, wide), :],
                preferred_element_type=jnp.float32,
            )
            acc = term if acc is None else acc + term
    slot_grad = jnp.sum(acc * hidden_ref[...].astype(jnp.float32), axis=1, keepdims=True)
    at = lax.broadcasted_iota(jnp.int32, (cap, tokens), 0).astype(jnp.float32)
    for g in range(group):
        source = step * group + g
        both = rows_ref[pl.ds(source, 1), :]
        prob, slot = both[:, :tokens], both[:, tokens:]
        hit = slot == at
        column = jnp.sum(jnp.where(hit, prob, 0.0), axis=1, keepdims=True)
        grad_ref[g * cap : (g + 1) * cap, :] = (column * acc[g * cap : (g + 1) * cap]).astype(
            jnp.bfloat16
        )
        token_ref[pl.ds(source, 1), :] = jnp.sum(
            jnp.where(hit, slot_grad[g * cap : (g + 1) * cap], 0.0), axis=0, keepdims=True
        )


def body(replicas, out_grad, combine, expert_ids, hidden, w_down):
    tokens, width = out_grad.shape
    _, count, cap, inner = hidden.shape
    slots = count * cap
    mine = lax.axis_index("expert")
    dp = lax.axis_index("dp")
    where = jnp.stack([mine, dp]).astype(jnp.int32)
    hidden2 = hidden.reshape(slots, inner)
    weight = w_down.reshape(width, inner)
    wide = width // (replicas * CHUNKS)
    columns = wide * replicas
    bits = replicas.bit_length() - 1
    masks = sorted(range(replicas), key=lambda m: [-(m >> b & 1) for b in range(bits)])

    vmem = pl.BlockSpec(memory_space=pltpu.VMEM)
    smem = pl.BlockSpec(memory_space=pltpu.SMEM)
    meta = pl.pallas_call(
        functools.partial(meta_kernel, count),
        out_shape=jax.ShapeDtypeStruct((16, columns), jnp.bfloat16),
        in_specs=[vmem, vmem],
        out_specs=vmem,
    )(expert_ids, combine)

    def columns_of(chunk):
        return jnp.concatenate(
            [
                lax.dynamic_slice(
                    out_grad, (0, (dp ^ m) * wide * CHUNKS + chunk * wide), (tokens, wide)
                )
                for m in masks
            ],
            axis=1,
        )

    walk = cycle_of(count)
    forth = [(walk[i], walk[(i + 1) % count]) for i in range(count)]
    back = [(b, a) for a, b in forth]
    own = [columns_of(c) for c in range(CHUNKS)]
    own[0] = jnp.concatenate([own[0], meta], axis=0)
    held = []
    for chunk in range(CHUNKS):
        offsets = offsets_of(count, chunk)
        got = {0: own[chunk]}
        for o in offsets[1:]:
            if o < 0:
                got[o] = lax.ppermute(got[o + 1], "expert", forth)
            else:
                got[o] = lax.ppermute(got[o - 1], "expert", back)
        held.append([got[o] for o in offsets])

    placed, parts, rows = [], [], None
    for chunk in range(CHUNKS):
        order = jnp.asarray(order_table(count, chunk))[mine]
        first = chunk == 0
        shapes = [
            jax.ShapeDtypeStruct((slots, columns), jnp.bfloat16),
            jax.ShapeDtypeStruct((columns, inner), jnp.bfloat16),
        ]
        if first:
            shapes.append(jax.ShapeDtypeStruct((count, 2 * tokens), jnp.float32))
        results = pl.pallas_call(
            functools.partial(place_kernel, first, count, cap, tokens),
            out_shape=shapes,
            in_specs=[smem, smem] + [vmem] * (count + (1 if first else 2)),
            out_specs=[vmem] * len(shapes),
            scratch_shapes=[pltpu.VMEM((slots, columns), jnp.bfloat16)],
            compiler_params=pltpu.CompilerParams(vmem_limit_bytes=32 * MIB),
            cost_estimate=pl.CostEstimate(
                flops=2 * slots * columns * inner, bytes_accessed=8 * MIB, transcendentals=0
            ),
        )(where, order, *held[chunk], *([] if first else [rows]), hidden2)
        placed.append(results[0])
        parts.append(results[1])
        if first:
            rows = results[2]

    group = max(1, 256 // cap)
    block = group * cap
    grad_hidden, by_token = pl.pallas_call(
        functools.partial(project_kernel, masks, count, cap, tokens, group),
        grid=(slots // block,),
        out_shape=[
            jax.ShapeDtypeStruct((slots, inner), jnp.bfloat16),
            jax.ShapeDtypeStruct((count, tokens), jnp.float32),
        ],
        in_specs=[smem]
        + [pl.BlockSpec((block, columns), lambda i: (i, 0))] * CHUNKS
        + [
            pl.BlockSpec((count, 2 * tokens), lambda i: (0, 0)),
            pl.BlockSpec((block, inner), lambda i: (i, 0)),
            pl.BlockSpec((width, inner), lambda i: (0, 0), pipeline_mode=pl.Buffered(1)),
        ],
        out_specs=[
            pl.BlockSpec((block, inner), lambda i: (i, 0)),
            pl.BlockSpec((count, tokens), lambda i: (0, 0)),
        ],
        compiler_params=pltpu.CompilerParams(vmem_limit_bytes=32 * MIB),
        cost_estimate=pl.CostEstimate(
            flops=2 * slots * width * inner, bytes_accessed=16 * MIB, transcendentals=0
        ),
    )(where, *placed, rows, hidden2, weight)

    downs = []
    for chunk in range(CHUNKS):
        part = parts[chunk]
        for b in range(bits):
            half = part.shape[0] // 2
            arrived = lax.ppermute(
                part[:half], "dp", [(r, r ^ (1 << b)) for r in range(replicas)]
            )
            part = (part[half:].astype(jnp.float32) + arrived.astype(jnp.float32)).astype(
                jnp.bfloat16
            )
        downs.append(part)
    grad_down = jnp.concatenate(downs, axis=0)[None]

    returned = lax.all_to_all(by_token, "expert", split_axis=0, concat_axis=0, tiled=True)
    hit = expert_ids[:, :, None] == jnp.arange(count, dtype=jnp.int32)[None, None, :]
    grad_probs = jnp.sum(jnp.where(hit, returned.T[:, None, :], 0.0), axis=2)
    return grad_hidden.reshape(hidden.shape), grad_down, grad_probs


def solution(mesh):
    in_specs = (
        P(("dp", "expert"), None),
        P(("dp", "expert"), None),
        P(("dp", "expert"), None),
        P("expert", "dp", None, None),
        P("expert", None, None),
    )
    out_specs = (P("expert", "dp", None, None), P("expert", "dp", None), P(("dp", "expert"), None))
    return jax.shard_map(
        functools.partial(body, mesh.shape["dp"]),
        mesh=mesh,
        in_specs=in_specs,
        out_specs=out_specs,
        check_vma=False,
    )
```

time: 219 us -> 107 us (0.49)
  waiting for transfers between devices: 127 us -> 41.9 us
  local copies, waits for them, and re-layouts: 33.6 us -> 7.48 us
  Pallas kernels: 0 us -> 21.7 us
  matrix products: 20.7 us -> 0 us
  between operations: 14.1 us -> 0.82 us
  blocking collectives: 0 us -> 11.1 us
  starting transfers between devices: 17.1 us -> 19.5 us
    all_to_all x3 -> x0, waiting for transfers between devices: 98.9 us -> none  [the longest x1 92.5 us: body(): lax.all_to_all(send_grad.reshape(experts_all, 1, capacity, model_width),...]
    ppermute x0 -> x18, waiting for transfers between devices: none -> 41.9 us  [the longest x7 30.7 us: body(): got[o] = lax.ppermute(got[o + 1], 'expert', forth)]
    reduce_scatter x1 -> x0, waiting for transfers between devices: 28.1 us -> none  [body(): lax.psum_scatter(blocks.astype(jnp.bfloat16), 'dp', scatter_dimension=0,...]
    pallas_call x0 -> x4, Pallas kernels: none -> 21.7 us  [the longest x2 10.7 us: body(): pl.pallas_call(functools.partial(place_kernel, first, count, cap, tokens)...]
    dot_general x2 -> x0, matrix products: 20.7 us -> none  [the longest x1 12 us: body(): jnp.dot(grad_rows, w_down[expert], preferred_element_type=jnp.float32)]
    ppermute x0 -> x18, starting transfers between devices: none -> 19.5 us  [the longest x7 12.1 us: body(): got[o] = lax.ppermute(got[o + 1], 'expert', forth)]
    scatter x2 -> x0, local copies, waits for them, and re-layouts: 18 us -> none  [the longest x1 9.35 us: body(): send_grad = jnp.zeros((experts_all * capacity, model_width), out_grad.dty...]
    all_to_all x3 -> x0, starting transfers between devices: 16.9 us -> none  [the longest x1 7.28 us: body(): lax.all_to_all(send_prob.reshape(experts_all, 1, capacity), 'expert', spl...]
  transfers between devices with their start and end apart: 4 -> 18, of which waited for: 3 -> 9; matrix products, arithmetic and copies ran while one was open for 15% -> 3% of each run, Pallas kernels for 0% -> 19%
where the time goes in v1:
time: 107 us; the launch traced here: 106 us
  waiting for transfers between devices  41.9 us (39%)
  Pallas kernels  21.7 us (20%)
  starting transfers between devices  19.5 us (18%)
  blocking collectives  11.1 us (10%)
  local copies, waits for them, and re-layouts  7.48 us (7%)
  other arithmetic  3.74 us (3%)
    ppermute x7, waiting for transfers between devices, body(): got[o] = lax.ppermute(got[o + 1], 'expert', forth)  30.7 us
    ppermute x7, starting transfers between devices, body(): got[o] = lax.ppermute(got[o + 1], 'expert', forth)  12.1 us
    all_to_all x1, blocking collectives, body(): lax.all_to_all(by_token, 'expert', split_axis=0, concat_axis=0, tiled=True)  11.1 us
    pallas_call x2, Pallas kernels, body(): pl.pallas_call(functools.partial(place_kernel, first, count, cap, tokens)...  10.7 us
    ppermute x4, waiting for transfers between devices, body(): lax.ppermute(part[:half], 'dp', [(r, r ^ 1 << b) for r in range(replicas)])  9.49 us
    pallas_call x1, Pallas kernels, body(): pl.pallas_call(functools.partial(project_kernel, masks, count, cap, token...  9.15 us
    unnamed x12, local copies, waits for them, and re-layouts  4.67 us
    ppermute x7, starting transfers between devices, body(): got[o] = lax.ppermute(got[o - 1], 'expert', back)  4.09 us
  transfers between devices with their start and end apart: 18, of which 9 were waited for; matrix products, arithmetic and copies ran while one was open for 3% of the time, Pallas kernels for 19%

profile of v1, /device:TPU:0, one launch (start us, length us, event | category | flops | bytes accessed | tf_op | source)
XLA Modules:
  0.0 106.2 jit_solution(2111042315231818138)
XLA Ops:
  0.7 1.4 %copy.20.combine_ref = bf16[128,6]{1,0:T(8,128)(2,1)} copy(bf16[128,6]{0,1:T(8,128)(2,1)} %param.8) | data formatting | bytes 3072 | tf_op args[1]
  2.1 1.4 %copy.19.ids_ref = s32[128,6]{1,0:T(8,128)} copy(s32[128,6]{0,1:T(8,128)} %param.9) | data formatting | bytes 6144 | tf_op args[2]
  3.5 1.8 %shard_map.94 = bf16[16,1024]{1,0:T(8,128)(2,1)} custom-call(s32[128,6]{1,0:T(8,128)} %copy.19.ids_ref, bf16[128,6]{1,0:T(8,128)(2,1)} %copy.20.combine_ref), custom_call_target="tpu_custom_call" | custom-call | tf_op jit(solution)/shard_map/pallas_call | solution.py:169
  5.3 1.1 %constant_dynamic-slice_fusion.3 = (bf16[128,256]{1,0:T(8,128)(2,1)S(1)}, bf16[128,256]{1,0:T(8,128)(2,1)S(1)}, bf16[128,256]{1,0:T(8,128)(2,1)S(1)}, bf16[128,2...) fusion(bf16[128,2048]{1,0:T(8,128)(2,1)} %param.7, ...), kind=kLoop, calls=%fused_computation.12 | loop fusion | bytes 1048608 | tf_op jit(solution)/shard_map/dynamic_slice | solution.py:179
  6.4 0.8 pad_maximum_fusion.refs_0_
  7.2 3.1 %collective-permute-start = (bf16[144,1024]{1,0:T(8,128)(2,1)S(1)}, bf16[144,1024]{1,0:T(8,128)(2,1)S(1)}, u32[]{:S(2)}, u32[]{:S(2)}) collective-permute-start(bf16[144,1024]{1,0:T(8,128)(2,1)S(1)} %pad_maximum_fusion.refs_0_), channel_id=1, source_target_pairs={{0,2},{2,4},{4,6},{6,7},{7,5},{5,3},{3,1},{1,0},{8,10},{10,12},{12... | collective-permute-start | bytes 884744 | tf_op jit(solution)/shard_map/ppermute | solution.py:198
  10.3 6.9 %collective-permute-done.refs_1_ = bf16[144,1024]{1,0:T(8,128)(2,1)S(1)} collective-permute-done((bf16[144,1024]{1,0:T(8,128)(2,1)S(1)}, bf16[144,1024]{1,0:T(8,128)(2,1)S(1)}, u32[]{:S(2)}, u32[]{:S(2)}) %collective-permute-start) | collective-permute-done | bytes 294944 | tf_op jit(solution)/shard_map/ppermute | solution.py:198
  17.2 1.8 %collective-permute-start.1 = (bf16[144,1024]{1,0:T(8,128)(2,1)S(1)}, bf16[144,1024]{1,0:T(8,128)(2,1)S(1)}, u32[]{:S(2)}, u32[]{:S(2)}) collective-permute-start(bf16[144,1024]{1,0:T(8,128)(2,1)S(1)} %collective-permute-done.refs_1_), channel_id=1, source_target_pairs={{0,2},{2,4},{4,6},{6,7},{7,5},{5,3},{3,1},{1,0},{8,10},{10,12},{12... | collective-permute-start | bytes 884744 | tf_op jit(solution)/shard_map/ppermute | solution.py:198
  19.0 0.2 collective-permute-start.5
  19.3 6.2 %collective-permute-done.1.refs_2_ = bf16[144,1024]{1,0:T(8,128)(2,1)S(1)} collective-permute-done((bf16[144,1024]{1,0:T(8,128)(2,1)S(1)}, bf16[144,1024]{1,0:T(8,128)(2,1)S(1)}, u32[]{:S(2)}, u32[]{:S(2)}) %collective-permute-start.1) | collective-permute-done | bytes 294944 | tf_op jit(solution)/shard_map/ppermute | solution.py:198
  25.4 1.5 %collective-permute-start.2 = (bf16[144,1024]{1,0:T(8,128)(2,1)S(1)}, bf16[144,1024]{1,0:T(8,128)(2,1)S(1)}, u32[]{:S(2)}, u32[]{:S(2)}) collective-permute-start(bf16[144,1024]{1,0:T(8,128)(2,1)S(1)} %collective-permute-done.1.refs_2_), channel_id=1, source_target_pairs={{0,2},{2,4},{4,6},{6,7},{7,5},{5,3},{3,1},{1,0},{8,10},{10,12},{12... | collective-permute-start | bytes 884744 | tf_op jit(solution)/shard_map/ppermute | solution.py:198
  26.9 0.6 collective-permute-start.10
  27.6 1.4 %collective-permute-start.6 = (bf16[144,1024]{1,0:T(8,128)(2,1)S(1)}, bf16[144,1024]{1,0:T(8,128)(2,1)S(1)}, u32[]{:S(2)}, u32[]{:S(2)}) collective-permute-start(bf16[144,1024]{1,0:T(8,128)(2,1)S(1)} %collective-permute-done.5.refs_6_), channel_id=1, source_target_pairs={{2,0},{4,2},{6,4},{7,6},{5,7},{3,5},{1,3},{0,1},{10,8},{12,10},{14... | collective-permute-start | bytes 884744 | tf_op jit(solution)/shard_map/ppermute | solution.py:200
  29.0 3.7 %collective-permute-done.2.refs_3_ = bf16[144,1024]{1,0:T(8,128)(2,1)S(1)} collective-permute-done((bf16[144,1024]{1,0:T(8,128)(2,1)S(1)}, bf16[144,1024]{1,0:T(8,128)(2,1)S(1)}, u32[]{:S(2)}, u32[]{:S(2)}) %collective-permute-start.2) | collective-permute-done | bytes 294944 | tf_op jit(solution)/shard_map/ppermute | solution.py:198
  32.7 1.4 %collective-permute-start.3 = (bf16[144,1024]{1,0:T(8,128)(2,1)S(1)}, bf16[144,1024]{1,0:T(8,128)(2,1)S(1)}, u32[]{:S(2)}, u32[]{:S(2)}) collective-permute-start(bf16[144,1024]{1,0:T(8,128)(2,1)S(1)} %collective-permute-done.2.refs_3_), channel_id=1, source_target_pairs={{0,2},{2,4},{4,6},{6,7},{7,5},{5,3},{3,1},{1,0},{8,10},{10,12},{12... | collective-permute-start | bytes 884744 | tf_op jit(solution)/shard_map/ppermute | solution.py:198
  34.1 1.6 %collective-permute-start.7 = (bf16[128,1024]{1,0:T(8,128)(2,1)S(1)}, bf16[128,1024]{1,0:T(8,128)(2,1)S(1)}, u32[]{:S(2)}, u32[]{:S(2)}) collective-permute-start(bf16[128,1024]{1,0:T(8,128)(2,1)S(1)} %pad_maximum_fusion.1.refs_0_), channel_id=1, source_target_pairs={{0,2},{2,4},{4,6},{6,7},{7,5},{5,3},{3,1},{1,0},{8,10},{10,12},{12... | collective-permute-start | bytes 786440 | tf_op jit(solution)/shard_map/ppermute | solution.py:198
  35.7 0.6 collective-permute-done.10.refs_4_
  36.2 0.5 collective-permute-start.11
  36.8 0.1 pad_add_fusion.mine_ref
  36.9 0.7 fusion.order_ref
  37.6 8.0 %collective-permute-done.7.refs_1_ = bf16[128,1024]{1,0:T(8,128)(2,1)S(1)} collective-permute-done((bf16[128,1024]{1,0:T(8,128)(2,1)S(1)}, bf16[128,1024]{1,0:T(8,128)(2,1)S(1)}, u32[]{:S(2)}, u32[]{:S(2)}) %collective-permute-start.7) | collective-permute-done | bytes 262176 | tf_op jit(solution)/shard_map/ppermute | solution.py:198
  45.5 1.4 %collective-permute-start.8 = (bf16[128,1024]{1,0:T(8,128)(2,1)S(1)}, bf16[128,1024]{1,0:T(8,128)(2,1)S(1)}, u32[]{:S(2)}, u32[]{:S(2)}) collective-permute-start(bf16[128,1024]{1,0:T(8,128)(2,1)S(1)} %collective-permute-done.7.refs_1_), channel_id=1, source_target_pairs={{0,2},{2,4},{4,6},{6,7},{7,5},{5,3},{3,1},{1,0},{8,10},{10,12},{12... | collective-permute-start | bytes 786440 | tf_op jit(solution)/shard_map/ppermute | solution.py:198
  46.9 0.6 collective-permute-start.12
  47.6 1.8 %copy-done = bf16[1,8,128,1408]{3,2,1,0:T(8,128)(2,1)S(1)} copy-done((bf16[1,8,128,1408]{3,2,1,0:T(8,128)(2,1)S(1)}, bf16[1,8,128,1408]{3,2,1,0:T(8,128)(2,1)}, u32[]{:S(2)}) %copy-start) | copy-done | bytes 2883608
  49.4 5.4 %shard_map.95 = (bf16[1024,1024]{1,0:T(8,128)(2,1)S(1)}, bf16[1024,1408]{1,0:T(8,128)(2,1)S(1)}, f32[8,256]{1,0:T(8,128)S(1)}) custom-call(s32[2]{0:T(128)S(1)} %pad_add_fusion.mine_ref, s32[8]{0:T(128)S(1)} %fusion.order_ref, bf16[144,1024]{1,0:T(8,128)(2,1)S(1)} %pad_maximum_fusion.refs_0_, bf16[144,1024]{1,0:T(8,128)(2,1)S(1)} %collective-permute-done.refs_1_, ...), custom_call_target="tpu_custom_call" | custom-call | flops 2952790016 | bytes 8388608 | tf_op jit(solution)/shard_map/pallas_call | solution.py:213
  54.8 0.1 slice.25
  54.9 0.1 collective-permute-start.14
  55.0 1.4 %collective-permute-start.9 = (bf16[128,1024]{1,0:T(8,128)(2,1)S(1)}, bf16[128,1024]{1,0:T(8,128)(2,1)S(1)}, u32[]{:S(2)}, u32[]{:S(2)}) collective-permute-start(bf16[128,1024]{1,0:T(8,128)(2,1)S(1)} %collective-permute-done.8.refs_2_), channel_id=1, source_target_pairs={{0,2},{2,4},{4,6},{6,7},{7,5},{5,3},{3,1},{1,0},{8,10},{10,12},{12... | collective-permute-start | bytes 786440 | tf_op jit(solution)/shard_map/ppermute | solution.py:198
  56.4 0.6 collective-permute-start.13
  57.0 0.7 fusion.1.order_ref
  57.7 5.9 %collective-permute-done.9.refs_3_ = bf16[128,1024]{1,0:T(8,128)(2,1)S(1)} collective-permute-done((bf16[128,1024]{1,0:T(8,128)(2,1)S(1)}, bf16[128,1024]{1,0:T(8,128)(2,1)S(1)}, u32[]{:S(2)}, u32[]{:S(2)}) %collective-permute-start.9) | collective-permute-done | bytes 262176 | tf_op jit(solution)/shard_map/ppermute | solution.py:198
  63.7 1.1 %collective-permute-done.13.refs_7_ = bf16[128,1024]{1,0:T(8,128)(2,1)S(1)} collective-permute-done((bf16[128,1024]{1,0:T(8,128)(2,1)S(1)}, bf16[128,1024]{1,0:T(8,128)(2,1)S(1)}, u32[]{:S(2)}, u32[]{:S(2)}) %collective-permute-start.13) | collective-permute-done | bytes 262176 | tf_op jit(solution)/shard_map/ppermute | solution.py:200
  64.8 5.3 %shard_map.96 = (bf16[1024,1024]{1,0:T(8,128)(2,1)S(1)}, bf16[1024,1408]{1,0:T(8,128)(2,1)S(1)}) custom-call(s32[2]{0:T(128)S(1)} %pad_add_fusion.mine_ref, s32[8]{0:T(128)S(1)} %fusion.1.order_ref, bf16[128,1024]{1,0:T(8,128)(2,1)S(1)} %pad_maximum_fusion.1.refs_0_, bf16[128,1024]{1,0:T(8,128)(2,1)S(1)} %collective-permute-done.7.refs_1_, ...), custom_call_target="tpu_custom_call" | custom-call | flops 2952790016 | bytes 8388608 | tf_op jit(solution)/shard_map/pallas_call | solution.py:213
  70.1 0.1 slice.29
  70.2 0.1 collective-permute-start.16
  70.3 0.3 add_convert_fusion.1
  70.7 0.1 slice.33
  70.7 1.6 %collective-permute-start.15 = (bf16[256,1408]{1,0:T(8,128)(2,1)S(1)}, bf16[256,1408]{1,0:T(8,128)(2,1)S(1)}, u32[]{:S(2)}, u32[]{:S(2)}) collective-permute-start(bf16[256,1408]{1,0:T(8,128)(2,1)S(1)} %slice.33), channel_id=1, source_target_pairs={{0,16},{8,24},{16,0},{24,8},{1,17},{9,25},{17,1},{25,9},{2,18},{10... | collective-permute-start | bytes 2162696 | tf_op jit(solution)/shard_map/ppermute | solution.py:260
  72.3 1.2 %collective-permute-done.16 = bf16[512,1408]{1,0:T(8,128)(2,1)S(1)} collective-permute-done((bf16[512,1408]{1,0:T(8,128)(2,1)S(1)}, bf16[512,1408]{1,0:T(8,128)(2,1)S(1)}, u32[]{:S(2)}, u32[]{:S(2)}) %collective-permute-start.16) | collective-permute-done | bytes 1441824 | tf_op jit(solution)/shard_map/ppermute | solution.py:260
  73.5 0.3 add_convert_fusion
  73.9 1.6 %collective-permute-start.17 = (bf16[256,1408]{1,0:T(8,128)(2,1)S(1)}, bf16[256,1408]{1,0:T(8,128)(2,1)S(1)}, u32[]{:S(2)}, u32[]{:S(2)}) collective-permute-start(bf16[256,1408]{1,0:T(8,128)(2,1)S(1)} %slice.35), channel_id=1, source_target_pairs={{0,16},{8,24},{16,0},{24,8},{1,17},{9,25},{17,1},{25,9},{2,18},{10... | collective-permute-start | bytes 2162696 | tf_op jit(solution)/shard_map/ppermute | solution.py:260
  75.5 9.2 %shard_map.97 = (bf16[1024,1408]{1,0:T(8,128)(2,1)}, f32[8,128]{1,0:T(8,128)S(1)}) custom-call(s32[2]{0:T(128)S(1)} %pad_add_fusion.mine_ref, bf16[1024,1024]{1,0:T(8,128)(2,1)S(1)} %get-tuple-element.10.refs_0_, bf16[1024,1024]{1,0:T(8,128)(2,1)S(1)} %get-tuple-element.12.refs_1_, f32[8,256]{1,0:T(8,128)S(1)} %get-tuple-element.11.refs_8_.refs_2_, ...), custom_call_target="tpu_custom_call" | custom-call | flops 5905580032 | bytes 16777216 | tf_op jit(solution)/shard_map/pallas_call | solution.py:231
  84.6 11.1 %all_to_all.12 = f32[8,1,128]{2,1,0:T(1,128)S(1)} all-to-all(f32[8,1,128]{2,1,0:T(1,128)S(1)} %bitcast.17), channel_id=1, replica_groups=mesh['dp'=4,'expert'=8] {'expert'}, dimensions={0} | all-to-all | bytes 8192 | tf_op jit(solution)/shard_map/all_to_all | solution.py:269
  95.7 0.6 select_reduce_fusion
  96.3 0.2 add_convert_fusion.3
  96.5 8.2 %collective-permute-done.17 = bf16[256,1408]{1,0:T(8,128)(2,1)S(1)} collective-permute-done((bf16[256,1408]{1,0:T(8,128)(2,1)S(1)}, bf16[256,1408]{1,0:T(8,128)(2,1)S(1)}, u32[]{:S(2)}, u32[]{:S(2)}) %collective-permute-start.17) | collective-permute-done | bytes 720928 | tf_op jit(solution)/shard_map/ppermute | solution.py:260
  104.8 0.2 add_convert_fusion.2
  105.0 1.2 %maximum_bitcast_fusion = bf16[1,512,1408]{2,1,0:T(8,128)(2,1)} fusion(bf16[256,1408]{1,0:T(8,128)(2,1)S(1)} %add_convert_fusion.2, bf16[256,1408]{1,0:T(8,128)(2,1)S(1)} %add_convert_fusion.3), kind=kLoop, calls=%fused_computation.2 | loop fusion | flops 2883584 | bytes 2883584 | tf_op jit(solution)/shard_map/broadcast_in_dim | solution.py:267
  (22 shorter events, 0.1 us)
Async XLA Ops:
  7.2 10.0 %collective-permute-start = (bf16[144,1024]{1,0:T(8,128)(2,1)S(1)}, bf16[144,1024]{1,0:T(8,128)(2,1)S(1)}, u32[]{:S(2)}, u32[]{:S(2)}) collective-permute-start(bf16[144,1024]{1,0:T(8,128)(2,1)S(1)} %pad_maximum_fusion.refs_0_), channel_id=1, source_target_pairs={{0,2},{2,4},{4,6},{6,7},{7,5},{5,3},{3,1},{1,0},{8,10},{10,12},{12... | collective-permute-start | bytes 884744 | tf_op jit(solution)/shard_map/ppermute | solution.py:198
  10.3 8.8 %collective-permute-start.4 = (bf16[144,1024]{1,0:T(8,128)(2,1)S(1)}, bf16[144,1024]{1,0:T(8,128)(2,1)S(1)}, u32[]{:S(2)}, u32[]{:S(2)}) collective-permute-start(bf16[144,1024]{1,0:T(8,128)(2,1)S(1)} %pad_maximum_fusion.refs_0_), channel_id=1, source_target_pairs={{2,0},{4,2},{6,4},{7,6},{5,7},{3,5},{1,3},{0,1},{10,8},{12,10},{14... | collective-permute-start | bytes 884744 | tf_op jit(solution)/shard_map/ppermute | solution.py:200
  17.2 8.2 %collective-permute-start.1 = (bf16[144,1024]{1,0:T(8,128)(2,1)S(1)}, bf16[144,1024]{1,0:T(8,128)(2,1)S(1)}, u32[]{:S(2)}, u32[]{:S(2)}) collective-permute-start(bf16[144,1024]{1,0:T(8,128)(2,1)S(1)} %collective-permute-done.refs_1_), channel_id=1, source_target_pairs={{0,2},{2,4},{4,6},{6,7},{7,5},{5,3},{3,1},{1,0},{8,10},{10,12},{12... | collective-permute-start | bytes 884744 | tf_op jit(solution)/shard_map/ppermute | solution.py:198
  19.0 8.5 %collective-permute-start.5 = (bf16[144,1024]{1,0:T(8,128)(2,1)S(1)}, bf16[144,1024]{1,0:T(8,128)(2,1)S(1)}, u32[]{:S(2)}, u32[]{:S(2)}) collective-permute-start(bf16[144,1024]{1,0:T(8,128)(2,1)S(1)} %collective-permute-done.4.refs_5_), channel_id=1, source_target_pairs={{2,0},{4,2},{6,4},{7,6},{5,7},{3,5},{1,3},{0,1},{10,8},{12,10},{14... | collective-permute-start | bytes 884744 | tf_op jit(solution)/shard_map/ppermute | solution.py:200
  25.4 7.3 %collective-permute-start.2 = (bf16[144,1024]{1,0:T(8,128)(2,1)S(1)}, bf16[144,1024]{1,0:T(8,128)(2,1)S(1)}, u32[]{:S(2)}, u32[]{:S(2)}) collective-permute-start(bf16[144,1024]{1,0:T(8,128)(2,1)S(1)} %collective-permute-done.1.refs_2_), channel_id=1, source_target_pairs={{0,2},{2,4},{4,6},{6,7},{7,5},{5,3},{3,1},{1,0},{8,10},{10,12},{12... | collective-permute-start | bytes 884744 | tf_op jit(solution)/shard_map/ppermute | solution.py:198
  26.9 9.3 %collective-permute-start.10 = (bf16[128,1024]{1,0:T(8,128)(2,1)S(1)}, bf16[128,1024]{1,0:T(8,128)(2,1)S(1)}, u32[]{:S(2)}, u32[]{:S(2)}) collective-permute-start(bf16[128,1024]{1,0:T(8,128)(2,1)S(1)} %pad_maximum_fusion.1.refs_0_), channel_id=1, source_target_pairs={{2,0},{4,2},{6,4},{7,6},{5,7},{3,5},{1,3},{0,1},{10,8},{12,10},{14... | collective-permute-start | bytes 786440 | tf_op jit(solution)/shard_map/ppermute | solution.py:200
  27.6 20.0 %collective-permute-start.6 = (bf16[144,1024]{1,0:T(8,128)(2,1)S(1)}, bf16[144,1024]{1,0:T(8,128)(2,1)S(1)}, u32[]{:S(2)}, u32[]{:S(2)}) collective-permute-start(bf16[144,1024]{1,0:T(8,128)(2,1)S(1)} %collective-permute-done.5.refs_6_), channel_id=1, source_target_pairs={{2,0},{4,2},{6,4},{7,6},{5,7},{3,5},{1,3},{0,1},{10,8},{12,10},{14... | collective-permute-start | bytes 884744 | tf_op jit(solution)/shard_map/ppermute | solution.py:200
  32.7 14.8 %collective-permute-start.3 = (bf16[144,1024]{1,0:T(8,128)(2,1)S(1)}, bf16[144,1024]{1,0:T(8,128)(2,1)S(1)}, u32[]{:S(2)}, u32[]{:S(2)}) collective-permute-start(bf16[144,1024]{1,0:T(8,128)(2,1)S(1)} %collective-permute-done.2.refs_3_), channel_id=1, source_target_pairs={{0,2},{2,4},{4,6},{6,7},{7,5},{5,3},{3,1},{1,0},{8,10},{10,12},{12... | collective-permute-start | bytes 884744 | tf_op jit(solution)/shard_map/ppermute | solution.py:198
  34.1 11.4 %collective-permute-start.7 = (bf16[128,1024]{1,0:T(8,128)(2,1)S(1)}, bf16[128,1024]{1,0:T(8,128)(2,1)S(1)}, u32[]{:S(2)}, u32[]{:S(2)}) collective-permute-start(bf16[128,1024]{1,0:T(8,128)(2,1)S(1)} %pad_maximum_fusion.1.refs_0_), channel_id=1, source_target_pairs={{0,2},{2,4},{4,6},{6,7},{7,5},{5,3},{3,1},{1,0},{8,10},{10,12},{12... | collective-permute-start | bytes 786440 | tf_op jit(solution)/shard_map/ppermute | solution.py:198
  36.2 10.7 %collective-permute-start.11 = (bf16[128,1024]{1,0:T(8,128)(2,1)S(1)}, bf16[128,1024]{1,0:T(8,128)(2,1)S(1)}, u32[]{:S(2)}, u32[]{:S(2)}) collective-permute-start(bf16[128,1024]{1,0:T(8,128)(2,1)S(1)} %collective-permute-done.10.refs_4_), channel_id=1, source_target_pairs={{2,0},{4,2},{6,4},{7,6},{5,7},{3,5},{1,3},{0,1},{10,8},{12,10},{14... | collective-permute-start | bytes 786440 | tf_op jit(solution)/shard_map/ppermute | solution.py:200
  45.5 9.4 %collective-permute-start.8 = (bf16[128,1024]{1,0:T(8,128)(2,1)S(1)}, bf16[128,1024]{1,0:T(8,128)(2,1)S(1)}, u32[]{:S(2)}, u32[]{:S(2)}) collective-permute-start(bf16[128,1024]{1,0:T(8,128)(2,1)S(1)} %collective-permute-done.7.refs_1_), channel_id=1, source_target_pairs={{0,2},{2,4},{4,6},{6,7},{7,5},{5,3},{3,1},{1,0},{8,10},{10,12},{12... | collective-permute-start | bytes 786440 | tf_op jit(solution)/shard_map/ppermute | solution.py:198
  46.9 9.5 %collective-permute-start.12 = (bf16[128,1024]{1,0:T(8,128)(2,1)S(1)}, bf16[128,1024]{1,0:T(8,128)(2,1)S(1)}, u32[]{:S(2)}, u32[]{:S(2)}) collective-permute-start(bf16[128,1024]{1,0:T(8,128)(2,1)S(1)} %collective-permute-done.11.refs_5_), channel_id=1, source_target_pairs={{2,0},{4,2},{6,4},{7,6},{5,7},{3,5},{1,3},{0,1},{10,8},{12,10},{14... | collective-permute-start | bytes 786440 | tf_op jit(solution)/shard_map/ppermute | solution.py:200
  47.5 1.8 %copy-start = (bf16[1,8,128,1408]{3,2,1,0:T(8,128)(2,1)S(1)}, bf16[1,8,128,1408]{3,2,1,0:T(8,128)(2,1)}, u32[]{:S(2)}) copy-start(bf16[1,8,128,1408]{3,2,1,0:T(8,128)(2,1)} %param.10) | copy-start | bytes 8650756
  54.7 10.0 %copy-start.1 = (bf16[1,8,128,1408]{3,2,1,0:T(8,128)(2,1)S(1)}, bf16[1,8,128,1408]{3,2,1,0:T(8,128)(2,1)}, u32[]{:S(2)}) copy-start(bf16[1,8,128,1408]{3,2,1,0:T(8,128)(2,1)} %param.10) | copy-start | bytes 8650756
  54.9 15.4 %collective-permute-start.14 = (bf16[512,1408]{1,0:T(8,128)(2,1)S(1)}, bf16[512,1408]{1,0:T(8,128)(2,1)S(1)}, u32[]{:S(2)}, u32[]{:S(2)}) collective-permute-start(bf16[512,1408]{1,0:T(8,128)(2,1)S(1)} %slice.25), channel_id=1, source_target_pairs={{0,8},{8,0},{16,24},{24,16},{1,9},{9,1},{17,25},{25,17},{2,10},{10... | collective-permute-start | bytes 4325384 | tf_op jit(solution)/shard_map/ppermute | solution.py:260
  55.0 8.7 %collective-permute-start.9 = (bf16[128,1024]{1,0:T(8,128)(2,1)S(1)}, bf16[128,1024]{1,0:T(8,128)(2,1)S(1)}, u32[]{:S(2)}, u32[]{:S(2)}) collective-permute-start(bf16[128,1024]{1,0:T(8,128)(2,1)S(1)} %collective-permute-done.8.refs_2_), channel_id=1, source_target_pairs={{0,2},{2,4},{4,6},{6,7},{7,5},{5,3},{3,1},{1,0},{8,10},{10,12},{12... | collective-permute-start | bytes 786440 | tf_op jit(solution)/shard_map/ppermute | solution.py:198
  56.4 8.4 %collective-permute-start.13 = (bf16[128,1024]{1,0:T(8,128)(2,1)S(1)}, bf16[128,1024]{1,0:T(8,128)(2,1)S(1)}, u32[]{:S(2)}, u32[]{:S(2)}) collective-permute-start(bf16[128,1024]{1,0:T(8,128)(2,1)S(1)} %collective-permute-done.12.refs_6_), channel_id=1, source_target_pairs={{2,0},{4,2},{6,4},{7,6},{5,7},{3,5},{1,3},{0,1},{10,8},{12,10},{14... | collective-permute-start | bytes 786440 | tf_op jit(solution)/shard_map/ppermute | solution.py:200
  64.8 10.7 %slice-start = ((s8[5767168]{0:T(1024)(128)(4,1)}), s8[4194304]{0:T(1024)(128)(4,1)S(1)}, s32[]{:S(2)}) async-start(s8[5767168]{0:T(1024)(128)(4,1)} %bitcast.18), calls=%async_computation.1 | async-start | bytes 8388608
  70.1 5.4 %slice-start.1 = ((s8[5767168]{0:T(1024)(128)(4,1)}), s8[1572864]{0:T(1024)(128)(4,1)S(1)}, s32[]{:S(2)}) async-start(s8[5767168]{0:T(1024)(128)(4,1)} %bitcast.18), calls=%async_computation.2 | async-start | bytes 3145728
  70.2 3.3 %collective-permute-start.16 = (bf16[512,1408]{1,0:T(8,128)(2,1)S(1)}, bf16[512,1408]{1,0:T(8,128)(2,1)S(1)}, u32[]{:S(2)}, u32[]{:S(2)}) collective-permute-start(bf16[512,1408]{1,0:T(8,128)(2,1)S(1)} %slice.29), channel_id=1, source_target_pairs={{0,8},{8,0},{16,24},{24,16},{1,9},{9,1},{17,25},{25,17},{2,10},{10... | collective-permute-start | bytes 4325384 | tf_op jit(solution)/shard_map/ppermute | solution.py:260
  70.7 25.6 %collective-permute-start.15 = (bf16[256,1408]{1,0:T(8,128)(2,1)S(1)}, bf16[256,1408]{1,0:T(8,128)(2,1)S(1)}, u32[]{:S(2)}, u32[]{:S(2)}) collective-permute-start(bf16[256,1408]{1,0:T(8,128)(2,1)S(1)} %slice.33), channel_id=1, source_target_pairs={{0,16},{8,24},{16,0},{24,8},{1,17},{9,25},{17,1},{25,9},{2,18},{10... | collective-permute-start | bytes 2162696 | tf_op jit(solution)/shard_map/ppermute | solution.py:260
  73.9 30.8 %collective-permute-start.17 = (bf16[256,1408]{1,0:T(8,128)(2,1)S(1)}, bf16[256,1408]{1,0:T(8,128)(2,1)S(1)}, u32[]{:S(2)}, u32[]{:S(2)}) collective-permute-start(bf16[256,1408]{1,0:T(8,128)(2,1)S(1)} %slice.35), channel_id=1, source_target_pairs={{0,16},{8,24},{16,0},{24,8},{1,17},{9,25},{17,1},{25,9},{2,18},{10... | collective-permute-start | bytes 2162696 | tf_op jit(solution)/shard_map/ppermute | solution.py:260
  75.5 20.2 %copy-start.2 = (s32[128,6]{0,1:T(8,128)S(1)}, s32[128,6]{0,1:T(8,128)}, u32[]{:S(2)}) copy-start(s32[128,6]{0,1:T(8,128)} %param.9) | copy-start | bytes 9220

commit v2 on v0

v2 whole, which is shorter than its diff:
```python
import functools

import jax
import jax.numpy as jnp
import numpy as np
from jax import lax
from jax.experimental import pallas as pl
from jax.experimental.pallas import tpu as pltpu
from jax.sharding import PartitionSpec as P

MIB = 1024 * 1024
CHUNKS = 2
CUTS = (12, 18, 26)


def cycle_of(count):
    bits = count.bit_length() - 1
    if count != 1 << bits or count < 4:
        return list(range(count))
    width = 1 << (bits // 2)
    depth = count // width
    walk = [z * width for z in range(depth)]
    for turn, z in enumerate(reversed(range(depth))):
        columns = list(range(1, width))
        walk += [z * width + y for y in (columns if turn % 2 == 0 else columns[::-1])]
    return walk


def offsets_of(count, chunk):
    far = count // 2
    behind = far - 1
    ahead = count - 2 - behind
    near = [-k for k in range(1, behind + 1)] + [k for k in range(1, ahead + 1)]
    return [0] + near + [-far if chunk % 2 == 0 else count - far]


def order_table(count, chunk):
    walk = cycle_of(count)
    place = {expert: at for at, expert in enumerate(walk)}
    offsets = offsets_of(count, chunk)
    return np.array(
        [[walk[(place[e] + o) % count] for o in offsets] for e in range(count)], np.int32
    )


def head_kernel(experts, masks, mine_ref, ids_ref, combine_ref, grad_ref, *own_refs):
    picks, rows = ids_ref.shape
    dp = mine_ref[1]
    columns = own_refs[0].shape[1]
    for c, own in enumerate(own_refs):
        wide = columns // len(masks[c])
        for j, mask in enumerate(masks[c]):
            start = pl.multiple_of((dp ^ mask) * wide, wide)
            own[:rows, j * wide : (j + 1) * wide] = grad_ref[:, pl.ds(start, wide)]
    ids = ids_ref[...]
    weights = combine_ref[...].astype(jnp.float32)
    line = lax.broadcasted_iota(jnp.int32, (experts, rows), 0)
    named = jnp.zeros((experts, rows), jnp.float32)
    prob = jnp.zeros((experts, rows), jnp.float32)
    for k in range(picks):
        hit = ids[k : k + 1, :] == line
        named = jnp.where(hit, 1.0, named)
        prob = jnp.where(hit, weights[k : k + 1, :], prob)
    earlier = (
        lax.broadcasted_iota(jnp.int32, (rows, rows), 0)
        < lax.broadcasted_iota(jnp.int32, (rows, rows), 1)
    ).astype(jnp.bfloat16)
    before = jnp.dot(named.astype(jnp.bfloat16), earlier, preferred_element_type=jnp.float32)
    slot = jnp.where(named > 0.5, before, -1.0)
    both = jnp.concatenate([prob, slot], axis=0).astype(jnp.bfloat16)
    groups = 2 * experts // 16
    for group in range(groups):
        own_refs[0][rows:, group * rows : (group + 1) * rows] = both[group * 16 : (group + 1) * 16]
    if groups * rows < columns:
        own_refs[0][rows:, groups * rows :] = jnp.zeros((16, columns - groups * rows), jnp.bfloat16)


def row_of(block, expert, count, tokens):
    sub = lax.broadcasted_iota(jnp.int32, (16, tokens), 0)
    prob = jnp.zeros((1, tokens), jnp.float32)
    slot = jnp.zeros((1, tokens), jnp.float32)
    for group in range(2 * count // 16):
        piece = block[tokens : tokens + 16, group * tokens : (group + 1) * tokens]
        piece = piece.astype(jnp.float32)
        row = sub + group * 16
        prob = prob + jnp.sum(jnp.where(row == expert, piece, 0.0), 0, keepdims=True)
        slot = slot + jnp.sum(jnp.where(row == expert + count, piece, 0.0), 0, keepdims=True)
    return jnp.concatenate([prob, slot], axis=1)


def weights_of(row, cap, tokens):
    at = lax.broadcasted_iota(jnp.int32, (cap, tokens), 0).astype(jnp.float32)
    return jnp.where(row[:, tokens:] == at, row[:, :tokens], 0.0).astype(jnp.bfloat16)


def product(left, right):
    return lax.dot_general(
        left, right, (((0,), (0,)), ((), ())), preferred_element_type=jnp.float32
    )


def early_kernel(at_order, count, cap, tokens, where_ref, *refs):
    blocks, refs = refs[: count - 1], refs[count - 1 :]
    hidden_ref, rows_ref, placed_ref, *sum_refs, scaled_ref = refs
    rows_ref[...] = jnp.zeros_like(rows_ref)
    for i in range(count):
        source = where_ref[at_order + i]
        here = pl.ds(pl.multiple_of(source * cap, cap), cap)
        if i == count - 1:
            scaled_ref[here, :] = jnp.zeros((cap, scaled_ref.shape[1]), jnp.bfloat16)
            continue
        row = row_of(blocks[i], where_ref[0], count, tokens)
        rows_ref[pl.ds(source, 1), :] = row
        spread(row, cap, tokens, blocks[i][:tokens, :], here, placed_ref, scaled_ref)
    wide = sum_refs[0].shape[0]
    for j, sum_ref in enumerate(sum_refs):
        sum_ref[...] = product(scaled_ref[:, j * wide : (j + 1) * wide], hidden_ref[...])


def spread(row, cap, tokens, grads, here, placed_ref, scaled_ref):
    at = lax.broadcasted_iota(jnp.int32, (cap, tokens), 0).astype(jnp.float32)
    hit = row[:, tokens:] == at
    for weight, out_ref in ((1.0, placed_ref), (row[:, :tokens], scaled_ref)):
        pick = jnp.where(hit, weight, 0.0).astype(jnp.bfloat16)
        out_ref[here, :] = jnp.dot(pick, grads, preferred_element_type=jnp.float32).astype(
            jnp.bfloat16
        )


def late_kernel(at_order, count, cap, tokens, where_ref, block_ref, near_ref, hidden_ref, *refs):
    *refs, rows_ref = refs
    source = where_ref[at_order + count - 1]
    row = row_of(block_ref, where_ref[0], count, tokens)
    rows_ref[...] = near_ref[...]
    rows_ref[pl.ds(source, 1), :] = row
    sum_refs, part_refs = refs[: len(refs) // 2], refs[len(refs) // 2 :]
    wide = sum_refs[0].shape[0]
    scaled = jnp.dot(
        weights_of(row, cap, tokens), block_ref[:tokens, :], preferred_element_type=jnp.float32
    ).astype(jnp.bfloat16)
    saved = hidden_ref[pl.ds(pl.multiple_of(source * cap, cap), cap), :]
    for j, (sum_ref, part_ref) in enumerate(zip(sum_refs, part_refs)):
        part_ref[...] = (
            sum_ref[...] + product(scaled[:, j * wide : (j + 1) * wide], saved)
        ).astype(jnp.bfloat16)


def part_kernel(scaled_ref, hidden_ref, *part_refs):
    wide = part_refs[0].shape[0]
    for j, part_ref in enumerate(part_refs):
        here = slice(j * wide, (j + 1) * wide)
        part_ref[...] = product(scaled_ref[:, here], hidden_ref[...]).astype(jnp.bfloat16)


def final_kernel(kept_ref, moved_ref, *refs):
    out_ref = refs[-1]
    low = 0
    for ref in refs[:-1]:
        here = slice(low, low + ref.shape[0])
        out_ref[here, :] = (
            kept_ref[here, :].astype(jnp.float32)
            + moved_ref[here, :].astype(jnp.float32)
            + ref[...].astype(jnp.float32)
        ).astype(out_ref.dtype)
        low += ref.shape[0]


def projected(rows, dp, masks, w_ref, wide):
    acc = None
    for j, mask in enumerate(masks):
        start = pl.multiple_of((dp ^ mask) * wide, wide)
        term = jnp.dot(
            rows[:, j * wide : (j + 1) * wide],
            w_ref[pl.ds(start, wide), :],
            preferred_element_type=jnp.float32,
        )
        acc = term if acc is None else acc + term
    return acc


def project_kernel(at_order, masks, count, cap, tokens, size, where_ref, block_ref, *refs):
    rows_ref, near_ref, w_ref, sum_ref, placed_ref = refs
    source = where_ref[at_order + count - 1]
    here = pl.ds(pl.multiple_of(source * cap, cap), cap)
    at = lax.broadcasted_iota(jnp.int32, (cap, tokens), 0).astype(jnp.float32)
    hit = rows_ref[pl.ds(source, 1), :][:, tokens:] == at
    placed_ref[...] = near_ref[...]
    placed_ref[here, :] = jnp.dot(
        jnp.where(hit, 1.0, 0.0).astype(jnp.bfloat16),
        block_ref[:tokens, :],
        preferred_element_type=jnp.float32,
    ).astype(jnp.bfloat16)
    wide = placed_ref.shape[1] // len(masks)

    def some(step, carry):
        here = pl.ds(pl.multiple_of(step * size, size), size)
        sum_ref[here, :] = projected(placed_ref[here, :], where_ref[1], masks, w_ref, wide)
        return carry

    lax.fori_loop(0, placed_ref.shape[0] // size, some, 0)


def finish(acc, row, cap, tokens, saved, grad_ref, here, token_ref, line):
    at = lax.broadcasted_iota(jnp.int32, (cap, tokens), 0).astype(jnp.float32)
    hit = row[:, tokens:] == at
    column = jnp.sum(jnp.where(hit, row[:, :tokens], 0.0), axis=1, keepdims=True)
    grad_ref[here, :] = (column * acc).astype(jnp.bfloat16)
    slot_grad = jnp.sum(acc * saved.astype(jnp.float32), axis=1, keepdims=True)
    token_ref[pl.ds(line, 1), :] = jnp.sum(
        jnp.where(hit, slot_grad, 0.0), axis=0, keepdims=True
    )


def finish_kernel(at_order, masks, count, cap, tokens, size, where_ref, *refs):
    blocks, refs = refs[:count], refs[count:]
    rows_ref, w_ref, before_ref, hidden_ref, grad_ref, token_ref, scaled_ref, placed_ref = refs
    wide = placed_ref.shape[1] // len(masks)
    for i in range(count):
        source = where_ref[at_order + i]
        here = pl.ds(pl.multiple_of(source * cap, cap), cap)
        row = rows_ref[pl.ds(source, 1), :]
        spread(row, cap, tokens, blocks[i][:tokens, :], here, placed_ref, scaled_ref)

    def some(step, carry):
        first = pl.multiple_of(step * size, size)
        here = pl.ds(first, size)
        acc = projected(placed_ref[here, :], where_ref[1], masks, w_ref, wide)
        acc = acc + before_ref[here, :]
        saved = hidden_ref[here, :]
        for g in range(size // cap):
            source = step * (size // cap) + g
            part = slice(g * cap, (g + 1) * cap)
            there = pl.ds(pl.multiple_of(first + g * cap, cap), cap)
            row = rows_ref[pl.ds(source, 1), :]
            line = source
            finish(acc[part], row, cap, tokens, saved[part], grad_ref, there, token_ref, line)
        return carry

    lax.fori_loop(0, placed_ref.shape[0] // size, some, 0)


def after(value, *others):
    return lax.optimization_barrier((value, *others))[0]


def body(replicas, out_grad, combine, expert_ids, hidden, w_down):
    tokens, width = out_grad.shape
    _, count, cap, inner = hidden.shape
    slots = count * cap
    mine = lax.axis_index("expert")
    dp = lax.axis_index("dp")
    where = jnp.stack([mine, dp]).astype(jnp.int32)
    hidden2 = hidden.reshape(slots, inner)
    weight = w_down.reshape(width, inner)
    columns = width // CHUNKS
    bits = replicas.bit_length() - 1
    top = replicas // 2
    masks = sorted(range(top), key=lambda m: [-(m >> b & 1) for b in range(bits)])
    masks = [[m | top for m in masks], masks]

    table = np.concatenate([order_table(count, c) for c in range(CHUNKS)], axis=1)
    table = np.array(
        [[e, r, *table[e]] for r in range(replicas) for e in range(count)], np.int32
    )
    places = lax.dynamic_slice(jnp.asarray(table), (dp * count + mine, 0), (1, table.shape[1]))[0]

    vmem = pl.BlockSpec(memory_space=pltpu.VMEM)
    smem = pl.BlockSpec(memory_space=pltpu.SMEM)
    anywhere = pl.BlockSpec(memory_space=pl.ANY)
    own = pl.pallas_call(
        functools.partial(head_kernel, count, masks),
        out_shape=[
            jax.ShapeDtypeStruct((tokens + (16 if c == 0 else 0), columns), jnp.bfloat16)
            for c in range(CHUNKS)
        ],
        grid=(1,),
        in_specs=[smem]
        + [
            pl.BlockSpec(v.shape, lambda i: (0, 0)) for v in (expert_ids.T, combine.T, out_grad)
        ],
        out_specs=[vmem] * CHUNKS,
        compiler_params=pltpu.CompilerParams(vmem_limit_bytes=8 * MIB),
    )(where, expert_ids.T, combine.T, out_grad)

    walk = cycle_of(count)
    forth = [(walk[i], walk[(i + 1) % count]) for i in range(count)]
    back = [(b, a) for a, b in forth]
    got = [{0: own[c]} for c in range(CHUNKS)]

    def step(chunk, k, *others):
        offsets = offsets_of(count, chunk)
        for sign, pairs in ((-1, forth), (1, back)):
            if sign * k in offsets:
                value = got[chunk][sign * (k - 1)]
                if others:
                    value = after(value, *others)
                got[chunk][sign * k] = lax.ppermute(value, "expert", pairs)

    wide = width // replicas

    def call(kernel, outs, args, scratch=(), limit=16, aliases=None):
        return pl.pallas_call(
            kernel,
            out_shape=[jax.ShapeDtypeStruct(*out) for out in outs],
            in_specs=[smem] + [vmem] * len(args),
            out_specs=[vmem] * len(outs),
            scratch_shapes=[pltpu.VMEM(*s) for s in scratch],
            input_output_aliases=aliases or {},
            compiler_params=pltpu.CompilerParams(vmem_limit_bytes=limit * MIB),
        )(places, *args)

    bf16, f32 = jnp.bfloat16, jnp.float32
    all_placed = ((slots, columns), bf16)
    piece = ((wide, inner), bf16)
    table = ((count, 2 * tokens), f32)
    size = max(1, 256 // cap) * cap

    def add(kept, arrived):
        return (kept.astype(jnp.float32) + arrived.astype(jnp.float32)).astype(jnp.bfloat16)

    def exchange(value, b):
        return lax.ppermute(value, "dp", [(r, r ^ (1 << b)) for r in range(replicas)])

    def reduced(parts, moved):
        for b in range(1, bits - 1):
            half = len(parts) // 2
            leaves = [add(k, a) for k, a in zip(parts[:half], moved[:half])]
            parts = [add(k, a) for k, a in zip(parts[half:], moved[half:])]
            moved = [exchange(v, b) for v in leaves]
        return parts[0], moved[0]

    far = count // 2
    at0, at1 = 2, 2 + count
    for k in range(1, far + 1):
        step(0, k, *([places] if k == 2 else []))
    step(1, 1, got[0][1 - far], got[0][far - 1])
    held = [got[0][o] for o in offsets_of(count, 0)]
    rows, placed, *sums = call(
        functools.partial(early_kernel, at0, count, cap, tokens),
        [table, all_placed] + [((wide, inner), f32)] * top,
        [*held[:-1], hidden2],
        [all_placed],
    )
    last = after(held[-1], got[1][-1], got[1][1])
    *parts, rows = call(
        functools.partial(late_kernel, at0, count, cap, tokens),
        [piece] * top + [table],
        [last, rows, hidden2, *sums],
    )
    moved = [exchange(p, 0) for p in parts[: top // 2]]
    parts = parts[top // 2 :]
    leaves = add(*reduced(parts, moved))
    cuts = [0, *(wide * c // 32 for c in CUTS), wide]

    def leave(n, *others):
        piece = leaves[cuts[n] : cuts[n + 1]]
        return exchange(after(piece, *others) if others else piece, bits - 1)

    for k in range(2, far - 1):
        step(1, k, *([got[1][1 - k], got[1][k - 1]] if k > 2 else []))
    arrived = [leave(0)]
    ready = (got[1][2 - far], got[1][far - 2], leaves)
    step(1, far - 1, *ready)
    acc = call(
        functools.partial(project_kernel, at0, masks[0], count, cap, tokens, size),
        [((slots, inner), f32)],
        [after(last, *ready), rows, placed, weight],
        [all_placed],
    )[0]
    ready = (got[1][1 - far], got[1][far - 1], acc, arrived[0])
    step(1, far, *ready)
    arrived.append(leave(1, *ready))
    held = [got[1][o] for o in offsets_of(count, 1)]
    ready = (held[-1], arrived[1])
    arrived.append(leave(2, *ready))
    grad_hidden, by_token, scaled = call(
        functools.partial(finish_kernel, at1, masks[1], count, cap, tokens, size),
        [((slots, inner), bf16), ((count, tokens), f32), all_placed],
        [after(held[0], *ready), *held[1:], rows, weight, acc, hidden2],
        [all_placed],
        limit=20,
    )
    ready = (arrived[2], by_token)
    arrived.append(leave(3, *ready))
    scaled = after(scaled, *ready)

    parts = pl.pallas_call(
        part_kernel,
        out_shape=[jax.ShapeDtypeStruct(*piece)] * top,
        in_specs=[vmem] * 2,
        out_specs=[vmem] * top,
        compiler_params=pltpu.CompilerParams(vmem_limit_bytes=16 * MIB),
    )(scaled, hidden2)
    moved = [exchange(p, 0) for p in parts[: top // 2]]
    kept, moved = reduced(parts[top // 2 :], moved)
    grad_down = pl.pallas_call(
        final_kernel,
        out_shape=jax.ShapeDtypeStruct((wide, inner), jnp.bfloat16),
        in_specs=[vmem] * (2 + len(arrived)),
        out_specs=vmem,
        compiler_params=pltpu.CompilerParams(vmem_limit_bytes=16 * MIB),
    )(kept, moved, *arrived)[None]

    returned = lax.all_to_all(by_token, "expert", split_axis=0, concat_axis=0, tiled=True)
    hit = expert_ids[:, :, None] == jnp.arange(count, dtype=jnp.int32)[None, None, :]
    grad_probs = jnp.sum(jnp.where(hit, returned.T[:, None, :], 0.0), axis=2)
    return grad_hidden.reshape(hidden.shape), grad_down, grad_probs


def solution(mesh):
    in_specs = (
        P(("dp", "expert"), None),
        P(("dp", "expert"), None),
        P(("dp", "expert"), None),
        P("expert", "dp", None, None),
        P("expert", None, None),
    )
    out_specs = (P("expert", "dp", None, None), P("expert", "dp", None), P(("dp", "expert"), None))
    return jax.shard_map(
        functools.partial(body, mesh.shape["dp"]),
        mesh=mesh,
        in_specs=in_specs,
        out_specs=out_specs,
        check_vma=False,
    )
```

time: 219 us -> 97.5 us (0.45)
  waiting for transfers between devices: 127 us -> 32.5 us
  local copies, waits for them, and re-layouts: 33.6 us -> 5.04 us
  Pallas kernels: 0 us -> 25.3 us
  matrix products: 20.7 us -> 0 us
  between operations: 14.1 us -> 0.75 us
  blocking collectives: 0 us -> 12.1 us
  other arithmetic: 5.76 us -> 1.03 us
  starting transfers between devices: 17.1 us -> 20.5 us
    all_to_all x3 -> x0, waiting for transfers between devices: 98.9 us -> none  [the longest x1 92.5 us: body(): lax.all_to_all(send_grad.reshape(experts_all, 1, capacity, model_width),...]
    ppermute x0 -> x20, waiting for transfers between devices: none -> 32.5 us  [the longest x14 31.1 us: step(): got[chunk][sign * k] = lax.ppermute(value, 'expert', pairs)]
    reduce_scatter x1 -> x0, waiting for transfers between devices: 28.1 us -> none  [body(): lax.psum_scatter(blocks.astype(jnp.bfloat16), 'dp', scatter_dimension=0,...]
    pallas_call x0 -> x7, Pallas kernels: none -> 25.3 us  [the longest x4 19.5 us: call(): pl.pallas_call(kernel, out_shape=[jax.ShapeDtypeStruct(*out) for out in o...]
    dot_general x2 -> x0, matrix products: 20.7 us -> none  [the longest x1 12 us: body(): jnp.dot(grad_rows, w_down[expert], preferred_element_type=jnp.float32)]
    ppermute x0 -> x20, starting transfers between devices: none -> 20.5 us  [the longest x14 16.1 us: step(): got[chunk][sign * k] = lax.ppermute(value, 'expert', pairs)]
    scatter x2 -> x0, local copies, waits for them, and re-layouts: 18 us -> none  [the longest x1 9.35 us: body(): send_grad = jnp.zeros((experts_all * capacity, model_width), out_grad.dty...]
    all_to_all x3 -> x0, starting transfers between devices: 16.9 us -> none  [the longest x1 7.28 us: body(): lax.all_to_all(send_prob.reshape(experts_all, 1, capacity), 'expert', spl...]
  transfers between devices with their start and end apart: 4 -> 20, of which waited for: 3 -> 11; matrix products, arithmetic and copies ran while one was open for 15% -> 2% of each run, Pallas kernels for 0% -> 18%
where the time goes in v2:
time: 97.5 us; the launch traced here: 97.2 us
  waiting for transfers between devices  32.5 us (33%)
  Pallas kernels  25.3 us (26%)
  starting transfers between devices  20.5 us (21%)
  blocking collectives  12.1 us (12%)
  local copies, waits for them, and re-layouts  5.04 us (5%)
  other arithmetic  1.03 us (1%)
    ppermute x14, waiting for transfers between devices, step(): got[chunk][sign * k] = lax.ppermute(value, 'expert', pairs)  31.1 us
    pallas_call x4, Pallas kernels, call(): pl.pallas_call(kernel, out_shape=[jax.ShapeDtypeStruct(*out) for out in o...  19.5 us
    ppermute x14, starting transfers between devices, step(): got[chunk][sign * k] = lax.ppermute(value, 'expert', pairs)  16.1 us
    all_to_all x1, blocking collectives, body(): lax.all_to_all(by_token, 'expert', split_axis=0, concat_axis=0, tiled=True)  12.1 us
    ppermute x6, starting transfers between devices, exchange(): return lax.ppermute(value, 'dp', [(r, r ^ 1 << b) for r in range(replicas)])  4.39 us
    unnamed x16, local copies, waits for them, and re-layouts  4.24 us
    pallas_call x1, Pallas kernels, body(): pl.pallas_call(part_kernel, out_shape=[jax.ShapeDtypeStruct(*piece)] * to...  3.45 us
  transfers between devices with their start and end apart: 20, of which 11 were waited for; matrix products, arithmetic and copies ran while one was open for 2% of the time, Pallas kernels for 18%

profile of v2, /device:TPU:0, one launch (start us, length us, event | category | flops | bytes accessed | tf_op | source)
XLA Modules:
  0.0 97.2 jit_solution(15871007632994647271)
XLA Ops:
  0.6 0.1 pad_add_fusion.mine_ref
  0.7 1.0 %copy-done.2 = bf16[128,2048]{1,0:T(8,128)(2,1)S(1)} copy-done((bf16[128,2048]{1,0:T(8,128)(2,1)S(1)}, bf16[128,2048]{1,0:T(8,128)(2,1)}, u32[]{:S(2)}) %copy-start.2) | copy-done | bytes 524312
  1.8 0.7 copy-done.3
  2.4 0.7 copy-done.5
  3.1 0.7 shard_map.85
  3.8 3.0 %collective-permute-start = (bf16[144,1024]{1,0:T(8,128)(2,1)S(1)}, bf16[144,1024]{1,0:T(8,128)(2,1)S(1)}, u32[]{:S(2)}, u32[]{:S(2)}) collective-permute-start(bf16[144,1024]{1,0:T(8,128)(2,1)S(1)} %get-tuple-element.31.refs_0_), channel_id=1, source_target_pairs={{0,2},{2,4},{4,6},{6,7},{7,5},{5,3},{3,1},{1,0},{8,10},{10,12},{12... | collective-permute-start | bytes 884744 | tf_op jit(solution)/shard_map/ppermute | solution.py:297
  6.9 0.0 collective-permute-start.3
  6.9 0.7 dynamic-slice_bitcast_fusion.where_ref
  7.6 6.3 %collective-permute-done.refs_1_ = bf16[144,1024]{1,0:T(8,128)(2,1)S(1)} collective-permute-done((bf16[144,1024]{1,0:T(8,128)(2,1)S(1)}, bf16[144,1024]{1,0:T(8,128)(2,1)S(1)}, u32[]{:S(2)}, u32[]{:S(2)}) %collective-permute-start) | collective-permute-done | bytes 294944 | tf_op jit(solution)/shard_map/ppermute | solution.py:297
  13.8 1.8 %collective-permute-start.1 = (bf16[144,1024]{1,0:T(8,128)(2,1)S(1)}, bf16[144,1024]{1,0:T(8,128)(2,1)S(1)}, u32[]{:S(2)}, u32[]{:S(2)}) collective-permute-start(bf16[144,1024]{1,0:T(8,128)(2,1)S(1)} %collective-permute-done.refs_1_), channel_id=1, source_target_pairs={{0,2},{2,4},{4,6},{6,7},{7,5},{5,3},{3,1},{1,0},{8,10},{10,12},{12... | collective-permute-start | bytes 884744 | tf_op jit(solution)/shard_map/ppermute | solution.py:297
  15.6 0.0 collective-permute-done.3.refs_4_
  15.6 0.2 collective-permute-start.4
  15.8 6.2 %collective-permute-done.1.refs_2_ = bf16[144,1024]{1,0:T(8,128)(2,1)S(1)} collective-permute-done((bf16[144,1024]{1,0:T(8,128)(2,1)S(1)}, bf16[144,1024]{1,0:T(8,128)(2,1)S(1)}, u32[]{:S(2)}, u32[]{:S(2)}) %collective-permute-start.1) | collective-permute-done | bytes 294944 | tf_op jit(solution)/shard_map/ppermute | solution.py:297
  22.0 1.5 %collective-permute-start.2 = (bf16[144,1024]{1,0:T(8,128)(2,1)S(1)}, bf16[144,1024]{1,0:T(8,128)(2,1)S(1)}, u32[]{:S(2)}, u32[]{:S(2)}) collective-permute-start(bf16[144,1024]{1,0:T(8,128)(2,1)S(1)} %collective-permute-done.1.refs_2_), channel_id=1, source_target_pairs={{0,2},{2,4},{4,6},{6,7},{7,5},{5,3},{3,1},{1,0},{8,10},{10,12},{12... | collective-permute-start | bytes 884744 | tf_op jit(solution)/shard_map/ppermute | solution.py:297
  23.5 0.5 collective-permute-start.5
  24.0 5.2 %collective-permute-done.2.refs_3_ = bf16[144,1024]{1,0:T(8,128)(2,1)S(1)} collective-permute-done((bf16[144,1024]{1,0:T(8,128)(2,1)S(1)}, bf16[144,1024]{1,0:T(8,128)(2,1)S(1)}, u32[]{:S(2)}, u32[]{:S(2)}) %collective-permute-start.2) | collective-permute-done | bytes 294944 | tf_op jit(solution)/shard_map/ppermute | solution.py:297
  29.3 1.4 %collective-permute-start.10 = (bf16[144,1024]{1,0:T(8,128)(2,1)S(1)}, bf16[144,1024]{1,0:T(8,128)(2,1)S(1)}, u32[]{:S(2)}, u32[]{:S(2)}) collective-permute-start(bf16[144,1024]{1,0:T(8,128)(2,1)S(1)} %collective-permute-done.2.refs_3_), channel_id=1, source_target_pairs={{0,2},{2,4},{4,6},{6,7},{7,5},{5,3},{3,1},{1,0},{8,10},{10,12},{12... | collective-permute-start | bytes 884744 | tf_op jit(solution)/shard_map/ppermute | solution.py:297
  30.7 1.6 %collective-permute-start.8 = (bf16[128,1024]{1,0:T(8,128)(2,1)S(1)}, bf16[128,1024]{1,0:T(8,128)(2,1)S(1)}, u32[]{:S(2)}, u32[]{:S(2)}) collective-permute-start(bf16[128,1024]{1,0:T(8,128)(2,1)S(1)} %get-tuple-element.48.refs_0_), channel_id=1, source_target_pairs={{0,2},{2,4},{4,6},{6,7},{7,5},{5,3},{3,1},{1,0},{8,10},{10,12},{12... | collective-permute-start | bytes 786440 | tf_op jit(solution)/shard_map/ppermute | solution.py:297
  32.2 0.4 collective-permute-start.6
  32.7 1.8 %copy-done = bf16[1,8,128,1408]{3,2,1,0:T(8,128)(2,1)S(1)} copy-done((bf16[1,8,128,1408]{3,2,1,0:T(8,128)(2,1)S(1)}, bf16[1,8,128,1408]{3,2,1,0:T(8,128)(2,1)}, u32[]{:S(2)}) %copy-start) | copy-done | bytes 2883608
  34.5 5.2 %shard_map.86 = (f32[8,256]{1,0:T(8,128)S(1)}, bf16[1024,1024]{1,0:T(8,128)(2,1)S(1)}, f32[512,1408]{1,0:T(8,128)S(1)}, f32[512,1408]{1,0:T(8,128)S(1)}) custom-call(s32[18]{0:T(128)S(1)} %dynamic-slice_bitcast_fusion.where_ref, bf16[144,1024]{1,0:T(8,128)(2,1)S(1)} %get-tuple-element.31.refs_0_, bf16[144,1024]{1,0:T(8,128)(2,1)S(1)} %collective-permute-done.refs_1_, ...), custom_call_target="tpu_custom_call" | custom-call | tf_op jit(solution)/shard_map/pallas_call | solution.py:302
  39.7 1.5 %collective-permute-done.8.refs_1_ = bf16[128,1024]{1,0:T(8,128)(2,1)S(1)} collective-permute-done((bf16[128,1024]{1,0:T(8,128)(2,1)S(1)}, bf16[128,1024]{1,0:T(8,128)(2,1)S(1)}, u32[]{:S(2)}, u32[]{:S(2)}) %collective-permute-start.8) | collective-permute-done | bytes 262176 | tf_op jit(solution)/shard_map/ppermute | solution.py:297
  41.3 1.7 %shard_map.87 = (bf16[512,1408]{1,0:T(8,128)(2,1)S(1)}, bf16[512,1408]{1,0:T(8,128)(2,1)S(1)}, f32[8,256]{1,0:T(8,128)S(1)}) custom-call(s32[18]{0:T(128)S(1)} %dynamic-slice_bitcast_fusion.where_ref, bf16[144,1024]{1,0:T(8,128)(2,1)S(1)} %collective-permute-done.10.block_ref, f32[8,256]{1,0:T(8,128)S(1)} %get-tuple-element.36.near_ref, ...), custom_call_target="tpu_custom_call" | custom-call | tf_op jit(solution)/shard_map/pallas_call | solution.py:302
  42.9 0.1 collective-permute-start.11
  43.0 1.2 %collective-permute-start.9 = (bf16[128,1024]{1,0:T(8,128)(2,1)S(1)}, bf16[128,1024]{1,0:T(8,128)(2,1)S(1)}, u32[]{:S(2)}, u32[]{:S(2)}) collective-permute-start(bf16[128,1024]{1,0:T(8,128)(2,1)S(1)} %collective-permute-done.8.refs_1_), channel_id=1, source_target_pairs={{0,2},{2,4},{4,6},{6,7},{7,5},{5,3},{3,1},{1,0},{8,10},{10,12},{12... | collective-permute-start | bytes 786440 | tf_op jit(solution)/shard_map/ppermute | solution.py:297
  44.2 0.9 collective-permute-start.7
  45.1 1.1 %collective-permute-done.11 = bf16[512,1408]{1,0:T(8,128)(2,1)S(1)} collective-permute-done((bf16[512,1408]{1,0:T(8,128)(2,1)S(1)}, bf16[512,1408]{1,0:T(8,128)(2,1)S(1)}, u32[]{:S(2)}, u32[]{:S(2)}) %collective-permute-start.11) | collective-permute-done | bytes 1441824 | tf_op jit(solution)/shard_map/ppermute | solution.py:322
  46.2 0.3 add_convert_fusion
  46.6 1.1 %collective-permute-start.14 = (bf16[192,1408]{1,0:T(8,128)(2,1)S(1)}, bf16[192,1408]{1,0:T(8,128)(2,1)S(1)}, u32[]{:S(2)}, u32[]{:S(2)}) collective-permute-start(bf16[192,1408]{1,0:T(8,128)(2,1)S(1)} %slice.16), channel_id=1, source_target_pairs={{0,16},{8,24},{16,0},{24,8},{1,17},{9,25},{17,1},{25,9},{2,18},{10... | collective-permute-start | bytes 1622024 | tf_op jit(solution)/shard_map/ppermute | solution.py:322
  47.7 4.0 %collective-permute-done.9.refs_2_ = bf16[128,1024]{1,0:T(8,128)(2,1)S(1)} collective-permute-done((bf16[128,1024]{1,0:T(8,128)(2,1)S(1)}, bf16[128,1024]{1,0:T(8,128)(2,1)S(1)}, u32[]{:S(2)}, u32[]{:S(2)}) %collective-permute-start.9) | collective-permute-done | bytes 262176 | tf_op jit(solution)/shard_map/ppermute | solution.py:297
  51.7 0.9 collective-permute-done.7.refs_5_
  52.6 0.9 collective-permute-start.12
  53.5 1.1 %collective-permute-start.13 = (bf16[128,1024]{1,0:T(8,128)(2,1)S(1)}, bf16[128,1024]{1,0:T(8,128)(2,1)S(1)}, u32[]{:S(2)}, u32[]{:S(2)}) collective-permute-start(bf16[128,1024]{1,0:T(8,128)(2,1)S(1)} %collective-permute-done.9.refs_2_), channel_id=1, source_target_pairs={{0,2},{2,4},{4,6},{6,7},{7,5},{5,3},{3,1},{1,0},{8,10},{10,12},{12... | collective-permute-start | bytes 786440 | tf_op jit(solution)/shard_map/ppermute | solution.py:297
  54.6 4.7 %shard_map.88.refs_10_ = f32[1024,1408]{1,0:T(8,128)S(1)} custom-call(s32[18]{0:T(128)S(1)} %dynamic-slice_bitcast_fusion.where_ref, bf16[144,1024]{1,0:T(8,128)(2,1)S(1)} %collective-permute-done.10.block_ref, f32[8,256]{1,0:T(8,128)S(1)} %get-tuple-element.44.refs_0_.refs_8_, bf16[1024,1024]{1,0:T(8,128)(2,1)S(1)} %get-tuple-element.45.refs_1_, ...), custom_call_target="tpu_custom_call" | custom-call | tf_op jit(solution)/shard_map/pallas_call | solution.py:302
  59.4 0.7 collective-permute-done.12.refs_6_
  60.1 0.6 collective-permute-done.13.refs_3_
  60.7 0.3 collective-permute-done.14.refs_0_
  61.0 1.0 %collective-permute-start.16 = (bf16[96,1408]{1,0:T(8,128)(2,1)S(1)}, bf16[96,1408]{1,0:T(8,128)(2,1)S(1)}, u32[]{:S(2)}, u32[]{:S(2)}) collective-permute-start(bf16[96,1408]{1,0:T(8,128)(2,1)S(1)} %get-tuple-element.47), channel_id=1, source_target_pairs={{0,16},{8,24},{16,0},{24,8},{1,17},{9,25},{17,1},{25,9},{2,18},{10... | collective-permute-start | bytes 811016 | tf_op jit(solution)/shard_map/ppermute | solution.py:322
  62.1 1.5 %collective-permute-start.15 = (bf16[128,1024]{1,0:T(8,128)(2,1)S(1)}, bf16[128,1024]{1,0:T(8,128)(2,1)S(1)}, u32[]{:S(2)}, u32[]{:S(2)}) collective-permute-start(bf16[128,1024]{1,0:T(8,128)(2,1)S(1)} %collective-permute-done.12.refs_6_), channel_id=1, source_target_pairs={{2,0},{4,2},{6,4},{7,6},{5,7},{3,5},{1,3},{0,1},{10,8},{12,10},{14... | collective-permute-start | bytes 786440 | tf_op jit(solution)/shard_map/ppermute | solution.py:297
  63.6 5.7 %collective-permute-done.15.refs_7_ = bf16[128,1024]{1,0:T(8,128)(2,1)S(1)} collective-permute-done((bf16[128,1024]{1,0:T(8,128)(2,1)S(1)}, bf16[128,1024]{1,0:T(8,128)(2,1)S(1)}, u32[]{:S(2)}, u32[]{:S(2)}) %collective-permute-start.15) | collective-permute-done | bytes 262176 | tf_op jit(solution)/shard_map/ppermute | solution.py:297
  69.3 1.0 %collective-permute-start.17 = (bf16[128,1408]{1,0:T(8,128)(2,1)S(1)}, bf16[128,1408]{1,0:T(8,128)(2,1)S(1)}, u32[]{:S(2)}, u32[]{:S(2)}) collective-permute-start(bf16[128,1408]{1,0:T(8,128)(2,1)S(1)} %slice.18), channel_id=1, source_target_pairs={{0,16},{8,24},{16,0},{24,8},{1,17},{9,25},{17,1},{25,9},{2,18},{10... | collective-permute-start | bytes 1081352 | tf_op jit(solution)/shard_map/ppermute | solution.py:322
  70.3 7.9 %shard_map.89 = (bf16[1024,1408]{1,0:T(8,128)(2,1)}, f32[8,128]{1,0:T(8,128)S(1)}, bf16[1024,1024]{1,0:T(8,128)(2,1)S(1)}) custom-call(s32[18]{0:T(128)S(1)} %dynamic-slice_bitcast_fusion.where_ref, bf16[128,1024]{1,0:T(8,128)(2,1)S(1)} %get-tuple-element.48.refs_0_, bf16[128,1024]{1,0:T(8,128)(2,1)S(1)} %collective-permute-done.8.refs_1_, ...), custom_call_target="tpu_custom_call" | custom-call | tf_op jit(solution)/shard_map/pallas_call | solution.py:302
  78.2 3.4 %shard_map.90 = (bf16[512,1408]{1,0:T(8,128)(2,1)S(1)}, bf16[512,1408]{1,0:T(8,128)(2,1)S(1)}) custom-call(bf16[1024,1024]{1,0:T(8,128)(2,1)S(1)} %get-tuple-element.53.scaled_ref, bf16[1024,1408]{1,0:T(8,128)(2,1)S(1)} %bitcast.19), custom_call_target="tpu_custom_call" | custom-call | tf_op jit(solution)/shard_map/pallas_call | solution.py:387
  81.7 0.1 collective-permute-start.18
  81.8 1.1 %collective-permute-start.19 = (bf16[96,1408]{1,0:T(8,128)(2,1)S(1)}, bf16[96,1408]{1,0:T(8,128)(2,1)S(1)}, u32[]{:S(2)}, u32[]{:S(2)}) collective-permute-start(bf16[96,1408]{1,0:T(8,128)(2,1)S(1)} %get-tuple-element.56), channel_id=1, source_target_pairs={{0,16},{8,24},{16,0},{24,8},{1,17},{9,25},{17,1},{25,9},{2,18},{10... | collective-permute-start | bytes 811016 | tf_op jit(solution)/shard_map/ppermute | solution.py:322
  82.9 12.1 %all_to_all.12 = f32[8,1,128]{2,1,0:T(1,128)S(1)} all-to-all(f32[8,1,128]{2,1,0:T(1,128)S(1)} %bitcast.25), channel_id=1, replica_groups=mesh['dp'=4,'expert'=8] {'expert'}, dimensions={0} | all-to-all | bytes 8192 | tf_op jit(solution)/shard_map/all_to_all | solution.py:404
  95.0 0.6 select_reduce_fusion
  95.6 1.6 %shard_map.91 = bf16[512,1408]{1,0:T(8,128)(2,1)} custom-call(bf16[512,1408]{1,0:T(8,128)(2,1)S(1)} %get-tuple-element.54.kept_ref, bf16[512,1408]{1,0:T(8,128)(2,1)S(1)} %collective-permute-done.18.moved_ref, bf16[192,1408]{1,0:T(8,128)(2,1)S(1)} %collective-permute-done.14.refs_0_, bf16[96,1408]{1,0:T(8,128)(2,1)S(1)} %collective-permute-done.16.refs_1_, ...), custom_call_target="tpu_custom_call" | custom-call | tf_op jit(solution)/shard_map/pallas_call | solution.py:396
  (24 shorter events, 0.2 us)
Async XLA Ops:
  0.7 1.0 %copy-start.2 = (bf16[128,2048]{1,0:T(8,128)(2,1)S(1)}, bf16[128,2048]{1,0:T(8,128)(2,1)}, u32[]{:S(2)}) copy-start(bf16[128,2048]{1,0:T(8,128)(2,1)} %grad_ref.1) | copy-start | bytes 1572868
  1.8 0.7 copy-start.3
  2.4 0.7 copy-start.5
  3.8 10.0 %collective-permute-start = (bf16[144,1024]{1,0:T(8,128)(2,1)S(1)}, bf16[144,1024]{1,0:T(8,128)(2,1)S(1)}, u32[]{:S(2)}, u32[]{:S(2)}) collective-permute-start(bf16[144,1024]{1,0:T(8,128)(2,1)S(1)} %get-tuple-element.31.refs_0_), channel_id=1, source_target_pairs={{0,2},{2,4},{4,6},{6,7},{7,5},{5,3},{3,1},{1,0},{8,10},{10,12},{12... | collective-permute-start | bytes 884744 | tf_op jit(solution)/shard_map/ppermute | solution.py:297
  6.9 8.8 %collective-permute-start.3 = (bf16[144,1024]{1,0:T(8,128)(2,1)S(1)}, bf16[144,1024]{1,0:T(8,128)(2,1)S(1)}, u32[]{:S(2)}, u32[]{:S(2)}) collective-permute-start(bf16[144,1024]{1,0:T(8,128)(2,1)S(1)} %get-tuple-element.31.refs_0_), channel_id=1, source_target_pairs={{2,0},{4,2},{6,4},{7,6},{5,7},{3,5},{1,3},{0,1},{10,8},{12,10},{14... | collective-permute-start | bytes 884744 | tf_op jit(solution)/shard_map/ppermute | solution.py:297
  13.8 8.2 %collective-permute-start.1 = (bf16[144,1024]{1,0:T(8,128)(2,1)S(1)}, bf16[144,1024]{1,0:T(8,128)(2,1)S(1)}, u32[]{:S(2)}, u32[]{:S(2)}) collective-permute-start(bf16[144,1024]{1,0:T(8,128)(2,1)S(1)} %collective-permute-done.refs_1_), channel_id=1, source_target_pairs={{0,2},{2,4},{4,6},{6,7},{7,5},{5,3},{3,1},{1,0},{8,10},{10,12},{12... | collective-permute-start | bytes 884744 | tf_op jit(solution)/shard_map/ppermute | solution.py:297
  15.6 7.9 %collective-permute-start.4 = (bf16[144,1024]{1,0:T(8,128)(2,1)S(1)}, bf16[144,1024]{1,0:T(8,128)(2,1)S(1)}, u32[]{:S(2)}, u32[]{:S(2)}) collective-permute-start(bf16[144,1024]{1,0:T(8,128)(2,1)S(1)} %collective-permute-done.3.refs_4_), channel_id=1, source_target_pairs={{2,0},{4,2},{6,4},{7,6},{5,7},{3,5},{1,3},{0,1},{10,8},{12,10},{14... | collective-permute-start | bytes 884744 | tf_op jit(solution)/shard_map/ppermute | solution.py:297
  22.0 7.3 %collective-permute-start.2 = (bf16[144,1024]{1,0:T(8,128)(2,1)S(1)}, bf16[144,1024]{1,0:T(8,128)(2,1)S(1)}, u32[]{:S(2)}, u32[]{:S(2)}) collective-permute-start(bf16[144,1024]{1,0:T(8,128)(2,1)S(1)} %collective-permute-done.1.refs_2_), channel_id=1, source_target_pairs={{0,2},{2,4},{4,6},{6,7},{7,5},{5,3},{3,1},{1,0},{8,10},{10,12},{12... | collective-permute-start | bytes 884744 | tf_op jit(solution)/shard_map/ppermute | solution.py:297
  23.5 7.2 %collective-permute-start.5 = (bf16[144,1024]{1,0:T(8,128)(2,1)S(1)}, bf16[144,1024]{1,0:T(8,128)(2,1)S(1)}, u32[]{:S(2)}, u32[]{:S(2)}) collective-permute-start(bf16[144,1024]{1,0:T(8,128)(2,1)S(1)} %collective-permute-done.4.refs_5_), channel_id=1, source_target_pairs={{2,0},{4,2},{6,4},{7,6},{5,7},{3,5},{1,3},{0,1},{10,8},{12,10},{14... | collective-permute-start | bytes 884744 | tf_op jit(solution)/shard_map/ppermute | solution.py:297
  29.3 12.0 %collective-permute-start.10 = (bf16[144,1024]{1,0:T(8,128)(2,1)S(1)}, bf16[144,1024]{1,0:T(8,128)(2,1)S(1)}, u32[]{:S(2)}, u32[]{:S(2)}) collective-permute-start(bf16[144,1024]{1,0:T(8,128)(2,1)S(1)} %collective-permute-done.2.refs_3_), channel_id=1, source_target_pairs={{0,2},{2,4},{4,6},{6,7},{7,5},{5,3},{3,1},{1,0},{8,10},{10,12},{12... | collective-permute-start | bytes 884744 | tf_op jit(solution)/shard_map/ppermute | solution.py:297
  30.7 10.6 %collective-permute-start.8 = (bf16[128,1024]{1,0:T(8,128)(2,1)S(1)}, bf16[128,1024]{1,0:T(8,128)(2,1)S(1)}, u32[]{:S(2)}, u32[]{:S(2)}) collective-permute-start(bf16[128,1024]{1,0:T(8,128)(2,1)S(1)} %get-tuple-element.48.refs_0_), channel_id=1, source_target_pairs={{0,2},{2,4},{4,6},{6,7},{7,5},{5,3},{3,1},{1,0},{8,10},{10,12},{12... | collective-permute-start | bytes 786440 | tf_op jit(solution)/shard_map/ppermute | solution.py:297
  32.2 9.0 %collective-permute-start.6 = (bf16[128,1024]{1,0:T(8,128)(2,1)S(1)}, bf16[128,1024]{1,0:T(8,128)(2,1)S(1)}, u32[]{:S(2)}, u32[]{:S(2)}) collective-permute-start(bf16[128,1024]{1,0:T(8,128)(2,1)S(1)} %get-tuple-element.48.refs_0_), channel_id=1, source_target_pairs={{2,0},{4,2},{6,4},{7,6},{5,7},{3,5},{1,3},{0,1},{10,8},{12,10},{14... | collective-permute-start | bytes 786440 | tf_op jit(solution)/shard_map/ppermute | solution.py:297
  32.7 1.8 %copy-start = (bf16[1,8,128,1408]{3,2,1,0:T(8,128)(2,1)S(1)}, bf16[1,8,128,1408]{3,2,1,0:T(8,128)(2,1)}, u32[]{:S(2)}) copy-start(bf16[1,8,128,1408]{3,2,1,0:T(8,128)(2,1)} %param.9) | copy-start | bytes 8650756
  34.5 6.8 %copy-start.1 = (bf16[1,8,128,1408]{3,2,1,0:T(8,128)(2,1)S(1)}, bf16[1,8,128,1408]{3,2,1,0:T(8,128)(2,1)}, u32[]{:S(2)}) copy-start(bf16[1,8,128,1408]{3,2,1,0:T(8,128)(2,1)} %param.9) | copy-start | bytes 8650756
  41.3 13.4 %slice-start = ((s8[5767168]{0:T(1024)(128)(4,1)}), s8[4194304]{0:T(1024)(128)(4,1)S(1)}, s32[]{:S(2)}) async-start(s8[5767168]{0:T(1024)(128)(4,1)} %bitcast.20), calls=%async_computation.1 | async-start | bytes 8388608
  41.3 13.3 %slice-start.1 = ((s8[5767168]{0:T(1024)(128)(4,1)}), s8[1572864]{0:T(1024)(128)(4,1)S(1)}, s32[]{:S(2)}) async-start(s8[5767168]{0:T(1024)(128)(4,1)} %bitcast.20), calls=%async_computation.2 | async-start | bytes 3145728
  42.9 3.3 %collective-permute-start.11 = (bf16[512,1408]{1,0:T(8,128)(2,1)S(1)}, bf16[512,1408]{1,0:T(8,128)(2,1)S(1)}, u32[]{:S(2)}, u32[]{:S(2)}) collective-permute-start(bf16[512,1408]{1,0:T(8,128)(2,1)S(1)} %get-tuple-element.40), channel_id=1, source_target_pairs={{0,8},{8,0},{16,24},{24,16},{1,9},{9,1},{17,25},{25,17},{2,10},{10... | collective-permute-start | bytes 4325384 | tf_op jit(solution)/shard_map/ppermute | solution.py:322
  43.0 8.7 %collective-permute-start.9 = (bf16[128,1024]{1,0:T(8,128)(2,1)S(1)}, bf16[128,1024]{1,0:T(8,128)(2,1)S(1)}, u32[]{:S(2)}, u32[]{:S(2)}) collective-permute-start(bf16[128,1024]{1,0:T(8,128)(2,1)S(1)} %collective-permute-done.8.refs_1_), channel_id=1, source_target_pairs={{0,2},{2,4},{4,6},{6,7},{7,5},{5,3},{3,1},{1,0},{8,10},{10,12},{12... | collective-permute-start | bytes 786440 | tf_op jit(solution)/shard_map/ppermute | solution.py:297
  44.2 8.4 %collective-permute-start.7 = (bf16[128,1024]{1,0:T(8,128)(2,1)S(1)}, bf16[128,1024]{1,0:T(8,128)(2,1)S(1)}, u32[]{:S(2)}, u32[]{:S(2)}) collective-permute-start(bf16[128,1024]{1,0:T(8,128)(2,1)S(1)} %collective-permute-done.6.refs_4_), channel_id=1, source_target_pairs={{2,0},{4,2},{6,4},{7,6},{5,7},{3,5},{1,3},{0,1},{10,8},{12,10},{14... | collective-permute-start | bytes 786440 | tf_op jit(solution)/shard_map/ppermute | solution.py:297
  46.6 14.4 %collective-permute-start.14 = (bf16[192,1408]{1,0:T(8,128)(2,1)S(1)}, bf16[192,1408]{1,0:T(8,128)(2,1)S(1)}, u32[]{:S(2)}, u32[]{:S(2)}) collective-permute-start(bf16[192,1408]{1,0:T(8,128)(2,1)S(1)} %slice.16), channel_id=1, source_target_pairs={{0,16},{8,24},{16,0},{24,8},{1,17},{9,25},{17,1},{25,9},{2,18},{10... | collective-permute-start | bytes 1622024 | tf_op jit(solution)/shard_map/ppermute | solution.py:322
  52.6 7.5 %collective-permute-start.12 = (bf16[128,1024]{1,0:T(8,128)(2,1)S(1)}, bf16[128,1024]{1,0:T(8,128)(2,1)S(1)}, u32[]{:S(2)}, u32[]{:S(2)}) collective-permute-start(bf16[128,1024]{1,0:T(8,128)(2,1)S(1)} %collective-permute-done.7.refs_5_), channel_id=1, source_target_pairs={{2,0},{4,2},{6,4},{7,6},{5,7},{3,5},{1,3},{0,1},{10,8},{12,10},{14... | collective-permute-start | bytes 786440 | tf_op jit(solution)/shard_map/ppermute | solution.py:297
  53.5 7.3 %collective-permute-start.13 = (bf16[128,1024]{1,0:T(8,128)(2,1)S(1)}, bf16[128,1024]{1,0:T(8,128)(2,1)S(1)}, u32[]{:S(2)}, u32[]{:S(2)}) collective-permute-start(bf16[128,1024]{1,0:T(8,128)(2,1)S(1)} %collective-permute-done.9.refs_2_), channel_id=1, source_target_pairs={{0,2},{2,4},{4,6},{6,7},{7,5},{5,3},{3,1},{1,0},{8,10},{10,12},{12... | collective-permute-start | bytes 786440 | tf_op jit(solution)/shard_map/ppermute | solution.py:297
  61.0 8.3 %collective-permute-start.16 = (bf16[96,1408]{1,0:T(8,128)(2,1)S(1)}, bf16[96,1408]{1,0:T(8,128)(2,1)S(1)}, u32[]{:S(2)}, u32[]{:S(2)}) collective-permute-start(bf16[96,1408]{1,0:T(8,128)(2,1)S(1)} %get-tuple-element.47), channel_id=1, source_target_pairs={{0,16},{8,24},{16,0},{24,8},{1,17},{9,25},{17,1},{25,9},{2,18},{10... | collective-permute-start | bytes 811016 | tf_op jit(solution)/shard_map/ppermute | solution.py:322
  62.1 7.2 %collective-permute-start.15 = (bf16[128,1024]{1,0:T(8,128)(2,1)S(1)}, bf16[128,1024]{1,0:T(8,128)(2,1)S(1)}, u32[]{:S(2)}, u32[]{:S(2)}) collective-permute-start(bf16[128,1024]{1,0:T(8,128)(2,1)S(1)} %collective-permute-done.12.refs_6_), channel_id=1, source_target_pairs={{2,0},{4,2},{6,4},{7,6},{5,7},{3,5},{1,3},{0,1},{10,8},{12,10},{14... | collective-permute-start | bytes 786440 | tf_op jit(solution)/shard_map/ppermute | solution.py:297
  69.3 8.9 %collective-permute-start.17 = (bf16[128,1408]{1,0:T(8,128)(2,1)S(1)}, bf16[128,1408]{1,0:T(8,128)(2,1)S(1)}, u32[]{:S(2)}, u32[]{:S(2)}) collective-permute-start(bf16[128,1408]{1,0:T(8,128)(2,1)S(1)} %slice.18), channel_id=1, source_target_pairs={{0,16},{8,24},{16,0},{24,8},{1,17},{9,25},{17,1},{25,9},{2,18},{10... | collective-permute-start | bytes 1081352 | tf_op jit(solution)/shard_map/ppermute | solution.py:322
  78.2 16.7 %copy-start.4 = (s32[128,6]{0,1:T(8,128)S(1)}, s32[128,6]{0,1:T(8,128)}, u32[]{:S(2)}) copy-start(s32[128,6]{0,1:T(8,128)} %param.8) | copy-start | bytes 9220
  81.7 13.9 %collective-permute-start.18 = (bf16[512,1408]{1,0:T(8,128)(2,1)S(1)}, bf16[512,1408]{1,0:T(8,128)(2,1)S(1)}, u32[]{:S(2)}, u32[]{:S(2)}) collective-permute-start(bf16[512,1408]{1,0:T(8,128)(2,1)S(1)} %get-tuple-element.55), channel_id=1, source_target_pairs={{0,8},{8,0},{16,24},{24,16},{1,9},{9,1},{17,25},{25,17},{2,10},{10... | collective-permute-start | bytes 4325384 | tf_op jit(solution)/shard_map/ppermute | solution.py:322
  81.8 13.8 %collective-permute-start.19 = (bf16[96,1408]{1,0:T(8,128)(2,1)S(1)}, bf16[96,1408]{1,0:T(8,128)(2,1)S(1)}, u32[]{:S(2)}, u32[]{:S(2)}) collective-permute-start(bf16[96,1408]{1,0:T(8,128)(2,1)S(1)} %get-tuple-element.56), channel_id=1, source_target_pairs={{0,16},{8,24},{16,0},{24,8},{1,17},{9,25},{17,1},{25,9},{2,18},{10... | collective-permute-start | bytes 811016 | tf_op jit(solution)/shard_map/ppermute | solution.py:322

commit v3 on v2

--- a/solution.py
+++ b/solution.py
@@ -10,7 +10,8 @@
 
 MIB = 1024 * 1024
 CHUNKS = 2
-CUTS = (12, 18, 26)
+CUTS = (11, 19)
+LAG = 2
 
 
 def cycle_of(count):
@@ -43,9 +44,9 @@
     )
 
 
-def head_kernel(experts, masks, mine_ref, ids_ref, combine_ref, grad_ref, *own_refs):
+def head_kernel(experts, masks, ids_ref, combine_ref, grad_ref, *own_refs):
     picks, rows = ids_ref.shape
-    dp = mine_ref[1]
+    dp = lax.axis_index("dp")
     columns = own_refs[0].shape[1]
     for c, own in enumerate(own_refs):
         wide = columns // len(masks[c])
@@ -120,11 +121,12 @@
 def spread(row, cap, tokens, grads, here, placed_ref, scaled_ref):
     at = lax.broadcasted_iota(jnp.int32, (cap, tokens), 0).astype(jnp.float32)
     hit = row[:, tokens:] == at
-    for weight, out_ref in ((1.0, placed_ref), (row[:, :tokens], scaled_ref)):
-        pick = jnp.where(hit, weight, 0.0).astype(jnp.bfloat16)
-        out_ref[here, :] = jnp.dot(pick, grads, preferred_element_type=jnp.float32).astype(
-            jnp.bfloat16
-        )
+    picks = jnp.concatenate(
+        [jnp.where(hit, weight, 0.0).astype(jnp.bfloat16) for weight in (1.0, row[:, :tokens])]
+    )
+    both = jnp.dot(picks, grads, preferred_element_type=jnp.float32).astype(jnp.bfloat16)
+    placed_ref[here, :] = both[:cap]
+    scaled_ref[here, :] = both[cap:]
 
 
 def late_kernel(at_order, count, cap, tokens, where_ref, block_ref, near_ref, hidden_ref, *refs):
@@ -145,10 +147,11 @@
         ).astype(jnp.bfloat16)
 
 
-def part_kernel(scaled_ref, hidden_ref, *part_refs):
+def part_kernel(low, scaled_ref, hidden_ref, *refs):
+    part_refs = refs if low == 0 else refs[1:]
     wide = part_refs[0].shape[0]
     for j, part_ref in enumerate(part_refs):
-        here = slice(j * wide, (j + 1) * wide)
+        here = slice(low + j * wide, low + (j + 1) * wide)
         part_ref[...] = product(scaled_ref[:, here], hidden_ref[...]).astype(jnp.bfloat16)
 
 
@@ -232,8 +235,7 @@
             part = slice(g * cap, (g + 1) * cap)
             there = pl.ds(pl.multiple_of(first + g * cap, cap), cap)
             row = rows_ref[pl.ds(source, 1), :]
-            line = source
-            finish(acc[part], row, cap, tokens, saved[part], grad_ref, there, token_ref, line)
+            finish(acc[part], row, cap, tokens, saved[part], grad_ref, there, token_ref, source)
         return carry
 
     lax.fori_loop(0, placed_ref.shape[0] // size, some, 0)
@@ -249,7 +251,6 @@
     slots = count * cap
     mine = lax.axis_index("expert")
     dp = lax.axis_index("dp")
-    where = jnp.stack([mine, dp]).astype(jnp.int32)
     hidden2 = hidden.reshape(slots, inner)
     weight = w_down.reshape(width, inner)
     columns = width // CHUNKS
@@ -274,13 +275,12 @@
             for c in range(CHUNKS)
         ],
         grid=(1,),
-        in_specs=[smem]
-        + [
+        in_specs=[
             pl.BlockSpec(v.shape, lambda i: (0, 0)) for v in (expert_ids.T, combine.T, out_grad)
         ],
         out_specs=[vmem] * CHUNKS,
-        compiler_params=pltpu.CompilerParams(vmem_limit_bytes=8 * MIB),
-    )(where, expert_ids.T, combine.T, out_grad)
+        compiler_params=pltpu.CompilerParams(vmem_limit_bytes=56 * MIB),
+    )(expert_ids.T, combine.T, out_grad)
 
     walk = cycle_of(count)
     forth = [(walk[i], walk[(i + 1) % count]) for i in range(count)]
@@ -331,9 +331,15 @@
 
     far = count // 2
     at0, at1 = 2, 2 + count
+    ready = ()
     for k in range(1, far + 1):
-        step(0, k, *([places] if k == 2 else []))
-    step(1, 1, got[0][1 - far], got[0][far - 1])
+        ready = (places,) if k == 2 else ready
+        step(0, k, *ready)
+        if k > LAG:
+            step(1, k - LAG, *ready)
+            ready = [got[1][o] for o in (LAG - k, k - LAG)]
+        if k >= LAG and k < far:
+            ready = [*(ready if k > LAG else ()), got[0][-k], got[0][k]]
     held = [got[0][o] for o in offsets_of(count, 0)]
     rows, placed, *sums = call(
         functools.partial(early_kernel, at0, count, cap, tokens),
@@ -341,7 +347,10 @@
         [*held[:-1], hidden2],
         [all_placed],
     )
-    last = after(held[-1], got[1][-1], got[1][1])
+    ready = (held[-1], got[1][LAG - far], got[1][far - LAG])
+    for k in range(far - LAG + 1, far):
+        step(1, k, *(ready if k == far - LAG + 1 else ()))
+    last = after(*ready)
     *parts, rows = call(
         functools.partial(late_kernel, at0, count, cap, tokens),
         [piece] * top + [table],
@@ -356,23 +365,18 @@
         piece = leaves[cuts[n] : cuts[n + 1]]
         return exchange(after(piece, *others) if others else piece, bits - 1)
 
-    for k in range(2, far - 1):
-        step(1, k, *([got[1][1 - k], got[1][k - 1]] if k > 2 else []))
     arrived = [leave(0)]
-    ready = (got[1][2 - far], got[1][far - 2], leaves)
-    step(1, far - 1, *ready)
+    ready = (got[1][1 - far], got[1][far - 1], leaves)
+    step(1, far, *ready)
     acc = call(
         functools.partial(project_kernel, at0, masks[0], count, cap, tokens, size),
         [((slots, inner), f32)],
         [after(last, *ready), rows, placed, weight],
         [all_placed],
     )[0]
-    ready = (got[1][1 - far], got[1][far - 1], acc, arrived[0])
-    step(1, far, *ready)
+    held = [got[1][o] for o in offsets_of(count, 1)]
+    ready = (held[-1], arrived[0], acc)
     arrived.append(leave(1, *ready))
-    held = [got[1][o] for o in offsets_of(count, 1)]
-    ready = (held[-1], arrived[1])
-    arrived.append(leave(2, *ready))
     grad_hidden, by_token, scaled = call(
         functools.partial(finish_kernel, at1, masks[1], count, cap, tokens, size),
         [((slots, inner), bf16), ((count, tokens), f32), all_placed],
@@ -380,19 +384,22 @@
         [all_placed],
         limit=20,
     )
-    ready = (arrived[2], by_token)
-    arrived.append(leave(3, *ready))
+    ready = (arrived[1], by_token)
+    arrived.append(leave(2, *ready))
+    returned = lax.all_to_all(by_token, "expert", split_axis=0, concat_axis=0, tiled=True)
     scaled = after(scaled, *ready)
 
-    parts = pl.pallas_call(
-        part_kernel,
-        out_shape=[jax.ShapeDtypeStruct(*piece)] * top,
-        in_specs=[vmem] * 2,
-        out_specs=[vmem] * top,
-        compiler_params=pltpu.CompilerParams(vmem_limit_bytes=16 * MIB),
-    )(scaled, hidden2)
-    moved = [exchange(p, 0) for p in parts[: top // 2]]
-    kept, moved = reduced(parts[top // 2 :], moved)
+    def part_of(low, *others):
+        return pl.pallas_call(
+            functools.partial(part_kernel, low),
+            out_shape=[jax.ShapeDtypeStruct(*piece)] * (top // 2),
+            in_specs=[vmem] * (2 + len(others)),
+            out_specs=[vmem] * (top // 2),
+            compiler_params=pltpu.CompilerParams(vmem_limit_bytes=16 * MIB),
+        )(scaled, hidden2, *others)
+
+    moved = [exchange(p, 0) for p in part_of(0)]
+    kept, moved = reduced(part_of(columns // 2, returned), moved)
     grad_down = pl.pallas_call(
         final_kernel,
         out_shape=jax.ShapeDtypeStruct((wide, inner), jnp.bfloat16),
@@ -401,7 +408,6 @@
         compiler_params=pltpu.CompilerParams(vmem_limit_bytes=16 * MIB),
     )(kept, moved, *arrived)[None]
 
-    returned = lax.all_to_all(by_token, "expert", split_axis=0, concat_axis=0, tiled=True)
     hit = expert_ids[:, :, None] == jnp.arange(count, dtype=jnp.int32)[None, None, :]
     grad_probs = jnp.sum(jnp.where(hit, returned.T[:, None, :], 0.0), axis=2)
     return grad_hidden.reshape(hidden.shape), grad_down, grad_probs

time: 97.5 us -> 94.7 us (0.971)
  waiting for transfers between devices: 32.5 us -> 30.6 us
  local copies, waits for them, and re-layouts: 5.04 us -> 3.6 us
  Pallas kernels: 25.3 us -> 26.7 us
    ppermute x14, waiting for transfers between devices: 31.1 us -> 28.9 us  [step(): got[chunk][sign * k] = lax.ppermute(value, 'expert', pairs)]
    unnamed x16 -> x14, local copies, waits for them, and re-layouts: 4.24 us -> 2.8 us
    pallas_call x1, Pallas kernels: 0.7 us -> 1.93 us  [body(): pl.pallas_call(functools.partial(head_kernel, count, masks), out_shape=[j...]
    pallas_call x1 -> x2, Pallas kernels: 3.45 us -> 3.64 us  [part_of(): pl.pallas_call(functools.partial(part_kernel, low), out_shape=[jax.ShapeD...]
    ppermute x6 -> x5, starting transfers between devices: 4.39 us -> 4.27 us  [exchange(): return lax.ppermute(value, 'dp', [(r, r ^ 1 << b) for r in range(replicas)])]
  transfers between devices with their start and end apart: 20 -> 19, of which waited for: 11 -> 11; matrix products, arithmetic and copies ran while one was open for 2% -> 2% of each run, Pallas kernels for 18% -> 21%
where the time goes in v3:
time: 94.7 us; the launch traced here: 94.4 us
  waiting for transfers between devices  30.6 us (32%)
  Pallas kernels  26.7 us (28%)
  starting transfers between devices  20.3 us (21%)
  blocking collectives  11.5 us (12%)
  local copies, waits for them, and re-layouts  3.6 us (4%)
  other arithmetic  0.96 us (1%)
    ppermute x14, waiting for transfers between devices, step(): got[chunk][sign * k] = lax.ppermute(value, 'expert', pairs)  28.9 us
    pallas_call x4, Pallas kernels, call(): pl.pallas_call(kernel, out_shape=[jax.ShapeDtypeStruct(*out) for out in o...  19.5 us
    ppermute x14, starting transfers between devices, step(): got[chunk][sign * k] = lax.ppermute(value, 'expert', pairs)  16 us
    all_to_all x1, blocking collectives, body(): lax.all_to_all(by_token, 'expert', split_axis=0, concat_axis=0, tiled=True)  11.5 us
    ppermute x5, starting transfers between devices, exchange(): return lax.ppermute(value, 'dp', [(r, r ^ 1 << b) for r in range(replicas)])  4.27 us
    pallas_call x2, Pallas kernels, part_of(): pl.pallas_call(functools.partial(part_kernel, low), out_shape=[jax.ShapeD...  3.64 us
    unnamed x14, local copies, waits for them, and re-layouts  2.8 us
    pallas_call x1, Pallas kernels, body(): pl.pallas_call(functools.partial(head_kernel, count, masks), out_shape=[j...  1.93 us
  transfers between devices with their start and end apart: 19, of which 11 were waited for; matrix products, arithmetic and copies ran while one was open for 2% of the time, Pallas kernels for 21%

profile of v3, /device:TPU:0, one launch (start us, length us, event | category | flops | bytes accessed | tf_op | source)
XLA Modules:
  0.0 94.4 jit_solution(7321995454208161572)
XLA Ops:
  0.6 1.9 %shard_map.85 = (bf16[144,1024]{1,0:T(8,128)(2,1)}, bf16[128,1024]{1,0:T(8,128)(2,1)}) custom-call(s32[6,128]{1,0:T(8,128)} %bitcast.27, bf16[6,128]{1,0:T(8,128)(2,1)} %bitcast.28, bf16[128,2048]{1,0:T(8,128)(2,1)} %grad_ref.1), custom_call_target="tpu_custom_call" | custom-call | tf_op jit(solution)/shard_map/pallas_call | solution.py:271
  2.6 3.0 %collective-permute-start.2 = (bf16[144,1024]{1,0:T(8,128)(2,1)}, bf16[144,1024]{1,0:T(8,128)(2,1)S(1)}, u32[]{:S(2)}, u32[]{:S(2)}) collective-permute-start(bf16[144,1024]{1,0:T(8,128)(2,1)} %get-tuple-element.33.refs_0_), channel_id=1, source_target_pairs={{2,0},{4,2},{6,4},{7,6},{5,7},{3,5},{1,3},{0,1},{10,8},{12,10},{14... | collective-permute-start | bytes 884744 | tf_op jit(solution)/shard_map/ppermute | solution.py:297
  5.5 0.1 collective-permute-start
  5.6 0.7 dynamic-slice_bitcast_fusion.where_ref
  6.3 6.5 %collective-permute-done.2.refs_4_ = bf16[144,1024]{1,0:T(8,128)(2,1)S(1)} collective-permute-done((bf16[144,1024]{1,0:T(8,128)(2,1)}, bf16[144,1024]{1,0:T(8,128)(2,1)S(1)}, u32[]{:S(2)}, u32[]{:S(2)}) %collective-permute-start.2) | collective-permute-done | bytes 294944 | tf_op jit(solution)/shard_map/ppermute | solution.py:297
  12.8 1.7 %collective-permute-start.3 = (bf16[144,1024]{1,0:T(8,128)(2,1)S(1)}, bf16[144,1024]{1,0:T(8,128)(2,1)S(1)}, u32[]{:S(2)}, u32[]{:S(2)}) collective-permute-start(bf16[144,1024]{1,0:T(8,128)(2,1)S(1)} %collective-permute-done.2.refs_4_), channel_id=1, source_target_pairs={{2,0},{4,2},{6,4},{7,6},{5,7},{3,5},{1,3},{0,1},{10,8},{12,10},{14... | collective-permute-start | bytes 884744 | tf_op jit(solution)/shard_map/ppermute | solution.py:297
  14.5 0.0 collective-permute-done.refs_1_
  14.5 0.3 collective-permute-start.1
  14.8 6.2 %collective-permute-done.3.refs_5_ = bf16[144,1024]{1,0:T(8,128)(2,1)S(1)} collective-permute-done((bf16[144,1024]{1,0:T(8,128)(2,1)S(1)}, bf16[144,1024]{1,0:T(8,128)(2,1)S(1)}, u32[]{:S(2)}, u32[]{:S(2)}) %collective-permute-start.3) | collective-permute-done | bytes 294944 | tf_op jit(solution)/shard_map/ppermute | solution.py:297
  21.0 1.1 %collective-permute-done.1.refs_2_ = bf16[144,1024]{1,0:T(8,128)(2,1)S(1)} collective-permute-done((bf16[144,1024]{1,0:T(8,128)(2,1)S(1)}, bf16[144,1024]{1,0:T(8,128)(2,1)S(1)}, u32[]{:S(2)}, u32[]{:S(2)}) %collective-permute-start.1) | collective-permute-done | bytes 294944 | tf_op jit(solution)/shard_map/ppermute | solution.py:297
  22.1 0.7 collective-permute-start.6
  22.8 1.4 %collective-permute-start.7 = (bf16[144,1024]{1,0:T(8,128)(2,1)S(1)}, bf16[144,1024]{1,0:T(8,128)(2,1)S(1)}, u32[]{:S(2)}, u32[]{:S(2)}) collective-permute-start(bf16[144,1024]{1,0:T(8,128)(2,1)S(1)} %collective-permute-done.3.refs_5_), channel_id=1, source_target_pairs={{2,0},{4,2},{6,4},{7,6},{5,7},{3,5},{1,3},{0,1},{10,8},{12,10},{14... | collective-permute-start | bytes 884744 | tf_op jit(solution)/shard_map/ppermute | solution.py:297
  24.1 0.7 collective-permute-start.5
  24.8 1.4 %collective-permute-start.4 = (bf16[128,1024]{1,0:T(8,128)(2,1)}, bf16[128,1024]{1,0:T(8,128)(2,1)S(1)}, u32[]{:S(2)}, u32[]{:S(2)}) collective-permute-start(bf16[128,1024]{1,0:T(8,128)(2,1)} %get-tuple-element.54.refs_0_), channel_id=1, source_target_pairs={{2,0},{4,2},{6,4},{7,6},{5,7},{3,5},{1,3},{0,1},{10,8},{12,10},{14... | collective-permute-start | bytes 786440 | tf_op jit(solution)/shard_map/ppermute | solution.py:297
  26.1 8.2 %collective-permute-done.5.refs_1_ = bf16[128,1024]{1,0:T(8,128)(2,1)S(1)} collective-permute-done((bf16[128,1024]{1,0:T(8,128)(2,1)}, bf16[128,1024]{1,0:T(8,128)(2,1)S(1)}, u32[]{:S(2)}, u32[]{:S(2)}) %collective-permute-start.5) | collective-permute-done | bytes 262176 | tf_op jit(solution)/shard_map/ppermute | solution.py:297
  34.4 0.7 collective-permute-done.4.refs_4_
  35.1 0.0 collective-permute-done.6.refs_3_
  35.1 0.0 collective-permute-done.7.refs_6_
  35.1 1.2 %collective-permute-start.9 = (bf16[144,1024]{1,0:T(8,128)(2,1)S(1)}, bf16[144,1024]{1,0:T(8,128)(2,1)S(1)}, u32[]{:S(2)}, u32[]{:S(2)}) collective-permute-start(bf16[144,1024]{1,0:T(8,128)(2,1)S(1)} %collective-permute-done.6.refs_3_), channel_id=1, source_target_pairs={{0,2},{2,4},{4,6},{6,7},{7,5},{5,3},{3,1},{1,0},{8,10},{10,12},{12... | collective-permute-start | bytes 884744 | tf_op jit(solution)/shard_map/ppermute | solution.py:297
  36.3 0.8 collective-permute-start.8
  37.1 1.2 %collective-permute-start.10 = (bf16[128,1024]{1,0:T(8,128)(2,1)S(1)}, bf16[128,1024]{1,0:T(8,128)(2,1)S(1)}, u32[]{:S(2)}, u32[]{:S(2)}) collective-permute-start(bf16[128,1024]{1,0:T(8,128)(2,1)S(1)} %collective-permute-done.5.refs_1_), channel_id=1, source_target_pairs={{0,2},{2,4},{4,6},{6,7},{7,5},{5,3},{3,1},{1,0},{8,10},{10,12},{12... | collective-permute-start | bytes 786440 | tf_op jit(solution)/shard_map/ppermute | solution.py:297
  38.3 1.8 %copy-done = bf16[1,8,128,1408]{3,2,1,0:T(8,128)(2,1)S(1)} copy-done((bf16[1,8,128,1408]{3,2,1,0:T(8,128)(2,1)S(1)}, bf16[1,8,128,1408]{3,2,1,0:T(8,128)(2,1)}, u32[]{:S(2)}) %copy-start) | copy-done | bytes 2883608
  40.2 1.0 %copy-done.2 = bf16[144,1024]{1,0:T(8,128)(2,1)S(1)} copy-done((bf16[144,1024]{1,0:T(8,128)(2,1)S(1)}, bf16[144,1024]{1,0:T(8,128)(2,1)}, u32[]{:S(2)}) %copy-start.2) | copy-done | bytes 294936
  41.1 5.2 %shard_map.86 = (f32[8,256]{1,0:T(8,128)S(1)}, bf16[1024,1024]{1,0:T(8,128)(2,1)S(1)}, f32[512,1408]{1,0:T(8,128)S(1)}, f32[512,1408]{1,0:T(8,128)S(1)}) custom-call(s32[18]{0:T(128)S(1)} %dynamic-slice_bitcast_fusion.where_ref, bf16[144,1024]{1,0:T(8,128)(2,1)S(1)} %copy-done.2, bf16[144,1024]{1,0:T(8,128)(2,1)S(1)} %collective-permute-done.refs_1_, ...), custom_call_target="tpu_custom_call" | custom-call | tf_op jit(solution)/shard_map/pallas_call | solution.py:302
  46.3 0.2 collective-permute-done.10.refs_2_
  46.5 1.7 %shard_map.87 = (bf16[512,1408]{1,0:T(8,128)(2,1)S(1)}, bf16[512,1408]{1,0:T(8,128)(2,1)S(1)}, f32[8,256]{1,0:T(8,128)S(1)}) custom-call(s32[18]{0:T(128)S(1)} %dynamic-slice_bitcast_fusion.where_ref, bf16[144,1024]{1,0:T(8,128)(2,1)S(1)} %collective-permute-done.9.block_ref, f32[8,256]{1,0:T(8,128)S(1)} %get-tuple-element.45.near_ref, ...), custom_call_target="tpu_custom_call" | custom-call | tf_op jit(solution)/shard_map/pallas_call | solution.py:302
  48.2 0.1 collective-permute-start.13
  48.3 1.4 %collective-permute-start.11 = (bf16[128,1024]{1,0:T(8,128)(2,1)S(1)}, bf16[128,1024]{1,0:T(8,128)(2,1)S(1)}, u32[]{:S(2)}, u32[]{:S(2)}) collective-permute-start(bf16[128,1024]{1,0:T(8,128)(2,1)S(1)} %collective-permute-done.8.refs_5_), channel_id=1, source_target_pairs={{2,0},{4,2},{6,4},{7,6},{5,7},{3,5},{1,3},{0,1},{10,8},{12,10},{14... | collective-permute-start | bytes 786440 | tf_op jit(solution)/shard_map/ppermute | solution.py:297
  49.7 0.6 collective-permute-start.12
  50.4 1.1 %collective-permute-done.13 = bf16[512,1408]{1,0:T(8,128)(2,1)S(1)} collective-permute-done((bf16[512,1408]{1,0:T(8,128)(2,1)S(1)}, bf16[512,1408]{1,0:T(8,128)(2,1)S(1)}, u32[]{:S(2)}, u32[]{:S(2)}) %collective-permute-start.13) | collective-permute-done | bytes 1441824 | tf_op jit(solution)/shard_map/ppermute | solution.py:322
  51.5 0.3 add_convert_fusion
  51.9 1.4 %collective-permute-start.15 = (bf16[176,1408]{1,0:T(8,128)(2,1)S(1)}, bf16[176,1408]{1,0:T(8,128)(2,1)S(1)}, u32[]{:S(2)}, u32[]{:S(2)}) collective-permute-start(bf16[176,1408]{1,0:T(8,128)(2,1)S(1)} %slice.12), channel_id=1, source_target_pairs={{0,16},{8,24},{16,0},{24,8},{1,17},{9,25},{17,1},{25,9},{2,18},{10... | collective-permute-start | bytes 1486856 | tf_op jit(solution)/shard_map/ppermute | solution.py:322
  53.3 3.7 %collective-permute-done.11.refs_6_ = bf16[128,1024]{1,0:T(8,128)(2,1)S(1)} collective-permute-done((bf16[128,1024]{1,0:T(8,128)(2,1)S(1)}, bf16[128,1024]{1,0:T(8,128)(2,1)S(1)}, u32[]{:S(2)}, u32[]{:S(2)}) %collective-permute-start.11) | collective-permute-done | bytes 262176 | tf_op jit(solution)/shard_map/ppermute | solution.py:297
  57.0 1.1 %collective-permute-done.12.refs_3_ = bf16[128,1024]{1,0:T(8,128)(2,1)S(1)} collective-permute-done((bf16[128,1024]{1,0:T(8,128)(2,1)S(1)}, bf16[128,1024]{1,0:T(8,128)(2,1)S(1)}, u32[]{:S(2)}, u32[]{:S(2)}) %collective-permute-start.12) | collective-permute-done | bytes 262176 | tf_op jit(solution)/shard_map/ppermute | solution.py:297
  58.1 1.6 %collective-permute-start.14 = (bf16[128,1024]{1,0:T(8,128)(2,1)S(1)}, bf16[128,1024]{1,0:T(8,128)(2,1)S(1)}, u32[]{:S(2)}, u32[]{:S(2)}) collective-permute-start(bf16[128,1024]{1,0:T(8,128)(2,1)S(1)} %collective-permute-done.11.refs_6_), channel_id=1, source_target_pairs={{2,0},{4,2},{6,4},{7,6},{5,7},{3,5},{1,3},{0,1},{10,8},{12,10},{14... | collective-permute-start | bytes 786440 | tf_op jit(solution)/shard_map/ppermute | solution.py:297
  59.7 0.0 copy-start.3
  59.8 4.7 %shard_map.88.refs_10_ = f32[1024,1408]{1,0:T(8,128)S(1)} custom-call(s32[18]{0:T(128)S(1)} %dynamic-slice_bitcast_fusion.where_ref, bf16[144,1024]{1,0:T(8,128)(2,1)S(1)} %collective-permute-done.9.block_ref, f32[8,256]{1,0:T(8,128)S(1)} %get-tuple-element.52.refs_0_.refs_8_, bf16[1024,1024]{1,0:T(8,128)(2,1)S(1)} %get-tuple-element.53.refs_1_, ...), custom_call_target="tpu_custom_call" | custom-call | tf_op jit(solution)/shard_map/pallas_call | solution.py:302
  64.5 1.2 %collective-permute-done.14.refs_7_ = bf16[128,1024]{1,0:T(8,128)(2,1)S(1)} collective-permute-done((bf16[128,1024]{1,0:T(8,128)(2,1)S(1)}, bf16[128,1024]{1,0:T(8,128)(2,1)S(1)}, u32[]{:S(2)}, u32[]{:S(2)}) %collective-permute-start.14) | collective-permute-done | bytes 262176 | tf_op jit(solution)/shard_map/ppermute | solution.py:297
  65.7 1.5 %collective-permute-start.16 = (bf16[128,1408]{1,0:T(8,128)(2,1)S(1)}, bf16[128,1408]{1,0:T(8,128)(2,1)S(1)}, u32[]{:S(2)}, u32[]{:S(2)}) collective-permute-start(bf16[128,1408]{1,0:T(8,128)(2,1)S(1)} %slice.13), channel_id=1, source_target_pairs={{0,16},{8,24},{16,0},{24,8},{1,17},{9,25},{17,1},{25,9},{2,18},{10... | collective-permute-start | bytes 1081352 | tf_op jit(solution)/shard_map/ppermute | solution.py:322
  67.1 7.9 %shard_map.89 = (bf16[1024,1408]{1,0:T(8,128)(2,1)}, f32[8,128]{1,0:T(8,128)S(1)}, bf16[1024,1024]{1,0:T(8,128)(2,1)S(1)}) custom-call(s32[18]{0:T(128)S(1)} %dynamic-slice_bitcast_fusion.where_ref, bf16[128,1024]{1,0:T(8,128)(2,1)S(1)} %copy-done.3, bf16[128,1024]{1,0:T(8,128)(2,1)S(1)} %collective-permute-done.5.refs_1_, ...), custom_call_target="tpu_custom_call" | custom-call | tf_op jit(solution)/shard_map/pallas_call | solution.py:302
  75.1 1.8 %shard_map.91 = bf16[512,1408]{1,0:T(8,128)(2,1)S(1)} custom-call(bf16[1024,1024]{1,0:T(8,128)(2,1)S(1)} %get-tuple-element.59.scaled_ref, bf16[1024,1408]{1,0:T(8,128)(2,1)S(1)} %bitcast.17), custom_call_target="tpu_custom_call" | custom-call | tf_op jit(solution)/shard_map/pallas_call | solution.py:393
  76.9 0.1 collective-permute-start.17
  77.0 1.2 %collective-permute-start.18 = (bf16[208,1408]{1,0:T(8,128)(2,1)S(1)}, bf16[208,1408]{1,0:T(8,128)(2,1)S(1)}, u32[]{:S(2)}, u32[]{:S(2)}) collective-permute-start(bf16[208,1408]{1,0:T(8,128)(2,1)S(1)} %slice.14), channel_id=1, source_target_pairs={{0,16},{8,24},{16,0},{24,8},{1,17},{9,25},{17,1},{25,9},{2,18},{10... | collective-permute-start | bytes 1757192 | tf_op jit(solution)/shard_map/ppermute | solution.py:322
  78.3 11.5 %all_to_all.11 = f32[8,1,128]{2,1,0:T(1,128)S(1)} all-to-all(f32[8,1,128]{2,1,0:T(1,128)S(1)} %bitcast.25), channel_id=1, replica_groups=mesh['dp'=4,'expert'=8] {'expert'}, dimensions={0} | all-to-all | bytes 8192 | tf_op jit(solution)/shard_map/all_to_all | solution.py:389
  89.8 0.6 select_reduce_fusion
  90.4 1.8 %shard_map.90.kept_ref = bf16[512,1408]{1,0:T(8,128)(2,1)S(1)} custom-call(bf16[1024,1024]{1,0:T(8,128)(2,1)S(1)} %get-tuple-element.59.scaled_ref, bf16[1024,1408]{1,0:T(8,128)(2,1)S(1)} %bitcast.18, f32[8,128]{1,0:T(8,128)S(1)} %bitcast.24), custom_call_target="tpu_custom_call" | custom-call | tf_op jit(solution)/shard_map/pallas_call | solution.py:393
  92.2 0.6 collective-permute-done.18.refs_2_
  92.8 1.7 %shard_map.92 = bf16[512,1408]{1,0:T(8,128)(2,1)} custom-call(bf16[512,1408]{1,0:T(8,128)(2,1)S(1)} %shard_map.90.kept_ref, bf16[512,1408]{1,0:T(8,128)(2,1)S(1)} %collective-permute-done.17.moved_ref, bf16[176,1408]{1,0:T(8,128)(2,1)S(1)} %collective-permute-done.15.refs_0_, bf16[128,1408]{1,0:T(8,128)(2,1)S(1)} %collective-permute-done.16.refs_1_, ...), custom_call_target="tpu_custom_call" | custom-call | tf_op jit(solution)/shard_map/pallas_call | solution.py:403
  (20 shorter events, 0.1 us)
Async XLA Ops:
  2.6 10.2 %collective-permute-start.2 = (bf16[144,1024]{1,0:T(8,128)(2,1)}, bf16[144,1024]{1,0:T(8,128)(2,1)S(1)}, u32[]{:S(2)}, u32[]{:S(2)}) collective-permute-start(bf16[144,1024]{1,0:T(8,128)(2,1)} %get-tuple-element.33.refs_0_), channel_id=1, source_target_pairs={{2,0},{4,2},{6,4},{7,6},{5,7},{3,5},{1,3},{0,1},{10,8},{12,10},{14... | collective-permute-start | bytes 884744 | tf_op jit(solution)/shard_map/ppermute | solution.py:297
  5.5 9.0 %collective-permute-start = (bf16[144,1024]{1,0:T(8,128)(2,1)}, bf16[144,1024]{1,0:T(8,128)(2,1)S(1)}, u32[]{:S(2)}, u32[]{:S(2)}) collective-permute-start(bf16[144,1024]{1,0:T(8,128)(2,1)} %get-tuple-element.33.refs_0_), channel_id=1, source_target_pairs={{0,2},{2,4},{4,6},{6,7},{7,5},{5,3},{3,1},{1,0},{8,10},{10,12},{12... | collective-permute-start | bytes 884744 | tf_op jit(solution)/shard_map/ppermute | solution.py:297
  12.8 8.2 %collective-permute-start.3 = (bf16[144,1024]{1,0:T(8,128)(2,1)S(1)}, bf16[144,1024]{1,0:T(8,128)(2,1)S(1)}, u32[]{:S(2)}, u32[]{:S(2)}) collective-permute-start(bf16[144,1024]{1,0:T(8,128)(2,1)S(1)} %collective-permute-done.2.refs_4_), channel_id=1, source_target_pairs={{2,0},{4,2},{6,4},{7,6},{5,7},{3,5},{1,3},{0,1},{10,8},{12,10},{14... | collective-permute-start | bytes 884744 | tf_op jit(solution)/shard_map/ppermute | solution.py:297
  14.5 7.6 %collective-permute-start.1 = (bf16[144,1024]{1,0:T(8,128)(2,1)S(1)}, bf16[144,1024]{1,0:T(8,128)(2,1)S(1)}, u32[]{:S(2)}, u32[]{:S(2)}) collective-permute-start(bf16[144,1024]{1,0:T(8,128)(2,1)S(1)} %collective-permute-done.refs_1_), channel_id=1, source_target_pairs={{0,2},{2,4},{4,6},{6,7},{7,5},{5,3},{3,1},{1,0},{8,10},{10,12},{12... | collective-permute-start | bytes 884744 | tf_op jit(solution)/shard_map/ppermute | solution.py:297
  22.1 13.0 %collective-permute-start.6 = (bf16[144,1024]{1,0:T(8,128)(2,1)S(1)}, bf16[144,1024]{1,0:T(8,128)(2,1)S(1)}, u32[]{:S(2)}, u32[]{:S(2)}) collective-permute-start(bf16[144,1024]{1,0:T(8,128)(2,1)S(1)} %collective-permute-done.1.refs_2_), channel_id=1, source_target_pairs={{0,2},{2,4},{4,6},{6,7},{7,5},{5,3},{3,1},{1,0},{8,10},{10,12},{12... | collective-permute-start | bytes 884744 | tf_op jit(solution)/shard_map/ppermute | solution.py:297
  22.8 12.3 %collective-permute-start.7 = (bf16[144,1024]{1,0:T(8,128)(2,1)S(1)}, bf16[144,1024]{1,0:T(8,128)(2,1)S(1)}, u32[]{:S(2)}, u32[]{:S(2)}) collective-permute-start(bf16[144,1024]{1,0:T(8,128)(2,1)S(1)} %collective-permute-done.3.refs_5_), channel_id=1, source_target_pairs={{2,0},{4,2},{6,4},{7,6},{5,7},{3,5},{1,3},{0,1},{10,8},{12,10},{14... | collective-permute-start | bytes 884744 | tf_op jit(solution)/shard_map/ppermute | solution.py:297
  24.1 10.3 %collective-permute-start.5 = (bf16[128,1024]{1,0:T(8,128)(2,1)}, bf16[128,1024]{1,0:T(8,128)(2,1)S(1)}, u32[]{:S(2)}, u32[]{:S(2)}) collective-permute-start(bf16[128,1024]{1,0:T(8,128)(2,1)} %get-tuple-element.54.refs_0_), channel_id=1, source_target_pairs={{0,2},{2,4},{4,6},{6,7},{7,5},{5,3},{3,1},{1,0},{8,10},{10,12},{12... | collective-permute-start | bytes 786440 | tf_op jit(solution)/shard_map/ppermute | solution.py:297
  24.8 10.3 %collective-permute-start.4 = (bf16[128,1024]{1,0:T(8,128)(2,1)}, bf16[128,1024]{1,0:T(8,128)(2,1)S(1)}, u32[]{:S(2)}, u32[]{:S(2)}) collective-permute-start(bf16[128,1024]{1,0:T(8,128)(2,1)} %get-tuple-element.54.refs_0_), channel_id=1, source_target_pairs={{2,0},{4,2},{6,4},{7,6},{5,7},{3,5},{1,3},{0,1},{10,8},{12,10},{14... | collective-permute-start | bytes 786440 | tf_op jit(solution)/shard_map/ppermute | solution.py:297
  35.1 11.4 %collective-permute-start.9 = (bf16[144,1024]{1,0:T(8,128)(2,1)S(1)}, bf16[144,1024]{1,0:T(8,128)(2,1)S(1)}, u32[]{:S(2)}, u32[]{:S(2)}) collective-permute-start(bf16[144,1024]{1,0:T(8,128)(2,1)S(1)} %collective-permute-done.6.refs_3_), channel_id=1, source_target_pairs={{0,2},{2,4},{4,6},{6,7},{7,5},{5,3},{3,1},{1,0},{8,10},{10,12},{12... | collective-permute-start | bytes 884744 | tf_op jit(solution)/shard_map/ppermute | solution.py:297
  36.3 10.0 %collective-permute-start.8 = (bf16[128,1024]{1,0:T(8,128)(2,1)S(1)}, bf16[128,1024]{1,0:T(8,128)(2,1)S(1)}, u32[]{:S(2)}, u32[]{:S(2)}) collective-permute-start(bf16[128,1024]{1,0:T(8,128)(2,1)S(1)} %collective-permute-done.4.refs_4_), channel_id=1, source_target_pairs={{2,0},{4,2},{6,4},{7,6},{5,7},{3,5},{1,3},{0,1},{10,8},{12,10},{14... | collective-permute-start | bytes 786440 | tf_op jit(solution)/shard_map/ppermute | solution.py:297
  37.1 9.4 %collective-permute-start.10 = (bf16[128,1024]{1,0:T(8,128)(2,1)S(1)}, bf16[128,1024]{1,0:T(8,128)(2,1)S(1)}, u32[]{:S(2)}, u32[]{:S(2)}) collective-permute-start(bf16[128,1024]{1,0:T(8,128)(2,1)S(1)} %collective-permute-done.5.refs_1_), channel_id=1, source_target_pairs={{0,2},{2,4},{4,6},{6,7},{7,5},{5,3},{3,1},{1,0},{8,10},{10,12},{12... | collective-permute-start | bytes 786440 | tf_op jit(solution)/shard_map/ppermute | solution.py:297
  38.3 1.8 %copy-start = (bf16[1,8,128,1408]{3,2,1,0:T(8,128)(2,1)S(1)}, bf16[1,8,128,1408]{3,2,1,0:T(8,128)(2,1)}, u32[]{:S(2)}) copy-start(bf16[1,8,128,1408]{3,2,1,0:T(8,128)(2,1)} %param.9) | copy-start | bytes 8650756
  40.2 1.0 %copy-start.2 = (bf16[144,1024]{1,0:T(8,128)(2,1)S(1)}, bf16[144,1024]{1,0:T(8,128)(2,1)}, u32[]{:S(2)}) copy-start(bf16[144,1024]{1,0:T(8,128)(2,1)} %get-tuple-element.33.refs_0_) | copy-start | bytes 884740
  41.1 5.4 %copy-start.1 = (bf16[1,8,128,1408]{3,2,1,0:T(8,128)(2,1)S(1)}, bf16[1,8,128,1408]{3,2,1,0:T(8,128)(2,1)}, u32[]{:S(2)}) copy-start(bf16[1,8,128,1408]{3,2,1,0:T(8,128)(2,1)} %param.9) | copy-start | bytes 8650756
  46.5 13.2 %slice-start = ((s8[5767168]{0:T(1024)(128)(4,1)}), s8[4194304]{0:T(1024)(128)(4,1)S(1)}, s32[]{:S(2)}) async-start(s8[5767168]{0:T(1024)(128)(4,1)} %bitcast.19), calls=%async_computation.1 | async-start | bytes 8388608
  46.5 13.2 %slice-start.1 = ((s8[5767168]{0:T(1024)(128)(4,1)}), s8[1572864]{0:T(1024)(128)(4,1)S(1)}, s32[]{:S(2)}) async-start(s8[5767168]{0:T(1024)(128)(4,1)} %bitcast.19), calls=%async_computation.2 | async-start | bytes 3145728
  48.2 3.3 %collective-permute-start.13 = (bf16[512,1408]{1,0:T(8,128)(2,1)S(1)}, bf16[512,1408]{1,0:T(8,128)(2,1)S(1)}, u32[]{:S(2)}, u32[]{:S(2)}) collective-permute-start(bf16[512,1408]{1,0:T(8,128)(2,1)S(1)} %get-tuple-element.49), channel_id=1, source_target_pairs={{0,8},{8,0},{16,24},{24,16},{1,9},{9,1},{17,25},{25,17},{2,10},{10... | collective-permute-start | bytes 4325384 | tf_op jit(solution)/shard_map/ppermute | solution.py:322
  48.3 8.7 %collective-permute-start.11 = (bf16[128,1024]{1,0:T(8,128)(2,1)S(1)}, bf16[128,1024]{1,0:T(8,128)(2,1)S(1)}, u32[]{:S(2)}, u32[]{:S(2)}) collective-permute-start(bf16[128,1024]{1,0:T(8,128)(2,1)S(1)} %collective-permute-done.8.refs_5_), channel_id=1, source_target_pairs={{2,0},{4,2},{6,4},{7,6},{5,7},{3,5},{1,3},{0,1},{10,8},{12,10},{14... | collective-permute-start | bytes 786440 | tf_op jit(solution)/shard_map/ppermute | solution.py:297
  49.7 8.4 %collective-permute-start.12 = (bf16[128,1024]{1,0:T(8,128)(2,1)S(1)}, bf16[128,1024]{1,0:T(8,128)(2,1)S(1)}, u32[]{:S(2)}, u32[]{:S(2)}) collective-permute-start(bf16[128,1024]{1,0:T(8,128)(2,1)S(1)} %collective-permute-done.10.refs_2_), channel_id=1, source_target_pairs={{0,2},{2,4},{4,6},{6,7},{7,5},{5,3},{3,1},{1,0},{8,10},{10,12},{12... | collective-permute-start | bytes 786440 | tf_op jit(solution)/shard_map/ppermute | solution.py:297
  51.9 13.8 %collective-permute-start.15 = (bf16[176,1408]{1,0:T(8,128)(2,1)S(1)}, bf16[176,1408]{1,0:T(8,128)(2,1)S(1)}, u32[]{:S(2)}, u32[]{:S(2)}) collective-permute-start(bf16[176,1408]{1,0:T(8,128)(2,1)S(1)} %slice.12), channel_id=1, source_target_pairs={{0,16},{8,24},{16,0},{24,8},{1,17},{9,25},{17,1},{25,9},{2,18},{10... | collective-permute-start | bytes 1486856 | tf_op jit(solution)/shard_map/ppermute | solution.py:322
  58.1 7.5 %collective-permute-start.14 = (bf16[128,1024]{1,0:T(8,128)(2,1)S(1)}, bf16[128,1024]{1,0:T(8,128)(2,1)S(1)}, u32[]{:S(2)}, u32[]{:S(2)}) collective-permute-start(bf16[128,1024]{1,0:T(8,128)(2,1)S(1)} %collective-permute-done.11.refs_6_), channel_id=1, source_target_pairs={{2,0},{4,2},{6,4},{7,6},{5,7},{3,5},{1,3},{0,1},{10,8},{12,10},{14... | collective-permute-start | bytes 786440 | tf_op jit(solution)/shard_map/ppermute | solution.py:297
  59.7 7.4 %copy-start.3 = (bf16[128,1024]{1,0:T(8,128)(2,1)S(1)}, bf16[128,1024]{1,0:T(8,128)(2,1)}, u32[]{:S(2)}) copy-start(bf16[128,1024]{1,0:T(8,128)(2,1)} %get-tuple-element.54.refs_0_) | copy-start | bytes 786436
  65.7 9.4 %collective-permute-start.16 = (bf16[128,1408]{1,0:T(8,128)(2,1)S(1)}, bf16[128,1408]{1,0:T(8,128)(2,1)S(1)}, u32[]{:S(2)}, u32[]{:S(2)}) collective-permute-start(bf16[128,1408]{1,0:T(8,128)(2,1)S(1)} %slice.13), channel_id=1, source_target_pairs={{0,16},{8,24},{16,0},{24,8},{1,17},{9,25},{17,1},{25,9},{2,18},{10... | collective-permute-start | bytes 1081352 | tf_op jit(solution)/shard_map/ppermute | solution.py:322
  75.1 14.7 %copy-start.4 = (s32[128,6]{0,1:T(8,128)S(1)}, s32[128,6]{0,1:T(8,128)}, u32[]{:S(2)}) copy-start(s32[128,6]{0,1:T(8,128)} %param.8) | copy-start | bytes 9220
  76.9 15.8 %collective-permute-start.17 = (bf16[512,1408]{1,0:T(8,128)(2,1)S(1)}, bf16[512,1408]{1,0:T(8,128)(2,1)S(1)}, u32[]{:S(2)}, u32[]{:S(2)}) collective-permute-start(bf16[512,1408]{1,0:T(8,128)(2,1)S(1)} %shard_map.91), channel_id=1, source_target_pairs={{0,8},{8,0},{16,24},{24,16},{1,9},{9,1},{17,25},{25,17},{2,10},{10... | collective-permute-start | bytes 4325384 | tf_op jit(solution)/shard_map/ppermute | solution.py:322
  77.0 15.7 %collective-permute-start.18 = (bf16[208,1408]{1,0:T(8,128)(2,1)S(1)}, bf16[208,1408]{1,0:T(8,128)(2,1)S(1)}, u32[]{:S(2)}, u32[]{:S(2)}) collective-permute-start(bf16[208,1408]{1,0:T(8,128)(2,1)S(1)} %slice.14), channel_id=1, source_target_pairs={{0,16},{8,24},{16,0},{24,8},{1,17},{9,25},{17,1},{25,9},{2,18},{10... | collective-permute-start | bytes 1757192 | tf_op jit(solution)/shard_map/ppermute | solution.py:322

commit v4 on v3

--- a/solution.py
+++ b/solution.py
@@ -147,8 +147,7 @@
         ).astype(jnp.bfloat16)
 
 
-def part_kernel(low, scaled_ref, hidden_ref, *refs):
-    part_refs = refs if low == 0 else refs[1:]
+def part_kernel(low, scaled_ref, hidden_ref, *part_refs):
     wide = part_refs[0].shape[0]
     for j, part_ref in enumerate(part_refs):
         here = slice(low + j * wide, low + (j + 1) * wide)
@@ -200,7 +199,7 @@
         sum_ref[here, :] = projected(placed_ref[here, :], where_ref[1], masks, w_ref, wide)
         return carry
 
-    lax.fori_loop(0, placed_ref.shape[0] // size, some, 0)
+    lax.fori_loop(0, placed_ref.shape[0] // size, some, 0, unroll=True)
 
 
 def finish(acc, row, cap, tokens, saved, grad_ref, here, token_ref, line):
@@ -238,7 +237,7 @@
             finish(acc[part], row, cap, tokens, saved[part], grad_ref, there, token_ref, source)
         return carry
 
-    lax.fori_loop(0, placed_ref.shape[0] // size, some, 0)
+    lax.fori_loop(0, placed_ref.shape[0] // size, some, 0, unroll=True)
 
 
 def after(value, *others):
@@ -389,17 +388,17 @@
     returned = lax.all_to_all(by_token, "expert", split_axis=0, concat_axis=0, tiled=True)
     scaled = after(scaled, *ready)
 
-    def part_of(low, *others):
+    def part_of(low):
         return pl.pallas_call(
             functools.partial(part_kernel, low),
             out_shape=[jax.ShapeDtypeStruct(*piece)] * (top // 2),
-            in_specs=[vmem] * (2 + len(others)),
+            in_specs=[vmem] * 2,
             out_specs=[vmem] * (top // 2),
             compiler_params=pltpu.CompilerParams(vmem_limit_bytes=16 * MIB),
-        )(scaled, hidden2, *others)
+        )(scaled, hidden2)
 
     moved = [exchange(p, 0) for p in part_of(0)]
-    kept, moved = reduced(part_of(columns // 2, returned), moved)
+    kept, moved = reduced(part_of(columns // 2), moved)
     grad_down = pl.pallas_call(
         final_kernel,
         out_shape=jax.ShapeDtypeStruct((wide, inner), jnp.bfloat16),

time: 94.7 us -> 94.5 us (level)
  Pallas kernels: 26.7 us -> 25.4 us
  waiting for transfers between devices: 30.6 us -> 31.6 us
    pallas_call x4, Pallas kernels: 19.5 us -> 18.3 us  [call(): pl.pallas_call(kernel, out_shape=[jax.ShapeDtypeStruct(*out) for out in o...]
  transfers between devices with their start and end apart: 19 -> 19, of which waited for: 11 -> 12; matrix products, arithmetic and copies ran while one was open for 2% -> 2% of each run, Pallas kernels for 21% -> 20%
where the time goes in v4:
time: 94.5 us; the launch traced here: 94.2 us
  waiting for transfers between devices  31.6 us (33%)
  Pallas kernels  25.4 us (27%)
  starting transfers between devices  20.4 us (22%)
  blocking collectives  11.5 us (12%)
  local copies, waits for them, and re-layouts  3.6 us (4%)
  other arithmetic  0.96 us (1%)
    ppermute x14, waiting for transfers between devices, step(): got[chunk][sign * k] = lax.ppermute(value, 'expert', pairs)  29.5 us
    pallas_call x4, Pallas kernels, call(): pl.pallas_call(kernel, out_shape=[jax.ShapeDtypeStruct(*out) for out in o...  18.3 us
    ppermute x14, starting transfers between devices, step(): got[chunk][sign * k] = lax.ppermute(value, 'expert', pairs)  16 us
    all_to_all x1, blocking collectives, body(): lax.all_to_all(by_token, 'expert', split_axis=0, concat_axis=0, tiled=True)  11.5 us
    ppermute x5, starting transfers between devices, exchange(): return lax.ppermute(value, 'dp', [(r, r ^ 1 << b) for r in range(replicas)])  4.42 us
    pallas_call x2, Pallas kernels, part_of(): pl.pallas_call(functools.partial(part_kernel, low), out_shape=[jax.ShapeD...  3.64 us
    unnamed x14, local copies, waits for them, and re-layouts  2.8 us
    ppermute x5, waiting for transfers between devices, exchange(): return lax.ppermute(value, 'dp', [(r, r ^ 1 << b) for r in range(replicas)])  2.08 us
  transfers between devices with their start and end apart: 19, of which 12 were waited for; matrix products, arithmetic and copies ran while one was open for 2% of the time, Pallas kernels for 20%

profile of v4, /device:TPU:0, one launch (start us, length us, event | category | flops | bytes accessed | tf_op | source)
XLA Modules:
  0.0 94.2 jit_solution(7799474601064485573)
XLA Ops:
  0.6 1.9 %shard_map.85 = (bf16[144,1024]{1,0:T(8,128)(2,1)}, bf16[128,1024]{1,0:T(8,128)(2,1)}) custom-call(s32[6,128]{1,0:T(8,128)} %bitcast.25, bf16[6,128]{1,0:T(8,128)(2,1)} %bitcast.27, bf16[128,2048]{1,0:T(8,128)(2,1)} %grad_ref.1), custom_call_target="tpu_custom_call" | custom-call | tf_op jit(solution)/shard_map/pallas_call | solution.py:270
  2.6 3.0 %collective-permute-start.2 = (bf16[144,1024]{1,0:T(8,128)(2,1)}, bf16[144,1024]{1,0:T(8,128)(2,1)S(1)}, u32[]{:S(2)}, u32[]{:S(2)}) collective-permute-start(bf16[144,1024]{1,0:T(8,128)(2,1)} %get-tuple-element.33.refs_0_), channel_id=1, source_target_pairs={{2,0},{4,2},{6,4},{7,6},{5,7},{3,5},{1,3},{0,1},{10,8},{12,10},{14... | collective-permute-start | bytes 884744 | tf_op jit(solution)/shard_map/ppermute | solution.py:296
  5.5 0.1 collective-permute-start
  5.6 0.7 dynamic-slice_bitcast_fusion.where_ref
  6.3 6.5 %collective-permute-done.2.refs_4_ = bf16[144,1024]{1,0:T(8,128)(2,1)S(1)} collective-permute-done((bf16[144,1024]{1,0:T(8,128)(2,1)}, bf16[144,1024]{1,0:T(8,128)(2,1)S(1)}, u32[]{:S(2)}, u32[]{:S(2)}) %collective-permute-start.2) | collective-permute-done | bytes 294944 | tf_op jit(solution)/shard_map/ppermute | solution.py:296
  12.8 1.7 %collective-permute-start.3 = (bf16[144,1024]{1,0:T(8,128)(2,1)S(1)}, bf16[144,1024]{1,0:T(8,128)(2,1)S(1)}, u32[]{:S(2)}, u32[]{:S(2)}) collective-permute-start(bf16[144,1024]{1,0:T(8,128)(2,1)S(1)} %collective-permute-done.2.refs_4_), channel_id=1, source_target_pairs={{2,0},{4,2},{6,4},{7,6},{5,7},{3,5},{1,3},{0,1},{10,8},{12,10},{14... | collective-permute-start | bytes 884744 | tf_op jit(solution)/shard_map/ppermute | solution.py:296
  14.5 0.3 collective-permute-start.1
  14.8 6.2 %collective-permute-done.3.refs_5_ = bf16[144,1024]{1,0:T(8,128)(2,1)S(1)} collective-permute-done((bf16[144,1024]{1,0:T(8,128)(2,1)S(1)}, bf16[144,1024]{1,0:T(8,128)(2,1)S(1)}, u32[]{:S(2)}, u32[]{:S(2)}) %collective-permute-start.3) | collective-permute-done | bytes 294944 | tf_op jit(solution)/shard_map/ppermute | solution.py:296
  21.0 1.1 %collective-permute-done.1.refs_2_ = bf16[144,1024]{1,0:T(8,128)(2,1)S(1)} collective-permute-done((bf16[144,1024]{1,0:T(8,128)(2,1)S(1)}, bf16[144,1024]{1,0:T(8,128)(2,1)S(1)}, u32[]{:S(2)}, u32[]{:S(2)}) %collective-permute-start.1) | collective-permute-done | bytes 294944 | tf_op jit(solution)/shard_map/ppermute | solution.py:296
  22.1 0.7 collective-permute-start.6
  22.8 1.4 %collective-permute-start.7 = (bf16[144,1024]{1,0:T(8,128)(2,1)S(1)}, bf16[144,1024]{1,0:T(8,128)(2,1)S(1)}, u32[]{:S(2)}, u32[]{:S(2)}) collective-permute-start(bf16[144,1024]{1,0:T(8,128)(2,1)S(1)} %collective-permute-done.3.refs_5_), channel_id=1, source_target_pairs={{2,0},{4,2},{6,4},{7,6},{5,7},{3,5},{1,3},{0,1},{10,8},{12,10},{14... | collective-permute-start | bytes 884744 | tf_op jit(solution)/shard_map/ppermute | solution.py:296
  24.1 0.7 collective-permute-start.5
  24.8 1.4 %collective-permute-start.4 = (bf16[128,1024]{1,0:T(8,128)(2,1)}, bf16[128,1024]{1,0:T(8,128)(2,1)S(1)}, u32[]{:S(2)}, u32[]{:S(2)}) collective-permute-start(bf16[128,1024]{1,0:T(8,128)(2,1)} %get-tuple-element.54.refs_0_), channel_id=1, source_target_pairs={{2,0},{4,2},{6,4},{7,6},{5,7},{3,5},{1,3},{0,1},{10,8},{12,10},{14... | collective-permute-start | bytes 786440 | tf_op jit(solution)/shard_map/ppermute | solution.py:296
  26.1 8.2 %collective-permute-done.5.refs_1_ = bf16[128,1024]{1,0:T(8,128)(2,1)S(1)} collective-permute-done((bf16[128,1024]{1,0:T(8,128)(2,1)}, bf16[128,1024]{1,0:T(8,128)(2,1)S(1)}, u32[]{:S(2)}, u32[]{:S(2)}) %collective-permute-start.5) | collective-permute-done | bytes 262176 | tf_op jit(solution)/shard_map/ppermute | solution.py:296
  34.4 0.7 collective-permute-done.4.refs_4_
  35.1 0.0 collective-permute-done.6.refs_3_
  35.1 1.2 %collective-permute-start.9 = (bf16[144,1024]{1,0:T(8,128)(2,1)S(1)}, bf16[144,1024]{1,0:T(8,128)(2,1)S(1)}, u32[]{:S(2)}, u32[]{:S(2)}) collective-permute-start(bf16[144,1024]{1,0:T(8,128)(2,1)S(1)} %collective-permute-done.6.refs_3_), channel_id=1, source_target_pairs={{0,2},{2,4},{4,6},{6,7},{7,5},{5,3},{3,1},{1,0},{8,10},{10,12},{12... | collective-permute-start | bytes 884744 | tf_op jit(solution)/shard_map/ppermute | solution.py:296
  36.3 0.8 collective-permute-start.8
  37.1 1.2 %collective-permute-start.10 = (bf16[128,1024]{1,0:T(8,128)(2,1)S(1)}, bf16[128,1024]{1,0:T(8,128)(2,1)S(1)}, u32[]{:S(2)}, u32[]{:S(2)}) collective-permute-start(bf16[128,1024]{1,0:T(8,128)(2,1)S(1)} %collective-permute-done.5.refs_1_), channel_id=1, source_target_pairs={{0,2},{2,4},{4,6},{6,7},{7,5},{5,3},{3,1},{1,0},{8,10},{10,12},{12... | collective-permute-start | bytes 786440 | tf_op jit(solution)/shard_map/ppermute | solution.py:296
  38.3 1.8 %copy-done = bf16[1,8,128,1408]{3,2,1,0:T(8,128)(2,1)S(1)} copy-done((bf16[1,8,128,1408]{3,2,1,0:T(8,128)(2,1)S(1)}, bf16[1,8,128,1408]{3,2,1,0:T(8,128)(2,1)}, u32[]{:S(2)}) %copy-start) | copy-done | bytes 2883608
  40.2 1.0 %copy-done.2 = bf16[144,1024]{1,0:T(8,128)(2,1)S(1)} copy-done((bf16[144,1024]{1,0:T(8,128)(2,1)S(1)}, bf16[144,1024]{1,0:T(8,128)(2,1)}, u32[]{:S(2)}) %copy-start.2) | copy-done | bytes 294936
  41.1 5.2 %shard_map.86 = (f32[8,256]{1,0:T(8,128)S(1)}, bf16[1024,1024]{1,0:T(8,128)(2,1)S(1)}, f32[512,1408]{1,0:T(8,128)S(1)}, f32[512,1408]{1,0:T(8,128)S(1)}) custom-call(s32[18]{0:T(128)S(1)} %dynamic-slice_bitcast_fusion.where_ref, bf16[144,1024]{1,0:T(8,128)(2,1)S(1)} %copy-done.2, bf16[144,1024]{1,0:T(8,128)(2,1)S(1)} %collective-permute-done.refs_1_, ...), custom_call_target="tpu_custom_call" | custom-call | tf_op jit(solution)/shard_map/pallas_call | solution.py:301
  46.3 0.0 collective-permute-done.8.refs_5_
  46.3 0.2 collective-permute-done.10.refs_2_
  46.5 1.7 %shard_map.87 = (bf16[512,1408]{1,0:T(8,128)(2,1)S(1)}, bf16[512,1408]{1,0:T(8,128)(2,1)S(1)}, f32[8,256]{1,0:T(8,128)S(1)}) custom-call(s32[18]{0:T(128)S(1)} %dynamic-slice_bitcast_fusion.where_ref, bf16[144,1024]{1,0:T(8,128)(2,1)S(1)} %collective-permute-done.9.block_ref, f32[8,256]{1,0:T(8,128)S(1)} %get-tuple-element.45.near_ref, ...), custom_call_target="tpu_custom_call" | custom-call | tf_op jit(solution)/shard_map/pallas_call | solution.py:301
  48.2 0.1 collective-permute-start.13
  48.3 1.4 %collective-permute-start.11 = (bf16[128,1024]{1,0:T(8,128)(2,1)S(1)}, bf16[128,1024]{1,0:T(8,128)(2,1)S(1)}, u32[]{:S(2)}, u32[]{:S(2)}) collective-permute-start(bf16[128,1024]{1,0:T(8,128)(2,1)S(1)} %collective-permute-done.8.refs_5_), channel_id=1, source_target_pairs={{2,0},{4,2},{6,4},{7,6},{5,7},{3,5},{1,3},{0,1},{10,8},{12,10},{14... | collective-permute-start | bytes 786440 | tf_op jit(solution)/shard_map/ppermute | solution.py:296
  49.7 0.6 collective-permute-start.12
  50.4 1.1 %collective-permute-done.13 = bf16[512,1408]{1,0:T(8,128)(2,1)S(1)} collective-permute-done((bf16[512,1408]{1,0:T(8,128)(2,1)S(1)}, bf16[512,1408]{1,0:T(8,128)(2,1)S(1)}, u32[]{:S(2)}, u32[]{:S(2)}) %collective-permute-start.13) | collective-permute-done | bytes 1441824 | tf_op jit(solution)/shard_map/ppermute | solution.py:321
  51.5 0.3 add_convert_fusion
  51.9 1.4 %collective-permute-start.15 = (bf16[176,1408]{1,0:T(8,128)(2,1)S(1)}, bf16[176,1408]{1,0:T(8,128)(2,1)S(1)}, u32[]{:S(2)}, u32[]{:S(2)}) collective-permute-start(bf16[176,1408]{1,0:T(8,128)(2,1)S(1)} %slice.12), channel_id=1, source_target_pairs={{0,16},{8,24},{16,0},{24,8},{1,17},{9,25},{17,1},{25,9},{2,18},{10... | collective-permute-start | bytes 1486856 | tf_op jit(solution)/shard_map/ppermute | solution.py:321
  53.3 3.7 %collective-permute-done.11.refs_6_ = bf16[128,1024]{1,0:T(8,128)(2,1)S(1)} collective-permute-done((bf16[128,1024]{1,0:T(8,128)(2,1)S(1)}, bf16[128,1024]{1,0:T(8,128)(2,1)S(1)}, u32[]{:S(2)}, u32[]{:S(2)}) %collective-permute-start.11) | collective-permute-done | bytes 262176 | tf_op jit(solution)/shard_map/ppermute | solution.py:296
  57.0 1.1 %collective-permute-done.12.refs_3_ = bf16[128,1024]{1,0:T(8,128)(2,1)S(1)} collective-permute-done((bf16[128,1024]{1,0:T(8,128)(2,1)S(1)}, bf16[128,1024]{1,0:T(8,128)(2,1)S(1)}, u32[]{:S(2)}, u32[]{:S(2)}) %collective-permute-start.12) | collective-permute-done | bytes 262176 | tf_op jit(solution)/shard_map/ppermute | solution.py:296
  58.1 1.6 %collective-permute-start.14 = (bf16[128,1024]{1,0:T(8,128)(2,1)S(1)}, bf16[128,1024]{1,0:T(8,128)(2,1)S(1)}, u32[]{:S(2)}, u32[]{:S(2)}) collective-permute-start(bf16[128,1024]{1,0:T(8,128)(2,1)S(1)} %collective-permute-done.11.refs_6_), channel_id=1, source_target_pairs={{2,0},{4,2},{6,4},{7,6},{5,7},{3,5},{1,3},{0,1},{10,8},{12,10},{14... | collective-permute-start | bytes 786440 | tf_op jit(solution)/shard_map/ppermute | solution.py:296
  59.7 0.0 copy-start.3
  59.8 4.2 %shard_map.88.refs_10_ = f32[1024,1408]{1,0:T(8,128)S(1)} custom-call(s32[18]{0:T(128)S(1)} %dynamic-slice_bitcast_fusion.where_ref, bf16[144,1024]{1,0:T(8,128)(2,1)S(1)} %collective-permute-done.9.block_ref, f32[8,256]{1,0:T(8,128)S(1)} %get-tuple-element.52.refs_0_.refs_8_, bf16[1024,1024]{1,0:T(8,128)(2,1)S(1)} %get-tuple-element.53.refs_1_, ...), custom_call_target="tpu_custom_call" | custom-call | tf_op jit(solution)/shard_map/pallas_call | solution.py:301
  63.9 1.7 %collective-permute-done.14.refs_7_ = bf16[128,1024]{1,0:T(8,128)(2,1)S(1)} collective-permute-done((bf16[128,1024]{1,0:T(8,128)(2,1)S(1)}, bf16[128,1024]{1,0:T(8,128)(2,1)S(1)}, u32[]{:S(2)}, u32[]{:S(2)}) %collective-permute-start.14) | collective-permute-done | bytes 262176 | tf_op jit(solution)/shard_map/ppermute | solution.py:296
  65.7 1.5 %collective-permute-start.16 = (bf16[128,1408]{1,0:T(8,128)(2,1)S(1)}, bf16[128,1408]{1,0:T(8,128)(2,1)S(1)}, u32[]{:S(2)}, u32[]{:S(2)}) collective-permute-start(bf16[128,1408]{1,0:T(8,128)(2,1)S(1)} %slice.13), channel_id=1, source_target_pairs={{0,16},{8,24},{16,0},{24,8},{1,17},{9,25},{17,1},{25,9},{2,18},{10... | collective-permute-start | bytes 1081352 | tf_op jit(solution)/shard_map/ppermute | solution.py:321
  67.1 7.2 %shard_map.89 = (bf16[1024,1408]{1,0:T(8,128)(2,1)}, f32[8,128]{1,0:T(8,128)S(1)}, bf16[1024,1024]{1,0:T(8,128)(2,1)S(1)}) custom-call(s32[18]{0:T(128)S(1)} %dynamic-slice_bitcast_fusion.where_ref, bf16[128,1024]{1,0:T(8,128)(2,1)S(1)} %copy-done.3, bf16[128,1024]{1,0:T(8,128)(2,1)S(1)} %collective-permute-done.5.refs_1_, ...), custom_call_target="tpu_custom_call" | custom-call | tf_op jit(solution)/shard_map/pallas_call | solution.py:301
  74.4 0.5 collective-permute-done.16.refs_1_
  74.9 1.8 %shard_map.91 = bf16[512,1408]{1,0:T(8,128)(2,1)S(1)} custom-call(bf16[1024,1024]{1,0:T(8,128)(2,1)S(1)} %get-tuple-element.59.scaled_ref, bf16[1024,1408]{1,0:T(8,128)(2,1)S(1)} %bitcast.17), custom_call_target="tpu_custom_call" | custom-call | tf_op jit(solution)/shard_map/pallas_call | solution.py:392
  76.8 0.1 collective-permute-start.17
  76.9 1.4 %collective-permute-start.18 = (bf16[208,1408]{1,0:T(8,128)(2,1)S(1)}, bf16[208,1408]{1,0:T(8,128)(2,1)S(1)}, u32[]{:S(2)}, u32[]{:S(2)}) collective-permute-start(bf16[208,1408]{1,0:T(8,128)(2,1)S(1)} %slice.14), channel_id=1, source_target_pairs={{0,16},{8,24},{16,0},{24,8},{1,17},{9,25},{17,1},{25,9},{2,18},{10... | collective-permute-start | bytes 1757192 | tf_op jit(solution)/shard_map/ppermute | solution.py:321
  78.3 11.5 %all_to_all.12 = f32[8,1,128]{2,1,0:T(1,128)S(1)} all-to-all(f32[8,1,128]{2,1,0:T(1,128)S(1)} %bitcast.23), channel_id=1, replica_groups=mesh['dp'=4,'expert'=8] {'expert'}, dimensions={0} | all-to-all | bytes 8192 | tf_op jit(solution)/shard_map/all_to_all | solution.py:388
  89.8 0.6 select_reduce_fusion
  90.4 1.8 %shard_map.90.kept_ref = bf16[512,1408]{1,0:T(8,128)(2,1)S(1)} custom-call(bf16[1024,1024]{1,0:T(8,128)(2,1)S(1)} %get-tuple-element.59.scaled_ref, bf16[1024,1408]{1,0:T(8,128)(2,1)S(1)} %bitcast.18), custom_call_target="tpu_custom_call" | custom-call | tf_op jit(solution)/shard_map/pallas_call | solution.py:392
  92.2 0.4 collective-permute-done.18.refs_2_
  92.6 1.6 %shard_map.92 = bf16[512,1408]{1,0:T(8,128)(2,1)} custom-call(bf16[512,1408]{1,0:T(8,128)(2,1)S(1)} %shard_map.90.kept_ref, bf16[512,1408]{1,0:T(8,128)(2,1)S(1)} %collective-permute-done.17.moved_ref, bf16[176,1408]{1,0:T(8,128)(2,1)S(1)} %collective-permute-done.15.refs_0_, bf16[128,1408]{1,0:T(8,128)(2,1)S(1)} %collective-permute-done.16.refs_1_, ...), custom_call_target="tpu_custom_call" | custom-call | tf_op jit(solution)/shard_map/pallas_call | solution.py:402
  (20 shorter events, 0.1 us)
Async XLA Ops:
  2.6 10.2 %collective-permute-start.2 = (bf16[144,1024]{1,0:T(8,128)(2,1)}, bf16[144,1024]{1,0:T(8,128)(2,1)S(1)}, u32[]{:S(2)}, u32[]{:S(2)}) collective-permute-start(bf16[144,1024]{1,0:T(8,128)(2,1)} %get-tuple-element.33.refs_0_), channel_id=1, source_target_pairs={{2,0},{4,2},{6,4},{7,6},{5,7},{3,5},{1,3},{0,1},{10,8},{12,10},{14... | collective-permute-start | bytes 884744 | tf_op jit(solution)/shard_map/ppermute | solution.py:296
  5.5 9.0 %collective-permute-start = (bf16[144,1024]{1,0:T(8,128)(2,1)}, bf16[144,1024]{1,0:T(8,128)(2,1)S(1)}, u32[]{:S(2)}, u32[]{:S(2)}) collective-permute-start(bf16[144,1024]{1,0:T(8,128)(2,1)} %get-tuple-element.33.refs_0_), channel_id=1, source_target_pairs={{0,2},{2,4},{4,6},{6,7},{7,5},{5,3},{3,1},{1,0},{8,10},{10,12},{12... | collective-permute-start | bytes 884744 | tf_op jit(solution)/shard_map/ppermute | solution.py:296
  12.8 8.2 %collective-permute-start.3 = (bf16[144,1024]{1,0:T(8,128)(2,1)S(1)}, bf16[144,1024]{1,0:T(8,128)(2,1)S(1)}, u32[]{:S(2)}, u32[]{:S(2)}) collective-permute-start(bf16[144,1024]{1,0:T(8,128)(2,1)S(1)} %collective-permute-done.2.refs_4_), channel_id=1, source_target_pairs={{2,0},{4,2},{6,4},{7,6},{5,7},{3,5},{1,3},{0,1},{10,8},{12,10},{14... | collective-permute-start | bytes 884744 | tf_op jit(solution)/shard_map/ppermute | solution.py:296
  14.5 7.6 %collective-permute-start.1 = (bf16[144,1024]{1,0:T(8,128)(2,1)S(1)}, bf16[144,1024]{1,0:T(8,128)(2,1)S(1)}, u32[]{:S(2)}, u32[]{:S(2)}) collective-permute-start(bf16[144,1024]{1,0:T(8,128)(2,1)S(1)} %collective-permute-done.refs_1_), channel_id=1, source_target_pairs={{0,2},{2,4},{4,6},{6,7},{7,5},{5,3},{3,1},{1,0},{8,10},{10,12},{12... | collective-permute-start | bytes 884744 | tf_op jit(solution)/shard_map/ppermute | solution.py:296
  22.1 13.0 %collective-permute-start.6 = (bf16[144,1024]{1,0:T(8,128)(2,1)S(1)}, bf16[144,1024]{1,0:T(8,128)(2,1)S(1)}, u32[]{:S(2)}, u32[]{:S(2)}) collective-permute-start(bf16[144,1024]{1,0:T(8,128)(2,1)S(1)} %collective-permute-done.1.refs_2_), channel_id=1, source_target_pairs={{0,2},{2,4},{4,6},{6,7},{7,5},{5,3},{3,1},{1,0},{8,10},{10,12},{12... | collective-permute-start | bytes 884744 | tf_op jit(solution)/shard_map/ppermute | solution.py:296
  22.8 12.3 %collective-permute-start.7 = (bf16[144,1024]{1,0:T(8,128)(2,1)S(1)}, bf16[144,1024]{1,0:T(8,128)(2,1)S(1)}, u32[]{:S(2)}, u32[]{:S(2)}) collective-permute-start(bf16[144,1024]{1,0:T(8,128)(2,1)S(1)} %collective-permute-done.3.refs_5_), channel_id=1, source_target_pairs={{2,0},{4,2},{6,4},{7,6},{5,7},{3,5},{1,3},{0,1},{10,8},{12,10},{14... | collective-permute-start | bytes 884744 | tf_op jit(solution)/shard_map/ppermute | solution.py:296
  24.1 10.3 %collective-permute-start.5 = (bf16[128,1024]{1,0:T(8,128)(2,1)}, bf16[128,1024]{1,0:T(8,128)(2,1)S(1)}, u32[]{:S(2)}, u32[]{:S(2)}) collective-permute-start(bf16[128,1024]{1,0:T(8,128)(2,1)} %get-tuple-element.54.refs_0_), channel_id=1, source_target_pairs={{0,2},{2,4},{4,6},{6,7},{7,5},{5,3},{3,1},{1,0},{8,10},{10,12},{12... | collective-permute-start | bytes 786440 | tf_op jit(solution)/shard_map/ppermute | solution.py:296
  24.8 10.3 %collective-permute-start.4 = (bf16[128,1024]{1,0:T(8,128)(2,1)}, bf16[128,1024]{1,0:T(8,128)(2,1)S(1)}, u32[]{:S(2)}, u32[]{:S(2)}) collective-permute-start(bf16[128,1024]{1,0:T(8,128)(2,1)} %get-tuple-element.54.refs_0_), channel_id=1, source_target_pairs={{2,0},{4,2},{6,4},{7,6},{5,7},{3,5},{1,3},{0,1},{10,8},{12,10},{14... | collective-permute-start | bytes 786440 | tf_op jit(solution)/shard_map/ppermute | solution.py:296
  35.1 11.4 %collective-permute-start.9 = (bf16[144,1024]{1,0:T(8,128)(2,1)S(1)}, bf16[144,1024]{1,0:T(8,128)(2,1)S(1)}, u32[]{:S(2)}, u32[]{:S(2)}) collective-permute-start(bf16[144,1024]{1,0:T(8,128)(2,1)S(1)} %collective-permute-done.6.refs_3_), channel_id=1, source_target_pairs={{0,2},{2,4},{4,6},{6,7},{7,5},{5,3},{3,1},{1,0},{8,10},{10,12},{12... | collective-permute-start | bytes 884744 | tf_op jit(solution)/shard_map/ppermute | solution.py:296
  36.3 10.0 %collective-permute-start.8 = (bf16[128,1024]{1,0:T(8,128)(2,1)S(1)}, bf16[128,1024]{1,0:T(8,128)(2,1)S(1)}, u32[]{:S(2)}, u32[]{:S(2)}) collective-permute-start(bf16[128,1024]{1,0:T(8,128)(2,1)S(1)} %collective-permute-done.4.refs_4_), channel_id=1, source_target_pairs={{2,0},{4,2},{6,4},{7,6},{5,7},{3,5},{1,3},{0,1},{10,8},{12,10},{14... | collective-permute-start | bytes 786440 | tf_op jit(solution)/shard_map/ppermute | solution.py:296
  37.1 9.4 %collective-permute-start.10 = (bf16[128,1024]{1,0:T(8,128)(2,1)S(1)}, bf16[128,1024]{1,0:T(8,128)(2,1)S(1)}, u32[]{:S(2)}, u32[]{:S(2)}) collective-permute-start(bf16[128,1024]{1,0:T(8,128)(2,1)S(1)} %collective-permute-done.5.refs_1_), channel_id=1, source_target_pairs={{0,2},{2,4},{4,6},{6,7},{7,5},{5,3},{3,1},{1,0},{8,10},{10,12},{12... | collective-permute-start | bytes 786440 | tf_op jit(solution)/shard_map/ppermute | solution.py:296
  38.3 1.8 %copy-start = (bf16[1,8,128,1408]{3,2,1,0:T(8,128)(2,1)S(1)}, bf16[1,8,128,1408]{3,2,1,0:T(8,128)(2,1)}, u32[]{:S(2)}) copy-start(bf16[1,8,128,1408]{3,2,1,0:T(8,128)(2,1)} %param.9) | copy-start | bytes 8650756
  40.2 1.0 %copy-start.2 = (bf16[144,1024]{1,0:T(8,128)(2,1)S(1)}, bf16[144,1024]{1,0:T(8,128)(2,1)}, u32[]{:S(2)}) copy-start(bf16[144,1024]{1,0:T(8,128)(2,1)} %get-tuple-element.33.refs_0_) | copy-start | bytes 884740
  41.1 5.4 %copy-start.1 = (bf16[1,8,128,1408]{3,2,1,0:T(8,128)(2,1)S(1)}, bf16[1,8,128,1408]{3,2,1,0:T(8,128)(2,1)}, u32[]{:S(2)}) copy-start(bf16[1,8,128,1408]{3,2,1,0:T(8,128)(2,1)} %param.9) | copy-start | bytes 8650756
  46.5 13.2 %slice-start = ((s8[5767168]{0:T(1024)(128)(4,1)}), s8[4194304]{0:T(1024)(128)(4,1)S(1)}, s32[]{:S(2)}) async-start(s8[5767168]{0:T(1024)(128)(4,1)} %bitcast.19), calls=%async_computation.1 | async-start | bytes 8388608
  46.5 13.2 %slice-start.1 = ((s8[5767168]{0:T(1024)(128)(4,1)}), s8[1572864]{0:T(1024)(128)(4,1)S(1)}, s32[]{:S(2)}) async-start(s8[5767168]{0:T(1024)(128)(4,1)} %bitcast.19), calls=%async_computation.2 | async-start | bytes 3145728
  48.2 3.3 %collective-permute-start.13 = (bf16[512,1408]{1,0:T(8,128)(2,1)S(1)}, bf16[512,1408]{1,0:T(8,128)(2,1)S(1)}, u32[]{:S(2)}, u32[]{:S(2)}) collective-permute-start(bf16[512,1408]{1,0:T(8,128)(2,1)S(1)} %get-tuple-element.49), channel_id=1, source_target_pairs={{0,8},{8,0},{16,24},{24,16},{1,9},{9,1},{17,25},{25,17},{2,10},{10... | collective-permute-start | bytes 4325384 | tf_op jit(solution)/shard_map/ppermute | solution.py:321
  48.3 8.7 %collective-permute-start.11 = (bf16[128,1024]{1,0:T(8,128)(2,1)S(1)}, bf16[128,1024]{1,0:T(8,128)(2,1)S(1)}, u32[]{:S(2)}, u32[]{:S(2)}) collective-permute-start(bf16[128,1024]{1,0:T(8,128)(2,1)S(1)} %collective-permute-done.8.refs_5_), channel_id=1, source_target_pairs={{2,0},{4,2},{6,4},{7,6},{5,7},{3,5},{1,3},{0,1},{10,8},{12,10},{14... | collective-permute-start | bytes 786440 | tf_op jit(solution)/shard_map/ppermute | solution.py:296
  49.7 8.4 %collective-permute-start.12 = (bf16[128,1024]{1,0:T(8,128)(2,1)S(1)}, bf16[128,1024]{1,0:T(8,128)(2,1)S(1)}, u32[]{:S(2)}, u32[]{:S(2)}) collective-permute-start(bf16[128,1024]{1,0:T(8,128)(2,1)S(1)} %collective-permute-done.10.refs_2_), channel_id=1, source_target_pairs={{0,2},{2,4},{4,6},{6,7},{7,5},{5,3},{3,1},{1,0},{8,10},{10,12},{12... | collective-permute-start | bytes 786440 | tf_op jit(solution)/shard_map/ppermute | solution.py:296
  51.9 13.8 %collective-permute-start.15 = (bf16[176,1408]{1,0:T(8,128)(2,1)S(1)}, bf16[176,1408]{1,0:T(8,128)(2,1)S(1)}, u32[]{:S(2)}, u32[]{:S(2)}) collective-permute-start(bf16[176,1408]{1,0:T(8,128)(2,1)S(1)} %slice.12), channel_id=1, source_target_pairs={{0,16},{8,24},{16,0},{24,8},{1,17},{9,25},{17,1},{25,9},{2,18},{10... | collective-permute-start | bytes 1486856 | tf_op jit(solution)/shard_map/ppermute | solution.py:321
  58.1 7.5 %collective-permute-start.14 = (bf16[128,1024]{1,0:T(8,128)(2,1)S(1)}, bf16[128,1024]{1,0:T(8,128)(2,1)S(1)}, u32[]{:S(2)}, u32[]{:S(2)}) collective-permute-start(bf16[128,1024]{1,0:T(8,128)(2,1)S(1)} %collective-permute-done.11.refs_6_), channel_id=1, source_target_pairs={{2,0},{4,2},{6,4},{7,6},{5,7},{3,5},{1,3},{0,1},{10,8},{12,10},{14... | collective-permute-start | bytes 786440 | tf_op jit(solution)/shard_map/ppermute | solution.py:296
  59.7 7.4 %copy-start.3 = (bf16[128,1024]{1,0:T(8,128)(2,1)S(1)}, bf16[128,1024]{1,0:T(8,128)(2,1)}, u32[]{:S(2)}) copy-start(bf16[128,1024]{1,0:T(8,128)(2,1)} %get-tuple-element.54.refs_0_) | copy-start | bytes 786436
  65.7 9.3 %collective-permute-start.16 = (bf16[128,1408]{1,0:T(8,128)(2,1)S(1)}, bf16[128,1408]{1,0:T(8,128)(2,1)S(1)}, u32[]{:S(2)}, u32[]{:S(2)}) collective-permute-start(bf16[128,1408]{1,0:T(8,128)(2,1)S(1)} %slice.13), channel_id=1, source_target_pairs={{0,16},{8,24},{16,0},{24,8},{1,17},{9,25},{17,1},{25,9},{2,18},{10... | collective-permute-start | bytes 1081352 | tf_op jit(solution)/shard_map/ppermute | solution.py:321
  74.9 14.8 %copy-start.4 = (s32[128,6]{0,1:T(8,128)S(1)}, s32[128,6]{0,1:T(8,128)}, u32[]{:S(2)}) copy-start(s32[128,6]{0,1:T(8,128)} %param.8) | copy-start | bytes 9220
  76.8 15.8 %collective-permute-start.17 = (bf16[512,1408]{1,0:T(8,128)(2,1)S(1)}, bf16[512,1408]{1,0:T(8,128)(2,1)S(1)}, u32[]{:S(2)}, u32[]{:S(2)}) collective-permute-start(bf16[512,1408]{1,0:T(8,128)(2,1)S(1)} %shard_map.91), channel_id=1, source_target_pairs={{0,8},{8,0},{16,24},{24,16},{1,9},{9,1},{17,25},{25,17},{2,10},{10... | collective-permute-start | bytes 4325384 | tf_op jit(solution)/shard_map/ppermute | solution.py:321
  76.9 15.7 %collective-permute-start.18 = (bf16[208,1408]{1,0:T(8,128)(2,1)S(1)}, bf16[208,1408]{1,0:T(8,128)(2,1)S(1)}, u32[]{:S(2)}, u32[]{:S(2)}) collective-permute-start(bf16[208,1408]{1,0:T(8,128)(2,1)S(1)} %slice.14), channel_id=1, source_target_pairs={{0,16},{8,24},{16,0},{24,8},{1,17},{9,25},{17,1},{25,9},{2,18},{10... | collective-permute-start | bytes 1757192 | tf_op jit(solution)/shard_map/ppermute | solution.py:321

commit v5 on v4

--- a/solution.py
+++ b/solution.py
@@ -68,25 +68,22 @@
     ).astype(jnp.bfloat16)
     before = jnp.dot(named.astype(jnp.bfloat16), earlier, preferred_element_type=jnp.float32)
     slot = jnp.where(named > 0.5, before, -1.0)
-    both = jnp.concatenate([prob, slot], axis=0).astype(jnp.bfloat16)
-    groups = 2 * experts // 16
-    for group in range(groups):
-        own_refs[0][rows:, group * rows : (group + 1) * rows] = both[group * 16 : (group + 1) * 16]
-    if groups * rows < columns:
-        own_refs[0][rows:, groups * rows :] = jnp.zeros((16, columns - groups * rows), jnp.bfloat16)
+    own_refs[0][rows:, :] = jnp.zeros((8, columns), jnp.bfloat16)
+    for group in range(experts // 8):
+        both = [v[group * 8 : (group + 1) * 8] for v in (prob, slot)]
+        own_refs[0][rows:, 2 * group * rows : 2 * (group + 1) * rows] = jnp.concatenate(
+            both, axis=1
+        ).astype(jnp.bfloat16)
 
 
 def row_of(block, expert, count, tokens):
-    sub = lax.broadcasted_iota(jnp.int32, (16, tokens), 0)
-    prob = jnp.zeros((1, tokens), jnp.float32)
-    slot = jnp.zeros((1, tokens), jnp.float32)
-    for group in range(2 * count // 16):
-        piece = block[tokens : tokens + 16, group * tokens : (group + 1) * tokens]
-        piece = piece.astype(jnp.float32)
-        row = sub + group * 16
-        prob = prob + jnp.sum(jnp.where(row == expert, piece, 0.0), 0, keepdims=True)
-        slot = slot + jnp.sum(jnp.where(row == expert + count, piece, 0.0), 0, keepdims=True)
-    return jnp.concatenate([prob, slot], axis=1)
+    sub = lax.broadcasted_iota(jnp.int32, (8, 2 * tokens), 0)
+    found = jnp.zeros((1, 2 * tokens), jnp.float32)
+    for group in range(count // 8):
+        piece = block[tokens : tokens + 8, 2 * group * tokens : 2 * (group + 1) * tokens]
+        own = jnp.where(sub + group * 8 == expert, piece.astype(jnp.float32), 0.0)
+        found = found + jnp.sum(own, 0, keepdims=True)
+    return found
 
 
 def weights_of(row, cap, tokens):
@@ -270,7 +267,7 @@
     own = pl.pallas_call(
         functools.partial(head_kernel, count, masks),
         out_shape=[
-            jax.ShapeDtypeStruct((tokens + (16 if c == 0 else 0), columns), jnp.bfloat16)
+            jax.ShapeDtypeStruct((tokens + (8 if c == 0 else 0), columns), jnp.bfloat16)
             for c in range(CHUNKS)
         ],
         grid=(1,),

time: 94.5 us -> 93.3 us (0.987)
  waiting for transfers between devices: 31.6 us -> 30.1 us
    ppermute x14, waiting for transfers between devices: 29.5 us -> 27.9 us  [step(): got[chunk][sign * k] = lax.ppermute(value, 'expert', pairs)]
  transfers between devices with their start and end apart: 19 -> 19, of which waited for: 12 -> 11; matrix products, arithmetic and copies ran while one was open for 2% -> 2% of each run, Pallas kernels for 20% -> 20%
where the time goes in v5:
time: 93.3 us; the launch traced here: 93 us
  waiting for transfers between devices  30.1 us (32%)
  Pallas kernels  25.4 us (27%)
  starting transfers between devices  20.8 us (22%)
  blocking collectives  11.4 us (12%)
  local copies, waits for them, and re-layouts  3.6 us (4%)
  other arithmetic  0.96 us (1%)
    ppermute x14, waiting for transfers between devices, step(): got[chunk][sign * k] = lax.ppermute(value, 'expert', pairs)  27.9 us
    pallas_call x4, Pallas kernels, call(): pl.pallas_call(kernel, out_shape=[jax.ShapeDtypeStruct(*out) for out in o...  18.3 us
    ppermute x14, starting transfers between devices, step(): got[chunk][sign * k] = lax.ppermute(value, 'expert', pairs)  16 us
    all_to_all x1, blocking collectives, body(): lax.all_to_all(by_token, 'expert', split_axis=0, concat_axis=0, tiled=True)  11.4 us
    ppermute x5, starting transfers between devices, exchange(): return lax.ppermute(value, 'dp', [(r, r ^ 1 << b) for r in range(replicas)])  4.75 us
    pallas_call x2, Pallas kernels, part_of(): pl.pallas_call(functools.partial(part_kernel, low), out_shape=[jax.ShapeD...  3.64 us
    unnamed x14, local copies, waits for them, and re-layouts  2.8 us
    ppermute x5, waiting for transfers between devices, exchange(): return lax.ppermute(value, 'dp', [(r, r ^ 1 << b) for r in range(replicas)])  2.16 us
  transfers between devices with their start and end apart: 19, of which 11 were waited for; matrix products, arithmetic and copies ran while one was open for 2% of the time, Pallas kernels for 20%

profile of v5, /device:TPU:0, one launch (start us, length us, event | category | flops | bytes accessed | tf_op | source)
XLA Modules:
  0.0 93.0 jit_solution(4166265417318949445)
XLA Ops:
  0.6 1.9 %shard_map.85 = (bf16[136,1024]{1,0:T(8,128)(2,1)}, bf16[128,1024]{1,0:T(8,128)(2,1)}) custom-call(s32[6,128]{1,0:T(8,128)} %bitcast.25, bf16[6,128]{1,0:T(8,128)(2,1)} %bitcast.27, bf16[128,2048]{1,0:T(8,128)(2,1)} %grad_ref.1), custom_call_target="tpu_custom_call" | custom-call | tf_op jit(solution)/shard_map/pallas_call | solution.py:267
  2.5 3.0 %collective-permute-start.2 = (bf16[136,1024]{1,0:T(8,128)(2,1)}, bf16[136,1024]{1,0:T(8,128)(2,1)S(1)}, u32[]{:S(2)}, u32[]{:S(2)}) collective-permute-start(bf16[136,1024]{1,0:T(8,128)(2,1)} %get-tuple-element.33.refs_0_), channel_id=1, source_target_pairs={{2,0},{4,2},{6,4},{7,6},{5,7},{3,5},{1,3},{0,1},{10,8},{12,10},{14... | collective-permute-start | bytes 835592 | tf_op jit(solution)/shard_map/ppermute | solution.py:293
  5.5 0.1 collective-permute-start
  5.6 0.7 dynamic-slice_bitcast_fusion.where_ref
  6.3 6.2 %collective-permute-done.2.refs_4_ = bf16[136,1024]{1,0:T(8,128)(2,1)S(1)} collective-permute-done((bf16[136,1024]{1,0:T(8,128)(2,1)}, bf16[136,1024]{1,0:T(8,128)(2,1)S(1)}, u32[]{:S(2)}, u32[]{:S(2)}) %collective-permute-start.2) | collective-permute-done | bytes 278560 | tf_op jit(solution)/shard_map/ppermute | solution.py:293
  12.4 1.7 %collective-permute-start.3 = (bf16[136,1024]{1,0:T(8,128)(2,1)S(1)}, bf16[136,1024]{1,0:T(8,128)(2,1)S(1)}, u32[]{:S(2)}, u32[]{:S(2)}) collective-permute-start(bf16[136,1024]{1,0:T(8,128)(2,1)S(1)} %collective-permute-done.2.refs_4_), channel_id=1, source_target_pairs={{2,0},{4,2},{6,4},{7,6},{5,7},{3,5},{1,3},{0,1},{10,8},{12,10},{14... | collective-permute-start | bytes 835592 | tf_op jit(solution)/shard_map/ppermute | solution.py:293
  14.1 0.0 collective-permute-done.refs_1_
  14.1 0.3 collective-permute-start.1
  14.5 5.8 %collective-permute-done.3.refs_5_ = bf16[136,1024]{1,0:T(8,128)(2,1)S(1)} collective-permute-done((bf16[136,1024]{1,0:T(8,128)(2,1)S(1)}, bf16[136,1024]{1,0:T(8,128)(2,1)S(1)}, u32[]{:S(2)}, u32[]{:S(2)}) %collective-permute-start.3) | collective-permute-done | bytes 278560 | tf_op jit(solution)/shard_map/ppermute | solution.py:293
  20.3 1.1 %collective-permute-done.1.refs_2_ = bf16[136,1024]{1,0:T(8,128)(2,1)S(1)} collective-permute-done((bf16[136,1024]{1,0:T(8,128)(2,1)S(1)}, bf16[136,1024]{1,0:T(8,128)(2,1)S(1)}, u32[]{:S(2)}, u32[]{:S(2)}) %collective-permute-start.1) | collective-permute-done | bytes 278560 | tf_op jit(solution)/shard_map/ppermute | solution.py:293
  21.4 0.7 collective-permute-start.6
  22.0 1.4 %collective-permute-start.7 = (bf16[136,1024]{1,0:T(8,128)(2,1)S(1)}, bf16[136,1024]{1,0:T(8,128)(2,1)S(1)}, u32[]{:S(2)}, u32[]{:S(2)}) collective-permute-start(bf16[136,1024]{1,0:T(8,128)(2,1)S(1)} %collective-permute-done.3.refs_5_), channel_id=1, source_target_pairs={{2,0},{4,2},{6,4},{7,6},{5,7},{3,5},{1,3},{0,1},{10,8},{12,10},{14... | collective-permute-start | bytes 835592 | tf_op jit(solution)/shard_map/ppermute | solution.py:293
  23.4 0.7 collective-permute-start.5
  24.1 1.4 %collective-permute-start.4 = (bf16[128,1024]{1,0:T(8,128)(2,1)}, bf16[128,1024]{1,0:T(8,128)(2,1)S(1)}, u32[]{:S(2)}, u32[]{:S(2)}) collective-permute-start(bf16[128,1024]{1,0:T(8,128)(2,1)} %get-tuple-element.54.refs_0_), channel_id=1, source_target_pairs={{2,0},{4,2},{6,4},{7,6},{5,7},{3,5},{1,3},{0,1},{10,8},{12,10},{14... | collective-permute-start | bytes 786440 | tf_op jit(solution)/shard_map/ppermute | solution.py:293
  25.4 7.9 %collective-permute-done.5.refs_1_ = bf16[128,1024]{1,0:T(8,128)(2,1)S(1)} collective-permute-done((bf16[128,1024]{1,0:T(8,128)(2,1)}, bf16[128,1024]{1,0:T(8,128)(2,1)S(1)}, u32[]{:S(2)}, u32[]{:S(2)}) %collective-permute-start.5) | collective-permute-done | bytes 262176 | tf_op jit(solution)/shard_map/ppermute | solution.py:293
  33.3 0.7 collective-permute-done.4.refs_4_
  34.0 0.0 collective-permute-done.6.refs_3_
  34.0 1.2 %collective-permute-start.9 = (bf16[136,1024]{1,0:T(8,128)(2,1)S(1)}, bf16[136,1024]{1,0:T(8,128)(2,1)S(1)}, u32[]{:S(2)}, u32[]{:S(2)}) collective-permute-start(bf16[136,1024]{1,0:T(8,128)(2,1)S(1)} %collective-permute-done.6.refs_3_), channel_id=1, source_target_pairs={{0,2},{2,4},{4,6},{6,7},{7,5},{5,3},{3,1},{1,0},{8,10},{10,12},{12... | collective-permute-start | bytes 835592 | tf_op jit(solution)/shard_map/ppermute | solution.py:293
  35.3 0.8 collective-permute-start.8
  36.1 1.2 %collective-permute-start.10 = (bf16[128,1024]{1,0:T(8,128)(2,1)S(1)}, bf16[128,1024]{1,0:T(8,128)(2,1)S(1)}, u32[]{:S(2)}, u32[]{:S(2)}) collective-permute-start(bf16[128,1024]{1,0:T(8,128)(2,1)S(1)} %collective-permute-done.5.refs_1_), channel_id=1, source_target_pairs={{0,2},{2,4},{4,6},{6,7},{7,5},{5,3},{3,1},{1,0},{8,10},{10,12},{12... | collective-permute-start | bytes 786440 | tf_op jit(solution)/shard_map/ppermute | solution.py:293
  37.3 1.8 %copy-done = bf16[1,8,128,1408]{3,2,1,0:T(8,128)(2,1)S(1)} copy-done((bf16[1,8,128,1408]{3,2,1,0:T(8,128)(2,1)S(1)}, bf16[1,8,128,1408]{3,2,1,0:T(8,128)(2,1)}, u32[]{:S(2)}) %copy-start) | copy-done | bytes 2883608
  39.1 1.0 %copy-done.2 = bf16[136,1024]{1,0:T(8,128)(2,1)S(1)} copy-done((bf16[136,1024]{1,0:T(8,128)(2,1)S(1)}, bf16[136,1024]{1,0:T(8,128)(2,1)}, u32[]{:S(2)}) %copy-start.2) | copy-done | bytes 278552
  40.1 5.2 %shard_map.86 = (f32[8,256]{1,0:T(8,128)S(1)}, bf16[1024,1024]{1,0:T(8,128)(2,1)S(1)}, f32[512,1408]{1,0:T(8,128)S(1)}, f32[512,1408]{1,0:T(8,128)S(1)}) custom-call(s32[18]{0:T(128)S(1)} %dynamic-slice_bitcast_fusion.where_ref, bf16[136,1024]{1,0:T(8,128)(2,1)S(1)} %copy-done.2, bf16[136,1024]{1,0:T(8,128)(2,1)S(1)} %collective-permute-done.refs_1_, ...), custom_call_target="tpu_custom_call" | custom-call | tf_op jit(solution)/shard_map/pallas_call | solution.py:298
  45.3 0.0 slice-start
  45.3 1.7 %shard_map.87 = (bf16[512,1408]{1,0:T(8,128)(2,1)S(1)}, bf16[512,1408]{1,0:T(8,128)(2,1)S(1)}, f32[8,256]{1,0:T(8,128)S(1)}) custom-call(s32[18]{0:T(128)S(1)} %dynamic-slice_bitcast_fusion.where_ref, bf16[136,1024]{1,0:T(8,128)(2,1)S(1)} %collective-permute-done.9.block_ref, f32[8,256]{1,0:T(8,128)S(1)} %get-tuple-element.45.near_ref, ...), custom_call_target="tpu_custom_call" | custom-call | tf_op jit(solution)/shard_map/pallas_call | solution.py:298
  47.0 0.1 collective-permute-start.13
  47.0 1.3 %collective-permute-start.11 = (bf16[128,1024]{1,0:T(8,128)(2,1)S(1)}, bf16[128,1024]{1,0:T(8,128)(2,1)S(1)}, u32[]{:S(2)}, u32[]{:S(2)}) collective-permute-start(bf16[128,1024]{1,0:T(8,128)(2,1)S(1)} %collective-permute-done.8.refs_5_), channel_id=1, source_target_pairs={{2,0},{4,2},{6,4},{7,6},{5,7},{3,5},{1,3},{0,1},{10,8},{12,10},{14... | collective-permute-start | bytes 786440 | tf_op jit(solution)/shard_map/ppermute | solution.py:293
  48.3 0.8 collective-permute-start.12
  49.1 1.1 %collective-permute-done.13 = bf16[512,1408]{1,0:T(8,128)(2,1)S(1)} collective-permute-done((bf16[512,1408]{1,0:T(8,128)(2,1)S(1)}, bf16[512,1408]{1,0:T(8,128)(2,1)S(1)}, u32[]{:S(2)}, u32[]{:S(2)}) %collective-permute-start.13) | collective-permute-done | bytes 1441824 | tf_op jit(solution)/shard_map/ppermute | solution.py:318
  50.3 0.3 add_convert_fusion
  50.7 1.6 %collective-permute-start.15 = (bf16[176,1408]{1,0:T(8,128)(2,1)S(1)}, bf16[176,1408]{1,0:T(8,128)(2,1)S(1)}, u32[]{:S(2)}, u32[]{:S(2)}) collective-permute-start(bf16[176,1408]{1,0:T(8,128)(2,1)S(1)} %slice.12), channel_id=1, source_target_pairs={{0,16},{8,24},{16,0},{24,8},{1,17},{9,25},{17,1},{25,9},{2,18},{10... | collective-permute-start | bytes 1486856 | tf_op jit(solution)/shard_map/ppermute | solution.py:318
  52.2 3.5 %collective-permute-done.11.refs_6_ = bf16[128,1024]{1,0:T(8,128)(2,1)S(1)} collective-permute-done((bf16[128,1024]{1,0:T(8,128)(2,1)S(1)}, bf16[128,1024]{1,0:T(8,128)(2,1)S(1)}, u32[]{:S(2)}, u32[]{:S(2)}) %collective-permute-start.11) | collective-permute-done | bytes 262176 | tf_op jit(solution)/shard_map/ppermute | solution.py:293
  55.8 0.9 %collective-permute-done.12.refs_3_ = bf16[128,1024]{1,0:T(8,128)(2,1)S(1)} collective-permute-done((bf16[128,1024]{1,0:T(8,128)(2,1)S(1)}, bf16[128,1024]{1,0:T(8,128)(2,1)S(1)}, u32[]{:S(2)}, u32[]{:S(2)}) %collective-permute-start.12) | collective-permute-done | bytes 262176 | tf_op jit(solution)/shard_map/ppermute | solution.py:293
  56.7 1.6 %collective-permute-start.14 = (bf16[128,1024]{1,0:T(8,128)(2,1)S(1)}, bf16[128,1024]{1,0:T(8,128)(2,1)S(1)}, u32[]{:S(2)}, u32[]{:S(2)}) collective-permute-start(bf16[128,1024]{1,0:T(8,128)(2,1)S(1)} %collective-permute-done.11.refs_6_), channel_id=1, source_target_pairs={{2,0},{4,2},{6,4},{7,6},{5,7},{3,5},{1,3},{0,1},{10,8},{12,10},{14... | collective-permute-start | bytes 786440 | tf_op jit(solution)/shard_map/ppermute | solution.py:293
  58.3 0.0 copy-start.3
  58.3 4.2 %shard_map.88.refs_10_ = f32[1024,1408]{1,0:T(8,128)S(1)} custom-call(s32[18]{0:T(128)S(1)} %dynamic-slice_bitcast_fusion.where_ref, bf16[136,1024]{1,0:T(8,128)(2,1)S(1)} %collective-permute-done.9.block_ref, f32[8,256]{1,0:T(8,128)S(1)} %get-tuple-element.52.refs_0_.refs_8_, bf16[1024,1024]{1,0:T(8,128)(2,1)S(1)} %get-tuple-element.53.refs_1_, ...), custom_call_target="tpu_custom_call" | custom-call | tf_op jit(solution)/shard_map/pallas_call | solution.py:298
  62.5 1.7 %collective-permute-done.14.refs_7_ = bf16[128,1024]{1,0:T(8,128)(2,1)S(1)} collective-permute-done((bf16[128,1024]{1,0:T(8,128)(2,1)S(1)}, bf16[128,1024]{1,0:T(8,128)(2,1)S(1)}, u32[]{:S(2)}, u32[]{:S(2)}) %collective-permute-start.14) | collective-permute-done | bytes 262176 | tf_op jit(solution)/shard_map/ppermute | solution.py:293
  64.2 1.5 %collective-permute-start.16 = (bf16[128,1408]{1,0:T(8,128)(2,1)S(1)}, bf16[128,1408]{1,0:T(8,128)(2,1)S(1)}, u32[]{:S(2)}, u32[]{:S(2)}) collective-permute-start(bf16[128,1408]{1,0:T(8,128)(2,1)S(1)} %slice.13), channel_id=1, source_target_pairs={{0,16},{8,24},{16,0},{24,8},{1,17},{9,25},{17,1},{25,9},{2,18},{10... | collective-permute-start | bytes 1081352 | tf_op jit(solution)/shard_map/ppermute | solution.py:318
  65.7 7.2 %shard_map.89 = (bf16[1024,1408]{1,0:T(8,128)(2,1)}, f32[8,128]{1,0:T(8,128)S(1)}, bf16[1024,1024]{1,0:T(8,128)(2,1)S(1)}) custom-call(s32[18]{0:T(128)S(1)} %dynamic-slice_bitcast_fusion.where_ref, bf16[128,1024]{1,0:T(8,128)(2,1)S(1)} %copy-done.3, bf16[128,1024]{1,0:T(8,128)(2,1)S(1)} %collective-permute-done.5.refs_1_, ...), custom_call_target="tpu_custom_call" | custom-call | tf_op jit(solution)/shard_map/pallas_call | solution.py:298
  73.0 0.7 collective-permute-done.16.refs_1_
  73.7 1.8 %shard_map.91 = bf16[512,1408]{1,0:T(8,128)(2,1)S(1)} custom-call(bf16[1024,1024]{1,0:T(8,128)(2,1)S(1)} %get-tuple-element.59.scaled_ref, bf16[1024,1408]{1,0:T(8,128)(2,1)S(1)} %bitcast.17), custom_call_target="tpu_custom_call" | custom-call | tf_op jit(solution)/shard_map/pallas_call | solution.py:389
  75.5 0.1 collective-permute-start.17
  75.7 1.6 %collective-permute-start.18 = (bf16[208,1408]{1,0:T(8,128)(2,1)S(1)}, bf16[208,1408]{1,0:T(8,128)(2,1)S(1)}, u32[]{:S(2)}, u32[]{:S(2)}) collective-permute-start(bf16[208,1408]{1,0:T(8,128)(2,1)S(1)} %slice.14), channel_id=1, source_target_pairs={{0,16},{8,24},{16,0},{24,8},{1,17},{9,25},{17,1},{25,9},{2,18},{10... | collective-permute-start | bytes 1757192 | tf_op jit(solution)/shard_map/ppermute | solution.py:318
  77.2 11.4 %all_to_all.12 = f32[8,1,128]{2,1,0:T(1,128)S(1)} all-to-all(f32[8,1,128]{2,1,0:T(1,128)S(1)} %bitcast.23), channel_id=1, replica_groups=mesh['dp'=4,'expert'=8] {'expert'}, dimensions={0} | all-to-all | bytes 8192 | tf_op jit(solution)/shard_map/all_to_all | solution.py:385
  88.6 0.6 select_reduce_fusion
  89.2 1.8 %shard_map.90.kept_ref = bf16[512,1408]{1,0:T(8,128)(2,1)S(1)} custom-call(bf16[1024,1024]{1,0:T(8,128)(2,1)S(1)} %get-tuple-element.59.scaled_ref, bf16[1024,1408]{1,0:T(8,128)(2,1)S(1)} %bitcast.18), custom_call_target="tpu_custom_call" | custom-call | tf_op jit(solution)/shard_map/pallas_call | solution.py:389
  91.0 0.3 collective-permute-done.18.refs_2_
  91.4 1.6 %shard_map.92 = bf16[512,1408]{1,0:T(8,128)(2,1)} custom-call(bf16[512,1408]{1,0:T(8,128)(2,1)S(1)} %shard_map.90.kept_ref, bf16[512,1408]{1,0:T(8,128)(2,1)S(1)} %collective-permute-done.17.moved_ref, bf16[176,1408]{1,0:T(8,128)(2,1)S(1)} %collective-permute-done.15.refs_0_, bf16[128,1408]{1,0:T(8,128)(2,1)S(1)} %collective-permute-done.16.refs_1_, ...), custom_call_target="tpu_custom_call" | custom-call | tf_op jit(solution)/shard_map/pallas_call | solution.py:399
  (20 shorter events, 0.1 us)
Async XLA Ops:
  2.5 9.9 %collective-permute-start.2 = (bf16[136,1024]{1,0:T(8,128)(2,1)}, bf16[136,1024]{1,0:T(8,128)(2,1)S(1)}, u32[]{:S(2)}, u32[]{:S(2)}) collective-permute-start(bf16[136,1024]{1,0:T(8,128)(2,1)} %get-tuple-element.33.refs_0_), channel_id=1, source_target_pairs={{2,0},{4,2},{6,4},{7,6},{5,7},{3,5},{1,3},{0,1},{10,8},{12,10},{14... | collective-permute-start | bytes 835592 | tf_op jit(solution)/shard_map/ppermute | solution.py:293
  5.5 8.6 %collective-permute-start = (bf16[136,1024]{1,0:T(8,128)(2,1)}, bf16[136,1024]{1,0:T(8,128)(2,1)S(1)}, u32[]{:S(2)}, u32[]{:S(2)}) collective-permute-start(bf16[136,1024]{1,0:T(8,128)(2,1)} %get-tuple-element.33.refs_0_), channel_id=1, source_target_pairs={{0,2},{2,4},{4,6},{6,7},{7,5},{5,3},{3,1},{1,0},{8,10},{10,12},{12... | collective-permute-start | bytes 835592 | tf_op jit(solution)/shard_map/ppermute | solution.py:293
  12.4 7.8 %collective-permute-start.3 = (bf16[136,1024]{1,0:T(8,128)(2,1)S(1)}, bf16[136,1024]{1,0:T(8,128)(2,1)S(1)}, u32[]{:S(2)}, u32[]{:S(2)}) collective-permute-start(bf16[136,1024]{1,0:T(8,128)(2,1)S(1)} %collective-permute-done.2.refs_4_), channel_id=1, source_target_pairs={{2,0},{4,2},{6,4},{7,6},{5,7},{3,5},{1,3},{0,1},{10,8},{12,10},{14... | collective-permute-start | bytes 835592 | tf_op jit(solution)/shard_map/ppermute | solution.py:293
  14.1 7.3 %collective-permute-start.1 = (bf16[136,1024]{1,0:T(8,128)(2,1)S(1)}, bf16[136,1024]{1,0:T(8,128)(2,1)S(1)}, u32[]{:S(2)}, u32[]{:S(2)}) collective-permute-start(bf16[136,1024]{1,0:T(8,128)(2,1)S(1)} %collective-permute-done.refs_1_), channel_id=1, source_target_pairs={{0,2},{2,4},{4,6},{6,7},{7,5},{5,3},{3,1},{1,0},{8,10},{10,12},{12... | collective-permute-start | bytes 835592 | tf_op jit(solution)/shard_map/ppermute | solution.py:293
  21.4 12.6 %collective-permute-start.6 = (bf16[136,1024]{1,0:T(8,128)(2,1)S(1)}, bf16[136,1024]{1,0:T(8,128)(2,1)S(1)}, u32[]{:S(2)}, u32[]{:S(2)}) collective-permute-start(bf16[136,1024]{1,0:T(8,128)(2,1)S(1)} %collective-permute-done.1.refs_2_), channel_id=1, source_target_pairs={{0,2},{2,4},{4,6},{6,7},{7,5},{5,3},{3,1},{1,0},{8,10},{10,12},{12... | collective-permute-start | bytes 835592 | tf_op jit(solution)/shard_map/ppermute | solution.py:293
  22.0 12.0 %collective-permute-start.7 = (bf16[136,1024]{1,0:T(8,128)(2,1)S(1)}, bf16[136,1024]{1,0:T(8,128)(2,1)S(1)}, u32[]{:S(2)}, u32[]{:S(2)}) collective-permute-start(bf16[136,1024]{1,0:T(8,128)(2,1)S(1)} %collective-permute-done.3.refs_5_), channel_id=1, source_target_pairs={{2,0},{4,2},{6,4},{7,6},{5,7},{3,5},{1,3},{0,1},{10,8},{12,10},{14... | collective-permute-start | bytes 835592 | tf_op jit(solution)/shard_map/ppermute | solution.py:293
  23.4 9.9 %collective-permute-start.5 = (bf16[128,1024]{1,0:T(8,128)(2,1)}, bf16[128,1024]{1,0:T(8,128)(2,1)S(1)}, u32[]{:S(2)}, u32[]{:S(2)}) collective-permute-start(bf16[128,1024]{1,0:T(8,128)(2,1)} %get-tuple-element.54.refs_0_), channel_id=1, source_target_pairs={{0,2},{2,4},{4,6},{6,7},{7,5},{5,3},{3,1},{1,0},{8,10},{10,12},{12... | collective-permute-start | bytes 786440 | tf_op jit(solution)/shard_map/ppermute | solution.py:293
  24.1 10.0 %collective-permute-start.4 = (bf16[128,1024]{1,0:T(8,128)(2,1)}, bf16[128,1024]{1,0:T(8,128)(2,1)S(1)}, u32[]{:S(2)}, u32[]{:S(2)}) collective-permute-start(bf16[128,1024]{1,0:T(8,128)(2,1)} %get-tuple-element.54.refs_0_), channel_id=1, source_target_pairs={{2,0},{4,2},{6,4},{7,6},{5,7},{3,5},{1,3},{0,1},{10,8},{12,10},{14... | collective-permute-start | bytes 786440 | tf_op jit(solution)/shard_map/ppermute | solution.py:293
  34.0 11.2 %collective-permute-start.9 = (bf16[136,1024]{1,0:T(8,128)(2,1)S(1)}, bf16[136,1024]{1,0:T(8,128)(2,1)S(1)}, u32[]{:S(2)}, u32[]{:S(2)}) collective-permute-start(bf16[136,1024]{1,0:T(8,128)(2,1)S(1)} %collective-permute-done.6.refs_3_), channel_id=1, source_target_pairs={{0,2},{2,4},{4,6},{6,7},{7,5},{5,3},{3,1},{1,0},{8,10},{10,12},{12... | collective-permute-start | bytes 835592 | tf_op jit(solution)/shard_map/ppermute | solution.py:293
  35.3 10.0 %collective-permute-start.8 = (bf16[128,1024]{1,0:T(8,128)(2,1)S(1)}, bf16[128,1024]{1,0:T(8,128)(2,1)S(1)}, u32[]{:S(2)}, u32[]{:S(2)}) collective-permute-start(bf16[128,1024]{1,0:T(8,128)(2,1)S(1)} %collective-permute-done.4.refs_4_), channel_id=1, source_target_pairs={{2,0},{4,2},{6,4},{7,6},{5,7},{3,5},{1,3},{0,1},{10,8},{12,10},{14... | collective-permute-start | bytes 786440 | tf_op jit(solution)/shard_map/ppermute | solution.py:293
  36.1 9.2 %collective-permute-start.10 = (bf16[128,1024]{1,0:T(8,128)(2,1)S(1)}, bf16[128,1024]{1,0:T(8,128)(2,1)S(1)}, u32[]{:S(2)}, u32[]{:S(2)}) collective-permute-start(bf16[128,1024]{1,0:T(8,128)(2,1)S(1)} %collective-permute-done.5.refs_1_), channel_id=1, source_target_pairs={{0,2},{2,4},{4,6},{6,7},{7,5},{5,3},{3,1},{1,0},{8,10},{10,12},{12... | collective-permute-start | bytes 786440 | tf_op jit(solution)/shard_map/ppermute | solution.py:293
  37.3 1.8 %copy-start = (bf16[1,8,128,1408]{3,2,1,0:T(8,128)(2,1)S(1)}, bf16[1,8,128,1408]{3,2,1,0:T(8,128)(2,1)}, u32[]{:S(2)}) copy-start(bf16[1,8,128,1408]{3,2,1,0:T(8,128)(2,1)} %param.9) | copy-start | bytes 8650756
  39.1 1.0 %copy-start.2 = (bf16[136,1024]{1,0:T(8,128)(2,1)S(1)}, bf16[136,1024]{1,0:T(8,128)(2,1)}, u32[]{:S(2)}) copy-start(bf16[136,1024]{1,0:T(8,128)(2,1)} %get-tuple-element.33.refs_0_) | copy-start | bytes 835588
  40.1 5.2 %copy-start.1 = (bf16[1,8,128,1408]{3,2,1,0:T(8,128)(2,1)S(1)}, bf16[1,8,128,1408]{3,2,1,0:T(8,128)(2,1)}, u32[]{:S(2)}) copy-start(bf16[1,8,128,1408]{3,2,1,0:T(8,128)(2,1)} %param.9) | copy-start | bytes 8650756
  45.3 13.0 %slice-start = ((s8[5767168]{0:T(1024)(128)(4,1)}), s8[4194304]{0:T(1024)(128)(4,1)S(1)}, s32[]{:S(2)}) async-start(s8[5767168]{0:T(1024)(128)(4,1)} %bitcast.19), calls=%async_computation.1 | async-start | bytes 8388608
  45.3 13.0 %slice-start.1 = ((s8[5767168]{0:T(1024)(128)(4,1)}), s8[1572864]{0:T(1024)(128)(4,1)S(1)}, s32[]{:S(2)}) async-start(s8[5767168]{0:T(1024)(128)(4,1)} %bitcast.19), calls=%async_computation.2 | async-start | bytes 3145728
  47.0 3.3 %collective-permute-start.13 = (bf16[512,1408]{1,0:T(8,128)(2,1)S(1)}, bf16[512,1408]{1,0:T(8,128)(2,1)S(1)}, u32[]{:S(2)}, u32[]{:S(2)}) collective-permute-start(bf16[512,1408]{1,0:T(8,128)(2,1)S(1)} %get-tuple-element.49), channel_id=1, source_target_pairs={{0,8},{8,0},{16,24},{24,16},{1,9},{9,1},{17,25},{25,17},{2,10},{10... | collective-permute-start | bytes 4325384 | tf_op jit(solution)/shard_map/ppermute | solution.py:318
  47.0 8.7 %collective-permute-start.11 = (bf16[128,1024]{1,0:T(8,128)(2,1)S(1)}, bf16[128,1024]{1,0:T(8,128)(2,1)S(1)}, u32[]{:S(2)}, u32[]{:S(2)}) collective-permute-start(bf16[128,1024]{1,0:T(8,128)(2,1)S(1)} %collective-permute-done.8.refs_5_), channel_id=1, source_target_pairs={{2,0},{4,2},{6,4},{7,6},{5,7},{3,5},{1,3},{0,1},{10,8},{12,10},{14... | collective-permute-start | bytes 786440 | tf_op jit(solution)/shard_map/ppermute | solution.py:293
  48.3 8.4 %collective-permute-start.12 = (bf16[128,1024]{1,0:T(8,128)(2,1)S(1)}, bf16[128,1024]{1,0:T(8,128)(2,1)S(1)}, u32[]{:S(2)}, u32[]{:S(2)}) collective-permute-start(bf16[128,1024]{1,0:T(8,128)(2,1)S(1)} %collective-permute-done.10.refs_2_), channel_id=1, source_target_pairs={{0,2},{2,4},{4,6},{6,7},{7,5},{5,3},{3,1},{1,0},{8,10},{10,12},{12... | collective-permute-start | bytes 786440 | tf_op jit(solution)/shard_map/ppermute | solution.py:293
  50.7 13.6 %collective-permute-start.15 = (bf16[176,1408]{1,0:T(8,128)(2,1)S(1)}, bf16[176,1408]{1,0:T(8,128)(2,1)S(1)}, u32[]{:S(2)}, u32[]{:S(2)}) collective-permute-start(bf16[176,1408]{1,0:T(8,128)(2,1)S(1)} %slice.12), channel_id=1, source_target_pairs={{0,16},{8,24},{16,0},{24,8},{1,17},{9,25},{17,1},{25,9},{2,18},{10... | collective-permute-start | bytes 1486856 | tf_op jit(solution)/shard_map/ppermute | solution.py:318
  56.7 7.5 %collective-permute-start.14 = (bf16[128,1024]{1,0:T(8,128)(2,1)S(1)}, bf16[128,1024]{1,0:T(8,128)(2,1)S(1)}, u32[]{:S(2)}, u32[]{:S(2)}) collective-permute-start(bf16[128,1024]{1,0:T(8,128)(2,1)S(1)} %collective-permute-done.11.refs_6_), channel_id=1, source_target_pairs={{2,0},{4,2},{6,4},{7,6},{5,7},{3,5},{1,3},{0,1},{10,8},{12,10},{14... | collective-permute-start | bytes 786440 | tf_op jit(solution)/shard_map/ppermute | solution.py:293
  58.3 7.4 %copy-start.3 = (bf16[128,1024]{1,0:T(8,128)(2,1)S(1)}, bf16[128,1024]{1,0:T(8,128)(2,1)}, u32[]{:S(2)}) copy-start(bf16[128,1024]{1,0:T(8,128)(2,1)} %get-tuple-element.54.refs_0_) | copy-start | bytes 786436
  64.2 9.5 %collective-permute-start.16 = (bf16[128,1408]{1,0:T(8,128)(2,1)S(1)}, bf16[128,1408]{1,0:T(8,128)(2,1)S(1)}, u32[]{:S(2)}, u32[]{:S(2)}) collective-permute-start(bf16[128,1408]{1,0:T(8,128)(2,1)S(1)} %slice.13), channel_id=1, source_target_pairs={{0,16},{8,24},{16,0},{24,8},{1,17},{9,25},{17,1},{25,9},{2,18},{10... | collective-permute-start | bytes 1081352 | tf_op jit(solution)/shard_map/ppermute | solution.py:318
  73.7 14.9 %copy-start.4 = (s32[128,6]{0,1:T(8,128)S(1)}, s32[128,6]{0,1:T(8,128)}, u32[]{:S(2)}) copy-start(s32[128,6]{0,1:T(8,128)} %param.8) | copy-start | bytes 9220
  75.5 15.8 %collective-permute-start.17 = (bf16[512,1408]{1,0:T(8,128)(2,1)S(1)}, bf16[512,1408]{1,0:T(8,128)(2,1)S(1)}, u32[]{:S(2)}, u32[]{:S(2)}) collective-permute-start(bf16[512,1408]{1,0:T(8,128)(2,1)S(1)} %shard_map.91), channel_id=1, source_target_pairs={{0,8},{8,0},{16,24},{24,16},{1,9},{9,1},{17,25},{25,17},{2,10},{10... | collective-permute-start | bytes 4325384 | tf_op jit(solution)/shard_map/ppermute | solution.py:318
  75.7 15.7 %collective-permute-start.18 = (bf16[208,1408]{1,0:T(8,128)(2,1)S(1)}, bf16[208,1408]{1,0:T(8,128)(2,1)S(1)}, u32[]{:S(2)}, u32[]{:S(2)}) collective-permute-start(bf16[208,1408]{1,0:T(8,128)(2,1)S(1)} %slice.14), channel_id=1, source_target_pairs={{0,16},{8,24},{16,0},{24,8},{1,17},{9,25},{17,1},{25,9},{2,18},{10... | collective-permute-start | bytes 1757192 | tf_op jit(solution)/shard_map/ppermute | solution.py:318
